TPU v7x, 512 devices: a whole 4x8x8 slice. The times are simulated.
512 devices in a mesh: grp: 4 (over y_hi, core), dev: 32 (over x, z), split: 4 (over y_lo).
Axes of the slice: x: 4, y: 8 (y_hi: 2, y_lo: 4; y = y_hi * 4 + y_lo), z: 8, core: 2. Of those that a mesh axis runs over, the one named last changes fastest.
Arguments:
- tokens: bfloat16 [16384, 2048], P(('grp', 'dev'), 'split'), may hold values from -6 to 6
- upstream: bfloat16 [16384, 2048], P(('grp', 'dev'), 'split'), may hold values from -0.29882812 to 0.29882812
- expert_ids: int32 [16384, 8], P(('grp', 'dev')), may hold values from 0 to 127, as said below
- gate_probs: float32 [16384, 8], P(('grp', 'dev')), may hold values from 0.1 to 0.5
- w_gate: bfloat16 [128, 2048, 768], P(('grp', 'dev'), None, 'split'), may hold values from -0.125 to 0.125
- w_up: bfloat16 [128, 2048, 768], P(('grp', 'dev'), None, 'split'), may hold values from -0.125 to 0.125
- w_down: bfloat16 [128, 768, 2048], P(('grp', 'dev'), None, 'split'), may hold values from -0.21875 to 0.21875
Outputs:
- mixed: bfloat16 [16384, 2048], P(('grp', 'dev'), 'split')
- gate_grads: float32 [16384, 8], P(('grp', 'dev'))
- down_grads: float32 [128, 768, 2048], P(('grp', 'dev'), None, 'split')
Inputs may be any that keep to these rules, and one draw needn't show every extreme that they name: `expert_ids`: each row names 8 different experts. The 128 rows of one device name any one expert at most 16 times, and 4 experts, the same for every device, exactly 16 times on every device.
All inputs are finite; a program needn't handle non-finite values.
Results may differ from a plain program's by a relative error of at most 0.0058.
Values may be sent and summed in bfloat16 or wider, within the bound.
No kernel may reach another device: no remote copies, remote signals or barrier semaphores. Data moves between devices by JAX's collectives and lax.ppermute only.
A program may use at most 64 MiB of HBM per device.

v0:
```python
import jax
import jax.numpy as jnp
from jax import lax
from jax.sharding import PartitionSpec as P


def place_pairs(expert_ids, experts, capacity):
    flat_ids = expert_ids.reshape(-1)
    member = (flat_ids[:, None] == jnp.arange(experts, dtype=jnp.int32)[None, :]).astype(jnp.int32)
    earlier = jnp.cumsum(member, axis=0) - member
    position = jnp.sum(earlier * member, axis=1)
    return flat_ids * capacity + position


def per_device(tokens, upstream, expert_ids, gate_probs, w_gate, w_up, w_down):
    experts = lax.axis_size(("grp", "dev"))
    tok_rows, top = expert_ids.shape
    capacity = min(tok_rows, 2 * tok_rows * top // experts)
    buffer_rows = experts * capacity
    target = place_pairs(expert_ids, experts, capacity)
    matched = target[None, :] == jnp.arange(buffer_rows, dtype=jnp.int32)[:, None]
    matched = matched.reshape(buffer_rows, tok_rows, top)
    selector = jnp.sum(matched.astype(jnp.int32), axis=2).astype(jnp.bfloat16)
    weighted = jnp.sum(jnp.where(matched, gate_probs[None, :, :], 0.0), axis=2)
    scaled_send = jnp.dot(
        weighted,
        upstream.astype(jnp.float32),
        precision=lax.Precision.HIGHEST,
        preferred_element_type=jnp.float32,
    ).astype(jnp.bfloat16)
    gate_rows = w_gate[0]
    up_rows = w_up[0]
    down_rows = w_down[0]
    gathered = lax.all_gather(tokens, "split", axis=1, tiled=True)
    outgoing = jnp.dot(selector, gathered, preferred_element_type=jnp.float32).astype(jnp.bfloat16)
    arrived = lax.all_to_all(outgoing, ("grp", "dev"), split_axis=0, concat_axis=0, tiled=True)
    pre_gate = jnp.dot(arrived, gate_rows, preferred_element_type=jnp.float32)
    pre_up = jnp.dot(arrived, up_rows, preferred_element_type=jnp.float32)
    hidden = (jax.nn.silu(pre_gate) * pre_up).astype(jnp.bfloat16)
    scaled_rows = lax.all_to_all(
        scaled_send, ("grp", "dev"), split_axis=0, concat_axis=0, tiled=True
    )
    piece = lax.all_gather(hidden, "split", axis=1, tiled=True)
    out_total = jnp.dot(piece, down_rows, preferred_element_type=jnp.float32)
    grad_block = lax.dot_general(
        piece, scaled_rows, (((0,), (0,)), ((), ())), preferred_element_type=jnp.float32
    )
    returned = lax.all_to_all(
        out_total.astype(jnp.bfloat16), ("grp", "dev"), split_axis=0, concat_axis=0, tiled=True
    )
    picked = jnp.take(returned, target, axis=0).reshape(tok_rows, top, -1).astype(jnp.float32)
    mixed = jnp.sum(gate_probs[:, :, None] * picked, axis=1).astype(jnp.bfloat16)
    partial_grads = jnp.sum(upstream.astype(jnp.float32)[:, None, :] * picked, axis=2)
    gate_grads = lax.psum(partial_grads, "split")
    return (mixed, gate_grads, grad_block[None])


def solution(mesh):
    return jax.shard_map(
        per_device,
        mesh=mesh,
        in_specs=(
            P(("grp", "dev"), "split"),
            P(("grp", "dev"), "split"),
            P(("grp", "dev"), None),
            P(("grp", "dev"), None),
            P(("grp", "dev"), None, "split"),
            P(("grp", "dev"), None, "split"),
            P(("grp", "dev"), None, "split"),
        ),
        out_specs=(
            P(("grp", "dev"), "split"),
            P(("grp", "dev"), None),
            P(("grp", "dev"), None, "split"),
        ),
        check_vma=False,
    )
```

profile of v0, /device:TPU:1, one launch (start us, length us, event | category | flops | bytes accessed | tf_op | source)
XLA Modules:
  0.0 471.4 jit_solution(9702620589845049706)
XLA Ops:
  7.2 0.9 copy.23
  8.1 0.1 eq.40
  8.2 0.1 reshape.108
  8.3 0.1 copy.26
  8.4 0.2 fusion.9
  8.7 0.1 copy.27
  8.8 0.4 fusion.7
  9.1 0.1 reduce_sum.52
  9.3 10.7 %convert_reduce_fusion = s32[2048,128]{1,0:T(8,128)S(1)} fusion(s32[128,8]{0,1:T(8,128)S(1)} %copy.28), kind=kLoop, calls=%fused_computation.2 | loop fusion | flops 6029312 | bytes 1052672 | tf_op jit(solution)/shard_map/reduce_sum | solution.py:23
  20.0 14.1 %all_gather.6 = bf16[128,2048]{1,0:T(8,128)(2,1)S(1)} all-gather(bf16[128,512]{1,0:T(8,128)(2,1)S(1)} %copy-done.4), channel_id=1, replica_groups=mesh['grp'=4,'dev'=32,'split'=4] {'split'}, dimensions={1}, use_global_device_ids=true | all-gather | bytes 655360 | tf_op jit(solution)/shard_map/all_gather | solution.py:34
  34.2 2.3 convolution_convert_fusion
  36.5 215.6 %all_to_all.36 = bf16[128,16,2048]{2,1,0:T(8,128)(2,1)S(1)} all-to-all(bf16[128,16,2048]{2,1,0:T(8,128)(2,1)S(1)} %bitcast.45), channel_id=1, replica_groups=mesh['grp'=4,'dev'=32,'split'=4] {'grp','dev'}, dimensions={0} | all-to-all | bytes 16777216 | tf_op jit(solution)/shard_map/all_to_all | solution.py:36
  252.1 2.9 fusion.4
  255.0 3.9 fusion
  259.0 10.8 %select_reduce_fusion = f32[2048,128]{1,0:T(8,128)S(1)} fusion(f32[128,8]{0,1:T(8,128)S(1)} %copy-done.5, s32[128,8]{0,1:T(8,128)S(1)} %copy.28), kind=kLoop, calls=%fused_computation.1 | loop fusion | flops 6029312 | bytes 1056768 | tf_op jit(solution)/shard_map/reduce_sum | solution.py:24
  269.8 3.2 convolution_convert_fusion.1
  273.0 7.7 %all-to-all-start.2 = ((bf16[128,16,512]{2,1,0:T(8,128)(2,1)}), bf16[128,16,512]{2,1,0:T(8,128)(2,1)S(1)}, u32[]{:S(2)}, u32[]{:S(2)}) async-start(bf16[128,16,512]{2,1,0:T(8,128)(2,1)} %bitcast.14), calls=%async_computation.2 | async-start | bytes 4194304 | tf_op jit(solution)/shard_map/all_to_all | solution.py:40
  280.8 82.7 %all-gather.2.cloned.1.call-done = bf16[2048,768]{0,1:T(8,128)(2,1)} async-done(((bf16[2048,192]{0,1:T(8,128)(2,1)}), bf16[2048,768]{0,1:T(8,128)(2,1)}) %all-gather.2.cloned.1.call-update) | async-done | bytes 3145744 | tf_op jit(solution)/shard_map/all_gather | solution.py:43
  363.5 5.1 %convolution_convert_fusion.2 = bf16[2048,512]{1,0:T(8,128)(2,1)} fusion(bf16[2048,768]{0,1:T(8,128)(2,1)} %all-gather.2.cloned.1.call-done, bf16[1,768,512]{2,1,0:T(8,128)(2,1)S(1)} %copy-done), kind=kOutput, calls=%fused_computation.6 | convolution fusion | flops 1611661312 | bytes 6029312 | tf_op jit(solution)/shard_map/dot_general | solution.py:44
  368.6 1.4 copy-done.2
  370.0 16.0 %all-to-all-start.1 = ((bf16[128,16,512]{2,1,0:T(8,128)(2,1)}), bf16[128,16,512]{2,1,0:T(8,128)(2,1)S(1)}, u32[]{:S(2)}, u32[]{:S(2)}) async-start(bf16[128,16,512]{2,1,0:T(8,128)(2,1)} %bitcast.50), calls=%async_computation.1 | async-start | bytes 4194304 | tf_op jit(solution)/shard_map/all_to_all | solution.py:48
  386.0 0.1 copy.22
  386.1 0.1 mul.60
  386.2 0.1 broadcast_in_dim.39
  386.3 5.5 %convolution_bitcast_fusion = f32[1,768,512]{2,1,0:T(8,128)} fusion(bf16[2048,768]{0,1:T(8,128)(2,1)} %all-gather.2.cloned.1.call-done, bf16[2048,512]{1,0:T(8,128)(2,1)} %bitcast.49), kind=kOutput, calls=%fused_computation.12 | convolution fusion | flops 1610612736 | bytes 6815744 | tf_op jit(solution)/shard_map/dot_general | solution.py:45
  391.8 49.0 %all-to-all-done.1 = bf16[128,16,512]{2,1,0:T(8,128)(2,1)S(1)} async-done(((bf16[128,16,512]{2,1,0:T(8,128)(2,1)}), bf16[128,16,512]{2,1,0:T(8,128)(2,1)S(1)}, u32[]{:S(2)}, u32[]{:S(2)}) %all-to-all-start.1) | async-done | bytes 2097184 | tf_op jit(solution)/shard_map/all_to_all | solution.py:48
  440.8 5.1 %gather_fusion = bf16[1024,512]{1,0:T(8,128)(2,1)} fusion(bf16[2048,512]{1,0:T(8,128)(2,1)S(1)} %bitcast.46, s32[1024]{0:T(1024)S(1)} %broadcast_clamp_fusion), kind=kCustom, calls=%fused_computation | custom fusion | bytes 2101248 | tf_op jit(solution)/shard_map/jit(_take)/gather | solution.py:51
  445.9 1.9 fusion.1
  447.7 0.1 reduce_sum.57
  447.8 14.6 %psum.7 = f32[128,8]{1,0:T(8,128)S(1)} all-reduce(f32[128,8]{1,0:T(8,128)S(1)} %reduce_sum.57), channel_id=1, replica_groups=mesh['grp'=4,'dev'=32,'split'=4] {'split'}, use_global_device_ids=true, to_apply=%region_6.7 | all-reduce | flops 1024 | bytes 8192 | tf_op jit(solution)/shard_map/psum | solution.py:54
  462.5 0.7 copy.29
  463.1 1.5 multiply_reduce_fusion
  (28 shorter events, 0.3 us)
Async XLA Ops:
  7.2 356.3 %copy-start = (bf16[1,768,512]{2,1,0:T(8,128)(2,1)S(1)}, bf16[1,768,512]{2,1,0:T(8,128)(2,1)}, u32[]{:S(2)}) copy-start(bf16[1,768,512]{2,1,0:T(8,128)(2,1)} %param.13) | copy-start | bytes 2359300
  7.2 356.3 %all-gather.2.cloned.1.call-start = ((), (), s32[]{:S(2)}) async-start(), calls=%async_computation.3 | async-start | bytes 3932160 | tf_op jit(solution)/shard_map/all_gather | solution.py:43
  8.6 11.5 %copy-start.4 = (bf16[128,512]{1,0:T(8,128)(2,1)S(1)}, bf16[128,512]{1,0:T(8,128)(2,1)}, u32[]{:S(2)}) copy-start(bf16[128,512]{1,0:T(8,128)(2,1)} %param.7) | copy-start | bytes 393220
  36.5 215.6 %copy-start.6 = (bf16[1,2048,192]{1,2,0:T(8,128)(2,1)S(1)}, bf16[1,2048,192]{1,2,0:T(8,128)(2,1)}, u32[]{:S(2)}) copy-start(bf16[1,2048,192]{1,2,0:T(8,128)(2,1)} %param.11) | copy-start | bytes 2359300
  252.1 2.9 copy-start.7
  255.0 4.0 copy-start.5
  255.0 14.8 %copy-start.3 = (bf16[128,512]{1,0:T(8,128)(2,1)S(1)}, bf16[128,512]{1,0:T(8,128)(2,1)}, u32[]{:S(2)}) copy-start(bf16[128,512]{1,0:T(8,128)(2,1)} %param.8) | copy-start | bytes 393220
  273.0 95.6 %all-to-all-start.2 = ((bf16[128,16,512]{2,1,0:T(8,128)(2,1)}), bf16[128,16,512]{2,1,0:T(8,128)(2,1)S(1)}, u32[]{:S(2)}, u32[]{:S(2)}) async-start(bf16[128,16,512]{2,1,0:T(8,128)(2,1)} %bitcast.14), calls=%async_computation.2 | async-start | bytes 4194304 | tf_op jit(solution)/shard_map/all_to_all | solution.py:40
  368.6 1.4 copy-start.2
  370.0 70.9 %all-to-all-start.1 = ((bf16[128,16,512]{2,1,0:T(8,128)(2,1)}), bf16[128,16,512]{2,1,0:T(8,128)(2,1)S(1)}, u32[]{:S(2)}, u32[]{:S(2)}) async-start(bf16[128,16,512]{2,1,0:T(8,128)(2,1)} %bitcast.50), calls=%async_computation.1 | async-start | bytes 4194304 | tf_op jit(solution)/shard_map/all_to_all | solution.py:48
  445.9 17.2 %copy-start.1 = (bf16[1024,512]{1,0:T(8,128)(2,1)S(1)}, bf16[1024,512]{1,0:T(8,128)(2,1)}, u32[]{:S(2)}) copy-start(bf16[1024,512]{1,0:T(8,128)(2,1)} %gather_fusion) | copy-start | bytes 3145732
Sparse Core Ops, SparseCore 0:
  259.1 104.3 all-gather.1
where the time goes:
time: 476 us; the launch traced here: 471 us
  blocking collectives  244 us (51%)
  waiting for transfers between devices  132 us (28%)
  other arithmetic  25.5 us (5%)
  starting transfers between devices  23.8 us (5%)
  matrix products  22.9 us (5%)
  between operations  14.2 us (3%)
  local copies, waits for them, and re-layouts  8.9 us (2%)
    all_to_all x1, blocking collectives, per_device(): lax.all_to_all(outgoing, ('grp', 'dev'), split_axis=0, concat_axis=0, til...  216 us
    all_gather x1, waiting for transfers between devices, per_device(): piece = lax.all_gather(hidden, 'split', axis=1, tiled=True)  82.7 us
    all_to_all x1, waiting for transfers between devices, per_device(): lax.all_to_all(out_total.astype(jnp.bfloat16), ('grp', 'dev'), split_axis...  49 us
    all_to_all x1, starting transfers between devices, per_device(): lax.all_to_all(out_total.astype(jnp.bfloat16), ('grp', 'dev'), split_axis...  16 us
    psum x1, blocking collectives, per_device(): gate_grads = lax.psum(partial_grads, 'split')  14.6 us
    all_gather x1, blocking collectives, per_device(): gathered = lax.all_gather(tokens, 'split', axis=1, tiled=True)  14.1 us
    reduce_sum x1, other arithmetic, per_device(): weighted = jnp.sum(jnp.where(matched, gate_probs[None, :, :], 0.0), axis=2)  10.8 us
    reduce_sum x1, other arithmetic, per_device(): selector = jnp.sum(matched.astype(jnp.int32), axis=2).astype(jnp.bfloat16)  10.7 us
  transfers between devices with their start and end apart: 3, of which 2 were waited for; matrix products, arithmetic and copies ran while one was open for 5% of the time, Pallas kernels for 0%

commit v1 on v0

v1 whole, which is shorter than its diff:
```python
import jax
import jax.numpy as jnp
from jax import lax
from jax.sharding import PartitionSpec as P

SLOTS = 16


def bf16_pieces(x, count):
    pieces = []
    for _ in range(count):
        top = lax.reduce_precision(x, exponent_bits=8, mantissa_bits=7)
        pieces.append(top.astype(jnp.bfloat16))
        x = x - top
    return pieces


def per_device(tokens, upstream, expert_ids, gate_probs, w_gate, w_up, w_down):
    grp = lax.axis_size("grp")
    dev = lax.axis_size("dev")
    split = lax.axis_size("split")
    grp_me = lax.axis_index("grp")
    split_me = lax.axis_index("split")
    rows, top = expert_ids.shape
    feats = tokens.shape[1]
    hidden_part = w_gate.shape[2]
    f32, bf16 = jnp.float32, jnp.bfloat16

    w_own = jnp.concatenate([w_gate[0].T, w_up[0].T], axis=0)
    w_all = lax.all_gather(w_own, "split", axis=0, tiled=False)

    ids_t = expert_ids.T.astype(bf16)
    meta = jnp.concatenate([ids_t] + bf16_pieces(gate_probs.T, 3), axis=0)
    meta = meta.reshape(-1, 2 * feats)
    meta = jnp.pad(meta, ((0, SLOTS - meta.shape[0]), (0, 0)))
    both = jnp.concatenate([jnp.concatenate([tokens, upstream], axis=1), meta], axis=0)
    both = jnp.broadcast_to(both[None], (grp,) + both.shape)
    near = lax.all_to_all(both, "grp", split_axis=0, concat_axis=0, tiled=True)
    near_tokens = near[:, :rows, :feats]
    near_upstream = near[:, :rows, feats:]
    near_meta = near[:, rows : rows + 4 * top * rows // (2 * feats), :].reshape(grp, 4, top, rows).astype(f32)
    near_ids = near_meta[:, 0]
    near_gates = near_meta[:, 1] + near_meta[:, 2] + near_meta[:, 3]

    mine = lax.all_to_all(near_tokens, "split", split_axis=0, concat_axis=0, tiled=True)
    mine = jnp.concatenate([mine[i] for i in range(split)], axis=1)

    expert = (grp_me * dev).astype(f32) + lax.broadcasted_iota(f32, (1, dev, 1), 1)
    equal = [near_ids[:, k][:, None, :] == expert for k in range(top)]
    member = sum(e.astype(f32) for e in equal)
    gate_of = sum(jnp.where(e, near_gates[:, k][:, None, :], 0.0) for k, e in enumerate(equal))
    before = (
        lax.broadcasted_iota(jnp.int32, (rows, rows), 0) < lax.broadcasted_iota(jnp.int32, (rows, rows), 1)
    ).astype(bf16)
    place = jnp.dot(member.astype(bf16).reshape(grp * dev, rows), before, preferred_element_type=f32)
    place = jnp.where(member > 0, place.reshape(grp, dev, rows), -1.0)
    slot = lax.broadcasted_iota(f32, (1, 1, SLOTS, 1), 2)
    chosen = place[:, :, None, :] == slot
    pick = chosen.astype(bf16).reshape(grp, dev * SLOTS, rows)
    weight = jnp.where(chosen, gate_of[:, :, None, :], 0.0).reshape(grp, dev * SLOTS, rows)
    gate_row = jnp.sum(weight, axis=2, keepdims=True)

    pick_mine = lax.dynamic_index_in_dim(pick, split_me, 0, keepdims=False)
    send = jnp.dot(pick_mine, mine, preferred_element_type=f32).astype(bf16)
    arrived = lax.all_to_all(
        send.reshape(dev, SLOTS, split * feats), "dev", split_axis=0, concat_axis=0, tiled=True
    ).reshape(dev * SLOTS, split * feats)
    scaled = jnp.einsum("grt,gtd->grd", pick, near_upstream, preferred_element_type=f32)
    scaled = (scaled * gate_row).astype(bf16).reshape(grp, dev, SLOTS, feats)
    arrived, scaled = lax.optimization_barrier((arrived, scaled))
    scaled_rows = lax.all_to_all(scaled, "dev", split_axis=1, concat_axis=1, tiled=True)
    scaled_rows = scaled_rows.reshape(grp, dev * SLOTS, feats)
    arrived, scaled_rows = lax.optimization_barrier((arrived, scaled_rows))

    pre = lax.dot_general(
        w_all.reshape(split * 2 * hidden_part, split * feats),
        arrived,
        (((1,), (1,)), ((), ())),
        preferred_element_type=f32,
    ).reshape(split, 2, hidden_part, dev * SLOTS)
    hidden = (jax.nn.silu(pre[:, 0]) * pre[:, 1]).astype(bf16).reshape(split * hidden_part, dev * SLOTS)
    hidden_all = lax.all_gather(hidden, "split", axis=0, tiled=False)

    out = jnp.einsum("gfr,fd->grd", hidden_all, w_down[0], preferred_element_type=f32).astype(bf16)
    returned = lax.all_to_all(
        out.reshape(grp, dev, SLOTS, feats), "dev", split_axis=1, concat_axis=1, tiled=True
    ).reshape(grp, dev * SLOTS, feats)
    grad_block = sum(
        jnp.dot(hidden_all[g], scaled_rows[g], preferred_element_type=f32) for g in range(grp)
    )

    mixed = sum(
        jnp.einsum("grt,grd->gtd", piece, returned, preferred_element_type=f32)
        for piece in bf16_pieces(weight, 2)
    ).astype(bf16)
    mixed = lax.all_to_all(mixed, "grp", split_axis=0, concat_axis=0, tiled=True)
    mixed = jnp.sum(mixed.astype(f32), axis=0).astype(bf16)

    dots = jnp.einsum("grd,gtd->grt", returned, near_upstream, preferred_element_type=f32)
    dots = jnp.where(chosen, dots.reshape(grp, dev, SLOTS, rows), 0.0).sum(axis=2)
    grads = jnp.stack([jnp.sum(jnp.where(e, dots, 0.0), axis=1) for e in equal], axis=1)
    grads = jnp.broadcast_to(grads[:, None], (grp, split, top, rows)).reshape(grp * split, top, rows)
    grads = lax.all_to_all(grads, ("grp", "split"), split_axis=0, concat_axis=0, tiled=True)
    gate_grads = jnp.sum(grads, axis=0).T
    return (mixed, gate_grads, grad_block[None])


def solution(mesh):
    return jax.shard_map(
        per_device,
        mesh=mesh,
        in_specs=(
            P(("grp", "dev"), "split"),
            P(("grp", "dev"), "split"),
            P(("grp", "dev"), None),
            P(("grp", "dev"), None),
            P(("grp", "dev"), None, "split"),
            P(("grp", "dev"), None, "split"),
            P(("grp", "dev"), None, "split"),
        ),
        out_specs=(
            P(("grp", "dev"), "split"),
            P(("grp", "dev"), None),
            P(("grp", "dev"), None, "split"),
        ),
        check_vma=False,
    )
```

time: 476 us -> 398 us (0.84)
  blocking collectives: 244 us -> 48.7 us
  waiting for transfers between devices: 132 us -> 226 us
  starting transfers between devices: 23.8 us -> 60.8 us
  other arithmetic: 25.5 us -> 8.57 us
  matrix products: 22.9 us -> 27.7 us
    all_to_all x1, blocking collectives: 216 us -> 48.7 us  [per_device(): lax.all_to_all(scaled, 'dev', split_axis=1, concat_axis=1, tiled=True)]
    all_to_all x2 -> x6, waiting for transfers between devices: 49 us -> 152 us  [the longest x1 44.7 us: per_device(): lax.all_to_all(out.reshape(grp, dev, SLOTS, feats), 'dev', split_axis=1,...]
    all_to_all x2 -> x6, starting transfers between devices: 23.7 us -> 60.8 us  [the longest x1 24.7 us: per_device(): lax.all_to_all(send.reshape(dev, SLOTS, split * feats), 'dev', split_axis...]
    reduce_sum x5 -> x4, other arithmetic: 25.2 us -> 1.87 us  [the longest x1 0.75 us: per_device(): mixed = jnp.sum(mixed.astype(f32), axis=0).astype(bf16)]
    psum x1 -> x0, blocking collectives: 14.6 us -> none  [per_device(): gate_grads = lax.psum(partial_grads, 'split')]
    all_gather x1 -> x0, blocking collectives: 14.1 us -> none  [per_device(): gathered = lax.all_gather(tokens, 'split', axis=1, tiled=True)]
    all_gather x1 -> x2, waiting for transfers between devices: 82.7 us -> 73.4 us  [the longest x1 73.4 us: per_device(): hidden_all = lax.all_gather(hidden, 'split', axis=0, tiled=False)]
    gather x1 -> x0, local copies, waits for them, and re-layouts: 5.06 us -> none  [per_device(): jnp.take(returned, target, axis=0).reshape(tok_rows, top, -1)]
  transfers between devices with their start and end apart: 3 -> 8, of which waited for: 2 -> 7; matrix products, arithmetic and copies ran while one was open for 5% -> 5% of each run, Pallas kernels for 0% -> 0%
where the time goes in v1:
time: 398 us; the launch traced here: 394 us
  waiting for transfers between devices  226 us (57%)
  starting transfers between devices  60.8 us (15%)
  blocking collectives  48.7 us (12%)
  matrix products  27.7 us (7%)
  between operations  14.5 us (4%)
  other arithmetic  8.57 us (2%)
  local copies, waits for them, and re-layouts  7.83 us (2%)
    all_gather x1, waiting for transfers between devices, per_device(): hidden_all = lax.all_gather(hidden, 'split', axis=0, tiled=False)  73.4 us
    all_to_all x1, blocking collectives, per_device(): lax.all_to_all(scaled, 'dev', split_axis=1, concat_axis=1, tiled=True)  48.7 us
    all_to_all x1, waiting for transfers between devices, per_device(): lax.all_to_all(out.reshape(grp, dev, SLOTS, feats), 'dev', split_axis=1,...  44.7 us
    all_to_all x1, waiting for transfers between devices, per_device(): lax.all_to_all(send.reshape(dev, SLOTS, split * feats), 'dev', split_axis...  42.2 us
    all_to_all x1, waiting for transfers between devices, per_device(): lax.all_to_all(near_tokens, 'split', split_axis=0, concat_axis=0, tiled=T...  27.5 us
    all_to_all x1, waiting for transfers between devices, per_device(): near = lax.all_to_all(both, 'grp', split_axis=0, concat_axis=0, tiled=True)  26.8 us
    all_to_all x1, starting transfers between devices, per_device(): lax.all_to_all(send.reshape(dev, SLOTS, split * feats), 'dev', split_axis...  24.7 us
    all_to_all x1, starting transfers between devices, per_device(): near = lax.all_to_all(both, 'grp', split_axis=0, concat_axis=0, tiled=True)  10.4 us
  transfers between devices with their start and end apart: 8, of which 7 were waited for; matrix products, arithmetic and copies ran while one was open for 5% of the time, Pallas kernels for 0%

profile of v1, /device:TPU:1, one launch (start us, length us, event | category | flops | bytes accessed | tf_op | source)
XLA Modules:
  0.0 393.9 jit_solution(3377651404707074661)
XLA Ops:
  8.7 1.1 fusion.28
  9.8 1.2 broadcast_in_dim.116
  11.0 10.4 %all-to-all-start = ((bf16[4,144,1024]{2,1,0:T(8,128)(2,1)}), bf16[4,144,1024]{2,1,0:T(8,128)(2,1)S(1)}, u32[]{:S(2)}, u32[]{:S(2)}) async-start(bf16[4,144,1024]{2,1,0:T(8,128)(2,1)} %broadcast_in_dim.116), calls=%async_computation | async-start | bytes 2359296 | tf_op jit(solution)/shard_map/all_to_all | solution.py:38
  21.4 1.2 pad_maximum_fusion
  22.7 26.8 %all-to-all-done = bf16[4,144,1024]{2,1,0:T(8,128)(2,1)S(1)} async-done(((bf16[4,144,1024]{2,1,0:T(8,128)(2,1)}), bf16[4,144,1024]{2,1,0:T(8,128)(2,1)S(1)}, u32[]{:S(2)}, u32[]{:S(2)}) %all-to-all-start) | async-done | bytes 1179680 | tf_op jit(solution)/shard_map/all_to_all | solution.py:38
  49.6 1.0 slice.169
  50.6 3.5 all-to-all-start.1
  54.6 27.5 %all-to-all-done.1 = bf16[4,128,512]{2,1,0:T(8,128)(2,1)S(1)} async-done(((bf16[4,128,512]{2,1,0:T(8,128)(2,1)}), bf16[4,128,512]{2,1,0:T(8,128)(2,1)S(1)}, u32[]{:S(2)}, u32[]{:S(2)}) %all-to-all-start.1) | async-done | bytes 524320 | tf_op jit(solution)/shard_map/all_to_all | solution.py:45
  82.2 2.0 convolution_convert_fusion
  84.3 24.7 %all-to-all-start.2 = ((bf16[32,16,2048]{2,1,0:T(8,128)(2,1)}), bf16[32,16,2048]{2,1,0:T(8,128)(2,1)}, u32[]{:S(2)}, u32[]{:S(2)}) async-start(bf16[32,16,2048]{2,1,0:T(8,128)(2,1)} %bitcast.33), calls=%async_computation.2 | async-start | bytes 4194304 | tf_op jit(solution)/shard_map/all_to_all | solution.py:65
  109.7 1.7 multiply_convert_fusion
  111.4 42.2 %all-to-all-done.2 = bf16[32,16,2048]{2,1,0:T(8,128)(2,1)} async-done(((bf16[32,16,2048]{2,1,0:T(8,128)(2,1)}), bf16[32,16,2048]{2,1,0:T(8,128)(2,1)}, u32[]{:S(2)}, u32[]{:S(2)}) %all-to-all-start.2) | async-done | bytes 2097184 | tf_op jit(solution)/shard_map/all_to_all | solution.py:65
  153.8 48.7 %all_to_all.35 = bf16[4,32,16,512]{3,2,0,1:T(8,128)(2,1)S(1)} all-to-all(bf16[4,32,16,512]{3,2,0,1:T(8,128)(2,1)S(1)} %copy.58), channel_id=1, replica_groups=mesh['grp'=4,'dev'=32,'split'=4] {'dev'}, dimensions={1} | all-to-all | bytes 4194304 | tf_op jit(solution)/shard_map/all_to_all | solution.py:71
  202.8 7.0 %fusion = f32[4,2,192,512]{3,2,1,0:T(8,128)S(1)} fusion(bf16[4,2,192,2048]{3,2,1,0:T(8,128)(2,1)} %bitcast.163, bf16[512,2048]{1,0:T(8,128)(2,1)} %bitcast.34), kind=kOutput, calls=%fused_computation.2 | convolution fusion | flops 3221225472 | bytes 11534336 | tf_op jit(solution)/shard_map/dot_general | solution.py:75
  210.1 1.4 multiply_convert_fusion.1
  211.5 73.4 %all-gather.4.cloned.1.call-done = bf16[4,768,512]{2,1,0:T(8,128)(2,1)} async-done(((bf16[1,768,512]{2,1,0:T(8,128)(2,1)}), bf16[4,768,512]{2,1,0:T(8,128)(2,1)}) %all-gather.4.cloned.1.call-update) | async-done | bytes 3145744 | tf_op jit(solution)/shard_map/all_gather | solution.py:82
  284.9 3.7 convolution_convert_fusion.1
  288.6 1.6 copy.61
  290.2 10.1 %all-to-all-start.4 = ((bf16[4,32,16,512]{3,2,0,1:T(8,128)(2,1)}), bf16[4,32,16,512]{3,2,0,1:T(8,128)(2,1)}, u32[]{:S(2)}, u32[]{:S(2)}) async-start(bf16[4,32,16,512]{3,2,0,1:T(8,128)(2,1)} %copy.61), calls=%async_computation.4 | async-start | bytes 4194304 | tf_op jit(solution)/shard_map/all_to_all | solution.py:85
  300.3 1.1 fusion.4
  301.4 2.8 fusion.6
  304.2 44.7 %all-to-all-done.4 = bf16[4,32,16,512]{3,2,0,1:T(8,128)(2,1)} async-done(((bf16[4,32,16,512]{3,2,0,1:T(8,128)(2,1)}), bf16[4,32,16,512]{3,2,0,1:T(8,128)(2,1)}, u32[]{:S(2)}, u32[]{:S(2)}) %all-to-all-start.4) | async-done | bytes 2097184 | tf_op jit(solution)/shard_map/all_to_all | solution.py:85
  348.9 1.8 copy.62
  350.8 1.8 select_reduce_fusion
  353.5 8.4 %all-to-all-start.6 = ((f32[16,8,128]{2,1,0:T(8,128)}), f32[16,8,128]{2,1,0:T(8,128)S(1)}, u32[]{:S(2)}, u32[]{:S(2)}) async-start(f32[16,8,128]{2,1,0:T(8,128)} %bitcast.54), calls=%async_computation.6 | async-start | bytes 131072 | tf_op jit(solution)/shard_map/all_to_all | solution.py:103
  362.9 1.4 fusion.2
  364.2 5.2 %all-to-all-done.6 = f32[16,8,128]{2,1,0:T(8,128)S(1)} async-done(((f32[16,8,128]{2,1,0:T(8,128)}), f32[16,8,128]{2,1,0:T(8,128)S(1)}, u32[]{:S(2)}, u32[]{:S(2)}) %all-to-all-start.6) | async-done | bytes 65568 | tf_op jit(solution)/shard_map/all_to_all | solution.py:103
  369.4 3.8 all-to-all-start.5
  373.3 1.8 fusion.7
  375.1 1.8 fusion.5
  377.0 2.9 add_bitcast_fusion
  380.4 5.9 %all-to-all-done.5 = bf16[4,128,512]{2,1,0:T(8,128)(2,1)S(1)} async-done(((bf16[4,128,512]{2,1,0:T(8,128)(2,1)}), bf16[4,128,512]{2,1,0:T(8,128)(2,1)S(1)}, u32[]{:S(2)}, u32[]{:S(2)}) %all-to-all-start.5) | async-done | bytes 524320 | tf_op jit(solution)/shard_map/all_to_all | solution.py:96
  (73 shorter events, 6.8 us)
Async XLA Ops:
  7.2 277.7 %copy-start = (bf16[1,768,512]{2,1,0:T(8,128)(2,1)S(1)}, bf16[1,768,512]{2,1,0:T(8,128)(2,1)}, u32[]{:S(2)}) copy-start(bf16[1,768,512]{2,1,0:T(8,128)(2,1)} %param.13) | copy-start | bytes 2359300
  8.7 12.7 %copy-start.6 = (bf16[1,2048,192]{1,2,0:T(8,128)(2,1)S(1)}, bf16[1,2048,192]{1,2,0:T(8,128)(2,1)}, u32[]{:S(2)}) copy-start(bf16[1,2048,192]{1,2,0:T(8,128)(2,1)} %param.12) | copy-start | bytes 2359300
  8.7 12.7 %copy-start.7 = (bf16[1,2048,192]{1,2,0:T(8,128)(2,1)S(1)}, bf16[1,2048,192]{1,2,0:T(8,128)(2,1)}, u32[]{:S(2)}) copy-start(bf16[1,2048,192]{1,2,0:T(8,128)(2,1)} %param.11) | copy-start | bytes 2359300
  11.0 38.6 %all-to-all-start = ((bf16[4,144,1024]{2,1,0:T(8,128)(2,1)}), bf16[4,144,1024]{2,1,0:T(8,128)(2,1)S(1)}, u32[]{:S(2)}, u32[]{:S(2)}) async-start(bf16[4,144,1024]{2,1,0:T(8,128)(2,1)} %broadcast_in_dim.116), calls=%async_computation | async-start | bytes 2359296 | tf_op jit(solution)/shard_map/all_to_all | solution.py:38
  21.3 181.4 %all-gather.6.cloned.1.call-start = ((), (), s32[]{:S(2)}) async-start(), calls=%async_computation.8 | async-start | bytes 7864320 | tf_op jit(solution)/shard_map/all_gather | solution.py:30
  22.7 86.3 %copy-start.18 = (f32[32]{0:T(128)}, f32[32]{0:T(128)S(1)}, u32[]{:S(2)}) copy-start(f32[32]{0:T(128)S(1)} %iota_add_fusion) | copy-start | bytes 388
  49.6 32.7 %copy-start.3 = (bf16[4,144,1024]{2,1,0:T(8,128)(2,1)}, bf16[4,144,1024]{2,1,0:T(8,128)(2,1)S(1)}, u32[]{:S(2)}) copy-start(bf16[4,144,1024]{2,1,0:T(8,128)(2,1)S(1)} %all-to-all-done) | copy-start | bytes 3538948
  50.6 31.6 %all-to-all-start.1 = ((bf16[4,128,512]{2,1,0:T(8,128)(2,1)}), bf16[4,128,512]{2,1,0:T(8,128)(2,1)S(1)}, u32[]{:S(2)}, u32[]{:S(2)}) async-start(bf16[4,128,512]{2,1,0:T(8,128)(2,1)} %slice.169), calls=%async_computation.1 | async-start | bytes 1048576 | tf_op jit(solution)/shard_map/all_to_all | solution.py:45
  54.1 54.9 %copy-start.8 = (f32[4,128]{1,0:T(4,128)}, f32[4,128]{1,0:T(4,128)S(1)}, u32[]{:S(2)}) copy-start(f32[4,128]{1,0:T(4,128)S(1)} %get-tuple-element.34) | copy-start | bytes 6148
  54.1 54.9 %copy-start.10 = (f32[4,128]{1,0:T(4,128)}, f32[4,128]{1,0:T(4,128)S(1)}, u32[]{:S(2)}) copy-start(f32[4,128]{1,0:T(4,128)S(1)} %get-tuple-element.35) | copy-start | bytes 6148
  54.1 54.9 %copy-start.12 = (f32[4,128]{1,0:T(4,128)}, f32[4,128]{1,0:T(4,128)S(1)}, u32[]{:S(2)}) copy-start(f32[4,128]{1,0:T(4,128)S(1)} %get-tuple-element.36) | copy-start | bytes 6148
  54.2 54.9 %copy-start.14 = (f32[4,128]{1,0:T(4,128)}, f32[4,128]{1,0:T(4,128)S(1)}, u32[]{:S(2)}) copy-start(f32[4,128]{1,0:T(4,128)S(1)} %get-tuple-element.37) | copy-start | bytes 6148
  54.2 54.9 %copy-start.16 = (f32[4,128]{1,0:T(4,128)}, f32[4,128]{1,0:T(4,128)S(1)}, u32[]{:S(2)}) copy-start(f32[4,128]{1,0:T(4,128)S(1)} %get-tuple-element.38) | copy-start | bytes 6148
  84.3 69.3 %all-to-all-start.2 = ((bf16[32,16,2048]{2,1,0:T(8,128)(2,1)}), bf16[32,16,2048]{2,1,0:T(8,128)(2,1)}, u32[]{:S(2)}, u32[]{:S(2)}) async-start(bf16[32,16,2048]{2,1,0:T(8,128)(2,1)} %bitcast.33), calls=%async_computation.2 | async-start | bytes 4194304 | tf_op jit(solution)/shard_map/all_to_all | solution.py:65
  109.0 175.9 %all-gather.4.cloned.1.call-start = ((), (), s32[]{:S(2)}) async-start(), calls=%async_computation.7 | async-start | bytes 3932160 | tf_op jit(solution)/shard_map/all_gather | solution.py:82
  202.7 98.6 %copy-start.1 = (bf16[4,32,16,512]{3,2,1,0:T(8,128)(2,1)}, bf16[4,32,16,512]{3,2,1,0:T(8,128)(2,1)S(1)}, u32[]{:S(2)}) copy-start(bf16[4,32,16,512]{3,2,1,0:T(8,128)(2,1)S(1)} %copy.59) | copy-start | bytes 6291460
  290.2 58.7 %all-to-all-start.4 = ((bf16[4,32,16,512]{3,2,0,1:T(8,128)(2,1)}), bf16[4,32,16,512]{3,2,0,1:T(8,128)(2,1)}, u32[]{:S(2)}, u32[]{:S(2)}) async-start(bf16[4,32,16,512]{3,2,0,1:T(8,128)(2,1)} %copy.61), calls=%async_computation.4 | async-start | bytes 4194304 | tf_op jit(solution)/shard_map/all_to_all | solution.py:85
  350.7 1.9 copy-start.9
  350.7 1.9 copy-start.11
  350.7 1.8 copy-start.13
  350.8 1.8 copy-start.15
  350.8 1.8 copy-start.17
  350.8 1.8 copy-start.19
  353.5 16.0 %all-to-all-start.6 = ((f32[16,8,128]{2,1,0:T(8,128)}), f32[16,8,128]{2,1,0:T(8,128)S(1)}, u32[]{:S(2)}, u32[]{:S(2)}) async-start(f32[16,8,128]{2,1,0:T(8,128)} %bitcast.54), calls=%async_computation.6 | async-start | bytes 131072 | tf_op jit(solution)/shard_map/all_to_all | solution.py:103
  361.8 1.0 copy-start.5
  364.2 10.9 %copy-start.2 = (bf16[4,32,16,512]{3,2,1,0:T(8,128)(2,1)S(1)}, bf16[4,32,16,512]{3,2,1,0:T(8,128)(2,1)}, u32[]{:S(2)}) copy-start(bf16[4,32,16,512]{3,2,1,0:T(8,128)(2,1)} %copy-done.1) | copy-start | bytes 6291460
  369.4 16.9 %all-to-all-start.5 = ((bf16[4,128,512]{2,1,0:T(8,128)(2,1)}), bf16[4,128,512]{2,1,0:T(8,128)(2,1)S(1)}, u32[]{:S(2)}, u32[]{:S(2)}) async-start(bf16[4,128,512]{2,1,0:T(8,128)(2,1)} %fusion.2), calls=%async_computation.5 | async-start | bytes 1048576 | tf_op jit(solution)/shard_map/all_to_all | solution.py:96
  375.1 1.8 copy-start.4
Sparse Core Ops, SparseCore 0:
  24.8 132.9 all-gather.5
  211.6 73.2 all-gather.3

commit v2 on v1

v2 whole, which is shorter than its diff:
```python
import jax
import jax.numpy as jnp
from jax import lax
from jax.sharding import PartitionSpec as P

SLOTS = 16


def bf16_pieces(x, count):
    pieces = []
    for _ in range(count):
        top = lax.reduce_precision(x, exponent_bits=8, mantissa_bits=7)
        pieces.append(top.astype(jnp.bfloat16))
        x = x - top
    return pieces


def per_device(tokens, upstream, expert_ids, gate_probs, w_gate, w_up, w_down):
    grp = lax.axis_size("grp")
    dev = lax.axis_size("dev")
    split = lax.axis_size("split")
    grp_me = lax.axis_index("grp")
    split_me = lax.axis_index("split")
    rows, top = expert_ids.shape
    feats = tokens.shape[1]
    hidden_part = w_gate.shape[2]
    f32, bf16 = jnp.float32, jnp.bfloat16

    w_own = jnp.concatenate([w_gate[0].T, w_up[0].T], axis=0)
    w_all = lax.all_gather(w_own, "split", axis=0, tiled=False)

    def flipped(size, bits):
        return [(i, i ^ bits) for i in range(size)]

    def spread(x):
        x = jnp.broadcast_to(x[None], (grp,) + x.shape)
        return lax.all_to_all(x, "grp", split_axis=0, concat_axis=0, tiled=True)

    def relative(x):
        parts = [lax.dynamic_index_in_dim(x, split_me ^ j, 0, keepdims=True) for j in range(grp)]
        return jnp.concatenate(parts, axis=0)

    meta = jnp.concatenate([expert_ids.T.astype(bf16)] + bf16_pieces(gate_probs.T, 3), axis=0)
    meta = meta.reshape(-1, feats)
    meta_rows = meta.shape[0]
    meta = jnp.pad(meta, ((0, SLOTS - meta_rows), (0, 0)))
    near = spread(jnp.concatenate([upstream, meta], axis=0))
    near_meta = relative(near[:, rows : rows + meta_rows].reshape(grp, 4, top, rows).astype(f32))
    near_ids = near_meta[:, 0]
    near_gates = near_meta[:, 1] + near_meta[:, 2] + near_meta[:, 3]
    near_upstream = relative(near[:, :rows])

    near_tokens = jnp.stack(
        [tokens] + [lax.ppermute(tokens, "grp", flipped(grp, m)) for m in range(1, grp)]
    )
    mine = []
    for m in range(split):
        piece = lax.dynamic_index_in_dim(near_tokens, grp_me ^ split_me ^ m, 0, keepdims=False)
        mine.append(lax.ppermute(piece, "split", flipped(split, m)) if m > 0 else piece)
    mine = relative(jnp.stack(mine))
    mine = jnp.concatenate([mine[i] for i in range(split)], axis=1)

    expert = (grp_me * dev).astype(f32) + lax.broadcasted_iota(f32, (1, dev, 1), 1)
    equal = [near_ids[:, k][:, None, :] == expert for k in range(top)]
    member = sum(e.astype(f32) for e in equal)
    gate_of = sum(jnp.where(e, near_gates[:, k][:, None, :], 0.0) for k, e in enumerate(equal))
    before = (
        lax.broadcasted_iota(jnp.int32, (rows, rows), 0) < lax.broadcasted_iota(jnp.int32, (rows, rows), 1)
    ).astype(bf16)
    place = jnp.dot(member.astype(bf16).reshape(grp * dev, rows), before, preferred_element_type=f32)
    place = jnp.where(member > 0, place.reshape(grp, dev, rows), -1.0)
    slot = lax.broadcasted_iota(f32, (1, 1, SLOTS, 1), 2)
    chosen = place[:, :, None, :] == slot
    pick = chosen.astype(bf16).reshape(grp, dev * SLOTS, rows)
    weight = jnp.where(chosen, gate_of[:, :, None, :], 0.0).reshape(grp, dev * SLOTS, rows)
    gate_row = jnp.sum(weight, axis=2, keepdims=True)

    scaled = jnp.einsum("grt,gtd->grd", pick, near_upstream, preferred_element_type=f32)
    scaled = (scaled * gate_row).astype(bf16).reshape(grp, dev, SLOTS, feats)
    scaled_rows = lax.all_to_all(scaled, "dev", split_axis=1, concat_axis=1, tiled=True)
    scaled_rows = scaled_rows.reshape(grp, dev * SLOTS, feats)
    send = jnp.dot(pick[0], mine, preferred_element_type=f32).astype(bf16)
    send, scaled_rows = lax.optimization_barrier((send, scaled_rows))
    arrived = lax.all_to_all(
        send.reshape(dev, SLOTS, split * feats), "dev", split_axis=0, concat_axis=0, tiled=True
    ).reshape(dev * SLOTS, split * feats)

    pre = lax.dot_general(
        w_all.reshape(split * 2 * hidden_part, split * feats),
        arrived,
        (((1,), (1,)), ((), ())),
        preferred_element_type=f32,
    ).reshape(split, 2, hidden_part, dev * SLOTS)
    hidden = (jax.nn.silu(pre[:, 0]) * pre[:, 1]).astype(bf16).reshape(split * hidden_part, dev * SLOTS)
    hidden_of = [hidden]
    hidden_of.append(lax.ppermute(hidden, "split", flipped(split, 1)))
    hidden_of.append(lax.ppermute(hidden, "split", flipped(split, 2)))
    hidden_of[1:] = lax.optimization_barrier(tuple(hidden_of[1:]))
    hidden_of.append(lax.ppermute(hidden_of[2], "split", flipped(split, 1)))

    mixed, dots = [], []
    for j in range(0, grp, 2):
        two = slice(j, j + 2)
        out = jnp.stack(
            [
                lax.dot_general(h, w_down[0], (((0,), (0,)), ((), ())), preferred_element_type=f32).astype(bf16)
                for h in hidden_of[two]
            ]
        )
        returned = lax.all_to_all(
            out.reshape(2, dev, SLOTS, feats), "dev", split_axis=1, concat_axis=1, tiled=True
        ).reshape(2, dev * SLOTS, feats)
        mixed.append(
            sum(
                jnp.einsum("grt,grd->gtd", piece, returned, preferred_element_type=f32)
                for piece in bf16_pieces(weight[two], 2)
            ).astype(bf16)
        )
        part = jnp.einsum("grd,gtd->grt", returned, near_upstream[two], preferred_element_type=f32)
        dots.append(jnp.where(chosen[two], part.reshape(2, dev, SLOTS, rows), 0.0).sum(axis=2))
    mixed = jnp.concatenate(mixed, axis=0)
    dots = jnp.concatenate(dots, axis=0)
    grads = jnp.stack([jnp.sum(jnp.where(e, dots, 0.0), axis=1) for e in equal], axis=1)
    grads = relative(grads)
    grads = jnp.broadcast_to(grads[:, None], (grp, split, top, rows)).reshape(grp * split, top, rows)
    grads = lax.all_to_all(grads, ("grp", "split"), split_axis=0, concat_axis=0, tiled=True)
    gate_grads = jnp.sum(grads, axis=0).T

    total = 0.0
    for m in range(grp):
        piece = lax.dynamic_index_in_dim(mixed, grp_me ^ split_me ^ m, 0, keepdims=False)
        if m > 0:
            piece = lax.ppermute(piece, "grp", flipped(grp, m))
        total = total + piece.astype(f32)

    grad_block = sum(
        jnp.dot(hidden_of[j], scaled_rows[j], preferred_element_type=f32) for j in range(grp)
    )
    return (total.astype(bf16), gate_grads, grad_block[None])


def solution(mesh):
    return jax.shard_map(
        per_device,
        mesh=mesh,
        in_specs=(
            P(("grp", "dev"), "split"),
            P(("grp", "dev"), "split"),
            P(("grp", "dev"), None),
            P(("grp", "dev"), None),
            P(("grp", "dev"), None, "split"),
            P(("grp", "dev"), None, "split"),
            P(("grp", "dev"), None, "split"),
        ),
        out_specs=(
            P(("grp", "dev"), "split"),
            P(("grp", "dev"), None),
            P(("grp", "dev"), None, "split"),
        ),
        check_vma=False,
    )
```

time: 398 us -> 343 us (0.86)
  waiting for transfers between devices: 226 us -> 119 us
  starting transfers between devices: 60.8 us -> 100 us
  blocking collectives: 48.7 us -> 57.4 us
  local copies, waits for them, and re-layouts: 7.83 us -> 15.9 us
  matrix products: 27.7 us -> 23.2 us
    all_to_all x5 -> x4, waiting for transfers between devices: 147 us -> 28.2 us  [the longest x1 14.1 us: spread(): return lax.all_to_all(x, 'grp', split_axis=0, concat_axis=0, tiled=True)]
    ppermute x0 -> x12, waiting for transfers between devices: none -> 90.8 us  [the longest x1 32 us: per_device(): hidden_of.append(lax.ppermute(hidden, 'split', flipped(split, 2)))]
    all_gather x1 -> x0, waiting for transfers between devices: 73.4 us -> none  [per_device(): hidden_all = lax.all_gather(hidden, 'split', axis=0, tiled=False)]
    ppermute x0 -> x12, starting transfers between devices: none -> 52.8 us  [the longest x3 18 us: per_device(): lax.ppermute(piece, 'split', flipped(split, m))]
    all_to_all x5 -> x4, starting transfers between devices: 52.4 us -> 38.9 us  [the longest x2 18.5 us: per_device(): lax.all_to_all(out.reshape(2, dev, SLOTS, feats), 'dev', split_axis=1, co...]
    all_to_all x1, blocking collectives: 48.7 us -> 57.4 us  [per_device(): lax.all_to_all(send.reshape(dev, SLOTS, split * feats), 'dev', split_axis...]
    all_to_all x1, waiting for transfers between devices: 5.19 us -> 0.01 us  [per_device(): lax.all_to_all(grads, ('grp', 'split'), split_axis=0, concat_axis=0, tile...]
    unnamed x40 -> x76, local copies, waits for them, and re-layouts: 0.64 us -> 4.8 us
  transfers between devices with their start and end apart: 8 -> 18, of which waited for: 7 -> 9; matrix products, arithmetic and copies ran while one was open for 5% -> 9% of each run, Pallas kernels for 0% -> 0%
where the time goes in v2:
time: 343 us; the launch traced here: 342 us
  waiting for transfers between devices  119 us (35%)
  starting transfers between devices  100 us (29%)
  blocking collectives  57.4 us (17%)
  matrix products  23.2 us (7%)
  local copies, waits for them, and re-layouts  15.9 us (5%)
  between operations  14.8 us (4%)
  other arithmetic  11.6 us (3%)
    all_to_all x1, blocking collectives, per_device(): lax.all_to_all(send.reshape(dev, SLOTS, split * feats), 'dev', split_axis...  57.4 us
    ppermute x1, waiting for transfers between devices, per_device(): hidden_of.append(lax.ppermute(hidden, 'split', flipped(split, 2)))  32 us
    ppermute x3, waiting for transfers between devices, per_device(): lax.ppermute(piece, 'split', flipped(split, m))  19.5 us
    all_to_all x2, starting transfers between devices, per_device(): lax.all_to_all(out.reshape(2, dev, SLOTS, feats), 'dev', split_axis=1, co...  18.5 us
    ppermute x3, starting transfers between devices, per_device(): lax.ppermute(piece, 'split', flipped(split, m))  18 us
    ppermute x1, waiting for transfers between devices, per_device(): hidden_of.append(lax.ppermute(hidden_of[2], 'split', flipped(split, 1)))  16.8 us
    ppermute x3, starting transfers between devices, per_device(): lax.ppermute(tokens, 'grp', flipped(grp, m))  15.1 us
    all_to_all x1, waiting for transfers between devices, spread(): return lax.all_to_all(x, 'grp', split_axis=0, concat_axis=0, tiled=True)  14.1 us
  transfers between devices with their start and end apart: 18, of which 9 were waited for; matrix products, arithmetic and copies ran while one was open for 9% of the time, Pallas kernels for 0%

profile of v2, /device:TPU:1, one launch (start us, length us, event | category | flops | bytes accessed | tf_op | source)
XLA Modules:
  0.0 342.0 jit_solution(10504664601075059359)
XLA Ops:
  10.5 10.3 %all-to-all-start = ((bf16[4,144,512]{2,1,0:T(8,128)(2,1)}), bf16[4,144,512]{2,1,0:T(8,128)(2,1)S(1)}, u32[]{:S(2)}, u32[]{:S(2)}) async-start(bf16[4,144,512]{2,1,0:T(8,128)(2,1)} %broadcast_in_dim.115), calls=%async_computation | async-start | bytes 1179648 | tf_op jit(solution)/shard_map/all_to_all | solution.py:37
  22.3 14.1 %all-to-all-done = bf16[4,144,512]{2,1,0:T(8,128)(2,1)S(1)} async-done(((bf16[4,144,512]{2,1,0:T(8,128)(2,1)}), bf16[4,144,512]{2,1,0:T(8,128)(2,1)S(1)}, u32[]{:S(2)}, u32[]{:S(2)}) %all-to-all-start) | async-done | bytes 589856 | tf_op jit(solution)/shard_map/all_to_all | solution.py:37
  41.0 10.1 %all-to-all-start.1 = ((bf16[4,32,16,512]{3,2,0,1:T(8,128)(2,1)}), bf16[4,32,16,512]{3,2,0,1:T(8,128)(2,1)S(1)}, u32[]{:S(2)}, u32[]{:S(2)}) async-start(bf16[4,32,16,512]{3,2,0,1:T(8,128)(2,1)} %copy.67), calls=%async_computation.1 | async-start | bytes 4194304 | tf_op jit(solution)/shard_map/all_to_all | solution.py:80
  51.1 6.1 %collective-permute-start = (bf16[128,512]{1,0:T(8,128)(2,1)S(1)}, bf16[128,512]{1,0:T(8,128)(2,1)S(1)}, u32[]{:S(2)}, u32[]{:S(2)}) collective-permute-start(bf16[128,512]{1,0:T(8,128)(2,1)S(1)} %copy-done.23), channel_id=1, source_target_pairs={{0,128},{128,0},{256,384},{384,256},{1,129},{129,1},{257,385},{385... | collective-permute-start | bytes 393224 | tf_op jit(solution)/shard_map/ppermute | solution.py:54
  57.2 1.9 collective-permute-start.2
  59.1 7.2 %collective-permute-start.1 = (bf16[128,512]{1,0:T(8,128)(2,1)S(1)}, bf16[128,512]{1,0:T(8,128)(2,1)}, u32[]{:S(2)}, u32[]{:S(2)}) collective-permute-start(bf16[128,512]{1,0:T(8,128)(2,1)S(1)} %copy-done.23), channel_id=1, source_target_pairs={{0,256},{128,384},{256,0},{384,128},{1,257},{129,385},{257,1},{385... | collective-permute-start | bytes 393224 | tf_op jit(solution)/shard_map/ppermute | solution.py:54
  66.4 6.6 %collective-permute-done.2 = bf16[128,512]{1,0:T(8,128)(2,1)S(1)} collective-permute-done((bf16[128,512]{1,0:T(8,128)(2,1)S(1)}, bf16[128,512]{1,0:T(8,128)(2,1)S(1)}, u32[]{:S(2)}, u32[]{:S(2)}) %collective-permute-start.2) | collective-permute-done | bytes 131104 | tf_op jit(solution)/shard_map/ppermute | solution.py:54
  73.0 6.7 %collective-permute-done.1 = bf16[128,512]{1,0:T(8,128)(2,1)} collective-permute-done((bf16[128,512]{1,0:T(8,128)(2,1)S(1)}, bf16[128,512]{1,0:T(8,128)(2,1)}, u32[]{:S(2)}, u32[]{:S(2)}) %collective-permute-start.1) | collective-permute-done | bytes 131104 | tf_op jit(solution)/shard_map/ppermute | solution.py:54
  80.7 1.9 collective-permute-start.5
  82.6 13.9 %collective-permute-start.4 = (bf16[128,512]{1,0:T(8,128)(2,1)S(1)}, bf16[128,512]{1,0:T(8,128)(2,1)S(1)}, u32[]{:S(2)}, u32[]{:S(2)}) collective-permute-start(bf16[128,512]{1,0:T(8,128)(2,1)S(1)} %get-tuple-element.39), channel_id=1, source_target_pairs={{0,2},{1,3},{2,0},{3,1},{4,6},{5,7},{6,4},{7,5},{8,10},{9,11},{10,... | collective-permute-start | bytes 393224 | tf_op jit(solution)/shard_map/ppermute | solution.py:59
  96.6 2.2 collective-permute-start.3
  98.8 19.5 %collective-permute-done.4 = bf16[128,512]{1,0:T(8,128)(2,1)S(1)} collective-permute-done((bf16[128,512]{1,0:T(8,128)(2,1)S(1)}, bf16[128,512]{1,0:T(8,128)(2,1)S(1)}, u32[]{:S(2)}, u32[]{:S(2)}) %collective-permute-start.4) | collective-permute-done | bytes 131104 | tf_op jit(solution)/shard_map/ppermute | solution.py:59
  119.2 2.1 convolution_convert_fusion
  123.7 57.4 %all_to_all.30 = bf16[32,16,2048]{2,1,0:T(8,128)(2,1)S(1)} all-to-all(bf16[32,16,2048]{2,1,0:T(8,128)(2,1)S(1)} %bitcast.199), channel_id=1, replica_groups=mesh['grp'=4,'dev'=32,'split'=4] {'dev'}, dimensions={0} | all-to-all | bytes 4194304 | tf_op jit(solution)/shard_map/all_to_all | solution.py:84
  181.1 5.6 %fusion.111 = f32[4,2,192,512]{3,2,1,0:T(8,128)S(1)} fusion(bf16[4,2,192,2048]{3,2,1,0:T(8,128)(2,1)} %bitcast.236, bf16[512,2048,1,1]{1,0,3,2:T(8,128)(2,1)S(1)} %bitcast.206), kind=kOutput, calls=%fused_computation.218 | convolution fusion | flops 3221225472 | bytes 11534336 | tf_op jit(solution)/shard_map/dot_general | solution.py:88
  187.9 1.9 collective-permute-start.7
  189.9 3.8 %collective-permute-start.6 = (bf16[768,512]{1,0:T(8,128)(2,1)S(1)}, bf16[768,512]{1,0:T(8,128)(2,1)S(1)}, u32[]{:S(2)}, u32[]{:S(2)}) collective-permute-start(bf16[768,512]{1,0:T(8,128)(2,1)S(1)} %fusion), channel_id=1, source_target_pairs={{0,1},{1,0},{2,3},{3,2},{4,5},{5,4},{6,7},{7,6},{8,9},{9,8},{10,11... | collective-permute-start | bytes 2359304 | tf_op jit(solution)/shard_map/ppermute | solution.py:96
  194.4 32.0 %collective-permute-done.7 = bf16[768,512]{1,0:T(8,128)(2,1)S(1)} collective-permute-done((bf16[768,512]{1,0:T(8,128)(2,1)S(1)}, bf16[768,512]{1,0:T(8,128)(2,1)S(1)}, u32[]{:S(2)}, u32[]{:S(2)}) %collective-permute-start.7) | collective-permute-done | bytes 786464 | tf_op jit(solution)/shard_map/ppermute | solution.py:97
  229.0 9.7 %all-to-all-start.3 = ((bf16[2,32,16,512]{3,2,0,1:T(8,128)(2,1)}), bf16[2,32,16,512]{3,2,0,1:T(8,128)(2,1)S(1)}, u32[]{:S(2)}, u32[]{:S(2)}) async-start(bf16[2,32,16,512]{3,2,0,1:T(8,128)(2,1)} %pad_maximum_fusion.1), calls=%async_computation.3 | async-start | bytes 2097152 | tf_op jit(solution)/shard_map/all_to_all | solution.py:110
  238.7 1.9 collective-permute-start.8
  241.2 16.8 %collective-permute-done.8 = bf16[768,512]{1,0:T(8,128)(2,1)S(1)} collective-permute-done((bf16[768,512]{1,0:T(8,128)(2,1)S(1)}, bf16[768,512]{1,0:T(8,128)(2,1)S(1)}, u32[]{:S(2)}, u32[]{:S(2)}) %collective-permute-start.8) | collective-permute-done | bytes 786464 | tf_op jit(solution)/shard_map/ppermute | solution.py:99
  260.6 2.8 all-to-all-done.3
  263.3 8.9 %all-to-all-start.4 = ((bf16[2,32,16,512]{3,2,0,1:T(8,128)(2,1)}), bf16[2,32,16,512]{3,2,0,1:T(8,128)(2,1)}, u32[]{:S(2)}, u32[]{:S(2)}) async-start(bf16[2,32,16,512]{3,2,0,1:T(8,128)(2,1)} %pad_maximum_fusion.2), calls=%async_computation.4 | async-start | bytes 2097152 | tf_op jit(solution)/shard_map/all_to_all | solution.py:110
  274.6 2.1 copy.66
  276.7 3.0 fusion.36
  285.5 11.3 %all-to-all-done.4 = bf16[2,32,16,512]{3,2,0,1:T(8,128)(2,1)} async-done(((bf16[2,32,16,512]{3,2,0,1:T(8,128)(2,1)}), bf16[2,32,16,512]{3,2,0,1:T(8,128)(2,1)}, u32[]{:S(2)}, u32[]{:S(2)}) %all-to-all-start.4) | async-done | bytes 1048608 | tf_op jit(solution)/shard_map/all_to_all | solution.py:110
  300.2 8.3 %all-to-all-start.5 = ((f32[16,8,128]{2,1,0:T(8,128)}), f32[16,8,128]{2,1,0:T(8,128)S(1)}, u32[]{:S(2)}, u32[]{:S(2)}) async-start(f32[16,8,128]{2,1,0:T(8,128)} %bitcast.78), calls=%async_computation.5 | async-start | bytes 131072 | tf_op jit(solution)/shard_map/all_to_all | solution.py:126
  309.6 2.2 collective-permute-start.9
  311.9 7.4 %collective-permute-start.10 = (bf16[128,512]{1,0:T(8,128)(2,1)S(1)}, bf16[128,512]{1,0:T(8,128)(2,1)S(1)}, u32[]{:S(2)}, u32[]{:S(2)}) collective-permute-start(bf16[128,512]{1,0:T(8,128)(2,1)S(1)} %get-tuple-element.27), channel_id=1, source_target_pairs={{0,256},{128,384},{256,0},{384,128},{1,257},{129,385},{257,1},{385... | collective-permute-start | bytes 393224 | tf_op jit(solution)/shard_map/ppermute | solution.py:133
  319.3 2.3 collective-permute-start.11
  321.6 3.0 add_bitcast_fusion
  325.2 9.2 %collective-permute-done.11 = bf16[128,512]{1,0:T(8,128)(2,1)S(1)} collective-permute-done((bf16[128,512]{1,0:T(8,128)(2,1)S(1)}, bf16[128,512]{1,0:T(8,128)(2,1)S(1)}, u32[]{:S(2)}, u32[]{:S(2)}) %collective-permute-start.11) | collective-permute-done | bytes 131104 | tf_op jit(solution)/shard_map/ppermute | solution.py:133
  (147 shorter events, 35.1 us)
Async XLA Ops:
  7.2 186.6 %copy-start = (bf16[1,768,512]{2,1,0:T(8,128)(2,1)S(1)}, bf16[1,768,512]{2,1,0:T(8,128)(2,1)}, u32[]{:S(2)}) copy-start(bf16[1,768,512]{2,1,0:T(8,128)(2,1)} %param.13) | copy-start | bytes 2359300
  7.2 13.7 %copy-start.13 = (bf16[1,2048,192]{1,2,0:T(8,128)(2,1)S(1)}, bf16[1,2048,192]{1,2,0:T(8,128)(2,1)}, u32[]{:S(2)}) copy-start(bf16[1,2048,192]{1,2,0:T(8,128)(2,1)} %param.12) | copy-start | bytes 2359300
  7.2 13.7 %copy-start.14 = (bf16[1,2048,192]{1,2,0:T(8,128)(2,1)S(1)}, bf16[1,2048,192]{1,2,0:T(8,128)(2,1)}, u32[]{:S(2)}) copy-start(bf16[1,2048,192]{1,2,0:T(8,128)(2,1)} %param.11) | copy-start | bytes 2359300
  10.5 25.9 %all-to-all-start = ((bf16[4,144,512]{2,1,0:T(8,128)(2,1)}), bf16[4,144,512]{2,1,0:T(8,128)(2,1)S(1)}, u32[]{:S(2)}, u32[]{:S(2)}) async-start(bf16[4,144,512]{2,1,0:T(8,128)(2,1)} %broadcast_in_dim.115), calls=%async_computation | async-start | bytes 1179648 | tf_op jit(solution)/shard_map/all_to_all | solution.py:37
  20.9 160.2 %all-gather.3.cloned.1.call-start = ((), (), s32[]{:S(2)}) async-start(), calls=%async_computation.6 | async-start | bytes 7864320 | tf_op jit(solution)/shard_map/all_gather | solution.py:30
  22.3 14.8 %copy-start.36 = (f32[32]{0:T(128)}, f32[32]{0:T(128)S(1)}, u32[]{:S(2)}) copy-start(f32[32]{0:T(128)S(1)} %iota_add_fusion) | copy-start | bytes 388
  41.0 10.1 %copy-start.23 = (bf16[128,512]{1,0:T(8,128)(2,1)S(1)}, bf16[128,512]{1,0:T(8,128)(2,1)}, u32[]{:S(2)}) copy-start(bf16[128,512]{1,0:T(8,128)(2,1)} %param.7) | copy-start | bytes 393220
  41.0 80.3 %all-to-all-start.1 = ((bf16[4,32,16,512]{3,2,0,1:T(8,128)(2,1)}), bf16[4,32,16,512]{3,2,0,1:T(8,128)(2,1)S(1)}, u32[]{:S(2)}, u32[]{:S(2)}) async-start(bf16[4,32,16,512]{3,2,0,1:T(8,128)(2,1)} %copy.67), calls=%async_computation.1 | async-start | bytes 4194304 | tf_op jit(solution)/shard_map/all_to_all | solution.py:80
  51.1 15.2 %collective-permute-start = (bf16[128,512]{1,0:T(8,128)(2,1)S(1)}, bf16[128,512]{1,0:T(8,128)(2,1)S(1)}, u32[]{:S(2)}, u32[]{:S(2)}) collective-permute-start(bf16[128,512]{1,0:T(8,128)(2,1)S(1)} %copy-done.23), channel_id=1, source_target_pairs={{0,128},{128,0},{256,384},{384,256},{1,129},{129,1},{257,385},{385... | collective-permute-start | bytes 393224 | tf_op jit(solution)/shard_map/ppermute | solution.py:54
  57.2 15.8 %collective-permute-start.2 = (bf16[128,512]{1,0:T(8,128)(2,1)S(1)}, bf16[128,512]{1,0:T(8,128)(2,1)S(1)}, u32[]{:S(2)}, u32[]{:S(2)}) collective-permute-start(bf16[128,512]{1,0:T(8,128)(2,1)S(1)} %copy-done.23), channel_id=1, source_target_pairs={{0,384},{128,256},{256,128},{384,0},{1,385},{129,257},{257,129},{3... | collective-permute-start | bytes 393224 | tf_op jit(solution)/shard_map/ppermute | solution.py:54
  59.1 20.5 %collective-permute-start.1 = (bf16[128,512]{1,0:T(8,128)(2,1)S(1)}, bf16[128,512]{1,0:T(8,128)(2,1)}, u32[]{:S(2)}, u32[]{:S(2)}) collective-permute-start(bf16[128,512]{1,0:T(8,128)(2,1)S(1)} %copy-done.23), channel_id=1, source_target_pairs={{0,256},{128,384},{256,0},{384,128},{1,257},{129,385},{257,1},{385... | collective-permute-start | bytes 393224 | tf_op jit(solution)/shard_map/ppermute | solution.py:54
  80.7 18.1 %collective-permute-start.5 = (bf16[128,512]{1,0:T(8,128)(2,1)S(1)}, bf16[128,512]{1,0:T(8,128)(2,1)S(1)}, u32[]{:S(2)}, u32[]{:S(2)}) collective-permute-start(bf16[128,512]{1,0:T(8,128)(2,1)S(1)} %get-tuple-element.38), channel_id=1, source_target_pairs={{0,3},{1,2},{2,1},{3,0},{4,7},{5,6},{6,5},{7,4},{8,11},{9,10},{10,... | collective-permute-start | bytes 393224 | tf_op jit(solution)/shard_map/ppermute | solution.py:59
  82.6 35.6 %collective-permute-start.4 = (bf16[128,512]{1,0:T(8,128)(2,1)S(1)}, bf16[128,512]{1,0:T(8,128)(2,1)S(1)}, u32[]{:S(2)}, u32[]{:S(2)}) collective-permute-start(bf16[128,512]{1,0:T(8,128)(2,1)S(1)} %get-tuple-element.39), channel_id=1, source_target_pairs={{0,2},{1,3},{2,0},{3,1},{4,6},{5,7},{6,4},{7,5},{8,10},{9,11},{10,... | collective-permute-start | bytes 393224 | tf_op jit(solution)/shard_map/ppermute | solution.py:59
  96.6 21.7 %collective-permute-start.3 = (bf16[128,512]{1,0:T(8,128)(2,1)S(1)}, bf16[128,512]{1,0:T(8,128)(2,1)S(1)}, u32[]{:S(2)}, u32[]{:S(2)}) collective-permute-start(bf16[128,512]{1,0:T(8,128)(2,1)S(1)} %get-tuple-element.40), channel_id=1, source_target_pairs={{0,1},{1,0},{2,3},{3,2},{4,5},{5,4},{6,7},{7,6},{8,9},{9,8},{10,11... | collective-permute-start | bytes 393224 | tf_op jit(solution)/shard_map/ppermute | solution.py:59
  187.4 6.3 %copy-start.10 = (bf16[4,1,192,512]{3,2,1,0:T(8,128)(2,1)}, bf16[4,1,192,512]{3,2,1,0:T(8,128)(2,1)S(1)}, u32[]{:S(2)}) copy-start(bf16[4,1,192,512]{3,2,1,0:T(8,128)(2,1)S(1)} %get-tuple-element.21) | copy-start | bytes 2359300
  187.9 38.5 %collective-permute-start.7 = (bf16[768,512]{1,0:T(8,128)(2,1)S(1)}, bf16[768,512]{1,0:T(8,128)(2,1)S(1)}, u32[]{:S(2)}, u32[]{:S(2)}) collective-permute-start(bf16[768,512]{1,0:T(8,128)(2,1)S(1)} %fusion), channel_id=1, source_target_pairs={{0,2},{1,3},{2,0},{3,1},{4,6},{5,7},{6,4},{7,5},{8,10},{9,11},{10,... | collective-permute-start | bytes 2359304 | tf_op jit(solution)/shard_map/ppermute | solution.py:97
  189.9 36.5 %collective-permute-start.6 = (bf16[768,512]{1,0:T(8,128)(2,1)S(1)}, bf16[768,512]{1,0:T(8,128)(2,1)S(1)}, u32[]{:S(2)}, u32[]{:S(2)}) collective-permute-start(bf16[768,512]{1,0:T(8,128)(2,1)S(1)} %fusion), channel_id=1, source_target_pairs={{0,1},{1,0},{2,3},{3,2},{4,5},{5,4},{6,7},{7,6},{8,9},{9,8},{10,11... | collective-permute-start | bytes 2359304 | tf_op jit(solution)/shard_map/ppermute | solution.py:96
  226.4 14.2 %copy-start.15 = (bf16[768,512]{1,0:T(8,128)(2,1)}, bf16[768,512]{1,0:T(8,128)(2,1)S(1)}, u32[]{:S(2)}) copy-start(bf16[768,512]{1,0:T(8,128)(2,1)S(1)} %collective-permute-done.7) | copy-start | bytes 2359300
  229.0 34.3 %all-to-all-start.3 = ((bf16[2,32,16,512]{3,2,0,1:T(8,128)(2,1)}), bf16[2,32,16,512]{3,2,0,1:T(8,128)(2,1)S(1)}, u32[]{:S(2)}, u32[]{:S(2)}) async-start(bf16[2,32,16,512]{3,2,0,1:T(8,128)(2,1)} %pad_maximum_fusion.1), calls=%async_computation.3 | async-start | bytes 2097152 | tf_op jit(solution)/shard_map/all_to_all | solution.py:110
  238.7 19.3 %collective-permute-start.8 = (bf16[768,512]{1,0:T(8,128)(2,1)S(1)}, bf16[768,512]{1,0:T(8,128)(2,1)S(1)}, u32[]{:S(2)}, u32[]{:S(2)}) collective-permute-start(bf16[768,512]{1,0:T(8,128)(2,1)S(1)} %collective-permute-done.7), channel_id=1, source_target_pairs={{0,1},{1,0},{2,3},{3,2},{4,5},{5,4},{6,7},{7,6},{8,9},{9,8},{10,11... | collective-permute-start | bytes 2359304 | tf_op jit(solution)/shard_map/ppermute | solution.py:99
  260.6 11.6 %copy-start.7 = (f32[4,32,16,128]{3,2,1,0:T(8,128)S(1)}, f32[4,32,16,128]{3,2,1,0:T(8,128)}, u32[]{:S(2)}) copy-start(f32[4,32,16,128]{3,2,1,0:T(8,128)} %get-tuple-element.41) | copy-start | bytes 3145732
  263.3 8.9 %copy-start.8 = (bf16[2,32,16,512]{3,2,0,1:T(8,128)(2,1)}, bf16[2,32,16,512]{3,2,0,1:T(8,128)(2,1)S(1)}, u32[]{:S(2)}) copy-start(bf16[2,32,16,512]{3,2,0,1:T(8,128)(2,1)S(1)} %all-to-all-done.3) | copy-start | bytes 3145732
  263.3 33.4 %all-to-all-start.4 = ((bf16[2,32,16,512]{3,2,0,1:T(8,128)(2,1)}), bf16[2,32,16,512]{3,2,0,1:T(8,128)(2,1)}, u32[]{:S(2)}, u32[]{:S(2)}) async-start(bf16[2,32,16,512]{3,2,0,1:T(8,128)(2,1)} %pad_maximum_fusion.2), calls=%async_computation.4 | async-start | bytes 2097152 | tf_op jit(solution)/shard_map/all_to_all | solution.py:110
  273.2 3.5 %copy-start.2 = (bf16[4,32,16,512]{3,2,1,0:T(8,128)(2,1)S(1)}, bf16[4,32,16,512]{3,2,1,0:T(8,128)(2,1)}, u32[]{:S(2)}) copy-start(bf16[4,32,16,512]{3,2,1,0:T(8,128)(2,1)} %copy.68) | copy-start | bytes 6291460
  276.7 3.0 copy-start.18
  300.2 24.4 %all-to-all-start.5 = ((f32[16,8,128]{2,1,0:T(8,128)}), f32[16,8,128]{2,1,0:T(8,128)S(1)}, u32[]{:S(2)}, u32[]{:S(2)}) async-start(f32[16,8,128]{2,1,0:T(8,128)} %bitcast.78), calls=%async_computation.5 | async-start | bytes 131072 | tf_op jit(solution)/shard_map/all_to_all | solution.py:126
  308.5 13.0 %copy-start.5 = (f32[768,512]{1,0:T(8,128)S(1)}, f32[768,512]{1,0:T(8,128)}, u32[]{:S(2)}) copy-start(f32[768,512]{1,0:T(8,128)} %fusion.32) | copy-start | bytes 4718596
  308.8 12.7 %copy-start.3 = (f32[768,512]{1,0:T(8,128)S(1)}, f32[768,512]{1,0:T(8,128)}, u32[]{:S(2)}) copy-start(f32[768,512]{1,0:T(8,128)} %fusion.36) | copy-start | bytes 4718596
  308.8 12.7 %copy-start.4 = (f32[768,512]{1,0:T(8,128)S(1)}, f32[768,512]{1,0:T(8,128)}, u32[]{:S(2)}) copy-start(f32[768,512]{1,0:T(8,128)} %fusion.34) | copy-start | bytes 4718596
  309.6 15.6 %collective-permute-start.9 = (bf16[128,512]{1,0:T(8,128)(2,1)S(1)}, bf16[128,512]{1,0:T(8,128)(2,1)S(1)}, u32[]{:S(2)}, u32[]{:S(2)}) collective-permute-start(bf16[128,512]{1,0:T(8,128)(2,1)S(1)} %get-tuple-element.26), channel_id=1, source_target_pairs={{0,128},{128,0},{256,384},{384,256},{1,129},{129,1},{257,385},{385... | collective-permute-start | bytes 393224 | tf_op jit(solution)/shard_map/ppermute | solution.py:133
  311.9 13.3 %collective-permute-start.10 = (bf16[128,512]{1,0:T(8,128)(2,1)S(1)}, bf16[128,512]{1,0:T(8,128)(2,1)S(1)}, u32[]{:S(2)}, u32[]{:S(2)}) collective-permute-start(bf16[128,512]{1,0:T(8,128)(2,1)S(1)} %get-tuple-element.27), channel_id=1, source_target_pairs={{0,256},{128,384},{256,0},{384,128},{1,257},{129,385},{257,1},{385... | collective-permute-start | bytes 393224 | tf_op jit(solution)/shard_map/ppermute | solution.py:133
  319.3 15.1 %collective-permute-start.11 = (bf16[128,512]{1,0:T(8,128)(2,1)S(1)}, bf16[128,512]{1,0:T(8,128)(2,1)S(1)}, u32[]{:S(2)}, u32[]{:S(2)}) collective-permute-start(bf16[128,512]{1,0:T(8,128)(2,1)S(1)} %get-tuple-element.28), channel_id=1, source_target_pairs={{0,384},{128,256},{256,128},{384,0},{1,385},{129,257},{257,129},{3... | collective-permute-start | bytes 393224 | tf_op jit(solution)/shard_map/ppermute | solution.py:133
  (24 other events, 25.1 us)
Sparse Core Ops, SparseCore 0:
  24.4 143.2 all-gather.2

commit v3 on v2

--- a/solution.py
+++ b/solution.py
@@ -26,9 +26,6 @@
     hidden_part = w_gate.shape[2]
     f32, bf16 = jnp.float32, jnp.bfloat16
 
-    w_own = jnp.concatenate([w_gate[0].T, w_up[0].T], axis=0)
-    w_all = lax.all_gather(w_own, "split", axis=0, tiled=False)
-
     def flipped(size, bits):
         return [(i, i ^ bits) for i in range(size)]
 
@@ -40,25 +37,34 @@
         parts = [lax.dynamic_index_in_dim(x, split_me ^ j, 0, keepdims=True) for j in range(grp)]
         return jnp.concatenate(parts, axis=0)
 
+    pieces = jnp.stack(
+        [
+            lax.ppermute(
+                tokens,
+                ("grp", "split"),
+                [(g * split + f, (f ^ m) * split + g) for g in range(grp) for f in range(split)],
+            )
+            for m in range(split)
+        ]
+    )
+
     meta = jnp.concatenate([expert_ids.T.astype(bf16)] + bf16_pieces(gate_probs.T, 3), axis=0)
     meta = meta.reshape(-1, feats)
     meta_rows = meta.shape[0]
     meta = jnp.pad(meta, ((0, SLOTS - meta_rows), (0, 0)))
     near = spread(jnp.concatenate([upstream, meta], axis=0))
+    w_own = jnp.concatenate([w_gate[0].T, w_up[0].T], axis=0)
+    near, pieces, w_own = lax.optimization_barrier((near, pieces, w_own))
+
+    w_all = lax.all_gather(w_own, "split", axis=0, tiled=False)
+
     near_meta = relative(near[:, rows : rows + meta_rows].reshape(grp, 4, top, rows).astype(f32))
     near_ids = near_meta[:, 0]
     near_gates = near_meta[:, 1] + near_meta[:, 2] + near_meta[:, 3]
     near_upstream = relative(near[:, :rows])
 
-    near_tokens = jnp.stack(
-        [tokens] + [lax.ppermute(tokens, "grp", flipped(grp, m)) for m in range(1, grp)]
-    )
-    mine = []
-    for m in range(split):
-        piece = lax.dynamic_index_in_dim(near_tokens, grp_me ^ split_me ^ m, 0, keepdims=False)
-        mine.append(lax.ppermute(piece, "split", flipped(split, m)) if m > 0 else piece)
-    mine = relative(jnp.stack(mine))
-    mine = jnp.concatenate([mine[i] for i in range(split)], axis=1)
+    mine = jnp.stack([lax.dynamic_index_in_dim(pieces, grp_me ^ f, 0, keepdims=False) for f in range(split)])
+    mine = jnp.concatenate([mine[f] for f in range(split)], axis=1)
 
     expert = (grp_me * dev).astype(f32) + lax.broadcasted_iota(f32, (1, dev, 1), 1)
     equal = [near_ids[:, k][:, None, :] == expert for k in range(top)]
@@ -95,29 +101,32 @@
     hidden_of = [hidden]
     hidden_of.append(lax.ppermute(hidden, "split", flipped(split, 1)))
     hidden_of.append(lax.ppermute(hidden, "split", flipped(split, 2)))
-    hidden_of[1:] = lax.optimization_barrier(tuple(hidden_of[1:]))
-    hidden_of.append(lax.ppermute(hidden_of[2], "split", flipped(split, 1)))
 
     mixed, dots = [], []
-    for j in range(0, grp, 2):
-        two = slice(j, j + 2)
+    for part_of in (slice(0, 1), slice(1, 3), slice(3, 4)):
+        count = part_of.stop - part_of.start
+        if part_of.start == 1:
+            returned, *hidden_of[1:] = lax.optimization_barrier((returned, *hidden_of[1:]))
+            hidden_of.append(lax.ppermute(hidden_of[2], "split", flipped(split, 1)))
+        if part_of.start == 3:
+            returned, hidden_of[3] = lax.optimization_barrier((returned, hidden_of[3]))
         out = jnp.stack(
             [
                 lax.dot_general(h, w_down[0], (((0,), (0,)), ((), ())), preferred_element_type=f32).astype(bf16)
-                for h in hidden_of[two]
+                for h in hidden_of[part_of]
             ]
         )
         returned = lax.all_to_all(
-            out.reshape(2, dev, SLOTS, feats), "dev", split_axis=1, concat_axis=1, tiled=True
-        ).reshape(2, dev * SLOTS, feats)
+            out.reshape(count, dev, SLOTS, feats), "dev", split_axis=1, concat_axis=1, tiled=True
+        ).reshape(count, dev * SLOTS, feats)
         mixed.append(
             sum(
                 jnp.einsum("grt,grd->gtd", piece, returned, preferred_element_type=f32)
-                for piece in bf16_pieces(weight[two], 2)
+                for piece in bf16_pieces(weight[part_of], 2)
             ).astype(bf16)
         )
-        part = jnp.einsum("grd,gtd->grt", returned, near_upstream[two], preferred_element_type=f32)
-        dots.append(jnp.where(chosen[two], part.reshape(2, dev, SLOTS, rows), 0.0).sum(axis=2))
+        part = jnp.einsum("grd,gtd->grt", returned, near_upstream[part_of], preferred_element_type=f32)
+        dots.append(jnp.where(chosen[part_of], part.reshape(count, dev, SLOTS, rows), 0.0).sum(axis=2))
     mixed = jnp.concatenate(mixed, axis=0)
     dots = jnp.concatenate(dots, axis=0)
     grads = jnp.stack([jnp.sum(jnp.where(e, dots, 0.0), axis=1) for e in equal], axis=1)

time: 343 us -> 343 us (level)
  waiting for transfers between devices: 119 us -> 99 us
  matrix products: 23.2 us -> 39.1 us
  starting transfers between devices: 100 us -> 106 us
  blocking collectives: 57.4 us -> 53.5 us
    all_to_all x1, waiting for transfers between devices: 0.01 us -> 46.1 us  [per_device(): lax.all_to_all(scaled, 'dev', split_axis=1, concat_axis=1, tiled=True)]
    ppermute x1, waiting for transfers between devices: 32 us -> 0.28 us  [per_device(): hidden_of.append(lax.ppermute(hidden, 'split', flipped(split, 2)))]
    ppermute x6 -> x4, waiting for transfers between devices: 32.8 us -> 9.39 us  [per_device(): lax.ppermute(tokens, ('grp', 'split'), [(g * split + f, (f ^ m) * split +...]
    ppermute x1, waiting for transfers between devices: 0.01 us -> 17.8 us  [per_device(): hidden_of.append(lax.ppermute(hidden, 'split', flipped(split, 1)))]
    ppermute x1, waiting for transfers between devices: 16.8 us -> 0.81 us  [per_device(): hidden_of.append(lax.ppermute(hidden_of[2], 'split', flipped(split, 1)))]
    ppermute x6 -> x4, starting transfers between devices: 33.2 us -> 17.3 us  [per_device(): lax.ppermute(tokens, ('grp', 'split'), [(g * split + f, (f ^ m) * split +...]
    all_to_all x2 -> x3, starting transfers between devices: 18.5 us -> 34.1 us  [per_device(): lax.all_to_all(out.reshape(count, dev, SLOTS, feats), 'dev', split_axis=1...]
    all_to_all x1, waiting for transfers between devices: 14.1 us -> 0.01 us  [spread(): return lax.all_to_all(x, 'grp', split_axis=0, concat_axis=0, tiled=True)]
  transfers between devices with their start and end apart: 18 -> 17, of which waited for: 9 -> 10; matrix products, arithmetic and copies ran while one was open for 9% -> 13% of each run, Pallas kernels for 0% -> 0%
where the time goes in v3:
time: 343 us; the launch traced here: 342 us
  starting transfers between devices  106 us (31%)
  waiting for transfers between devices  99 us (29%)
  blocking collectives  53.5 us (16%)
  matrix products  39.1 us (11%)
  between operations  14.8 us (4%)
  local copies, waits for them, and re-layouts  14.7 us (4%)
  other arithmetic  14.5 us (4%)
    all_to_all x1, blocking collectives, per_device(): lax.all_to_all(send.reshape(dev, SLOTS, split * feats), 'dev', split_axis...  53.5 us
    all_to_all x1, waiting for transfers between devices, per_device(): lax.all_to_all(scaled, 'dev', split_axis=1, concat_axis=1, tiled=True)  46.1 us
    all_to_all x3, starting transfers between devices, per_device(): lax.all_to_all(out.reshape(count, dev, SLOTS, feats), 'dev', split_axis=1...  34.1 us
    ppermute x1, waiting for transfers between devices, per_device(): hidden_of.append(lax.ppermute(hidden, 'split', flipped(split, 1)))  17.8 us
    ppermute x4, starting transfers between devices, per_device(): lax.ppermute(tokens, ('grp', 'split'), [(g * split + f, (f ^ m) * split +...  17.3 us
    all_to_all x1, starting transfers between devices, per_device(): lax.all_to_all(scaled, 'dev', split_axis=1, concat_axis=1, tiled=True)  12.8 us
    all_to_all x3, waiting for transfers between devices, per_device(): lax.all_to_all(out.reshape(count, dev, SLOTS, feats), 'dev', split_axis=1...  12.7 us
    ppermute x3, starting transfers between devices, per_device(): piece = lax.ppermute(piece, 'grp', flipped(grp, m))  11.8 us
  transfers between devices with their start and end apart: 17, of which 10 were waited for; matrix products, arithmetic and copies ran while one was open for 13% of the time, Pallas kernels for 0%

profile of v3, /device:TPU:1, one launch (start us, length us, event | category | flops | bytes accessed | tf_op | source)
XLA Modules:
  0.0 341.9 jit_solution(11316190420063035138)
XLA Ops:
  10.6 10.3 %all-to-all-start = ((bf16[4,144,512]{2,1,0:T(8,128)(2,1)}), bf16[4,144,512]{2,1,0:T(8,128)(2,1)S(1)}, u32[]{:S(2)}, u32[]{:S(2)}) async-start(bf16[4,144,512]{2,1,0:T(8,128)(2,1)} %broadcast_in_dim.119), calls=%async_computation | async-start | bytes 1179648 | tf_op jit(solution)/shard_map/all_to_all | solution.py:34
  22.8 1.9 collective-permute-start.1
  24.7 11.6 %collective-permute-start.2 = (bf16[128,512]{1,0:T(8,128)(2,1)}, bf16[128,512]{1,0:T(8,128)(2,1)S(1)}, u32[]{:S(2)}, u32[]{:S(2)}) collective-permute-start(bf16[128,512]{1,0:T(8,128)(2,1)} %param.7), channel_id=1, source_target_pairs={{0,256},{1,384},{2,0},{3,128},{128,257},{129,385},{130,1},{131,129... | collective-permute-start | bytes 393224 | tf_op jit(solution)/shard_map/ppermute | solution.py:42
  39.6 3.4 collective-permute-done.1
  43.0 6.0 %collective-permute-done.3 = bf16[128,512]{1,0:T(8,128)(2,1)S(1)} collective-permute-done((bf16[128,512]{1,0:T(8,128)(2,1)}, bf16[128,512]{1,0:T(8,128)(2,1)S(1)}, u32[]{:S(2)}, u32[]{:S(2)}) %collective-permute-start.3) | collective-permute-done | bytes 131104 | tf_op jit(solution)/shard_map/ppermute | solution.py:42
  56.4 12.8 %all-to-all-start.1 = ((bf16[4,32,16,512]{3,2,0,1:T(8,128)(2,1)}), bf16[4,32,16,512]{3,2,0,1:T(8,128)(2,1)S(1)}, u32[]{:S(2)}, u32[]{:S(2)}) async-start(bf16[4,32,16,512]{3,2,0,1:T(8,128)(2,1)} %copy.94), calls=%async_computation.1 | async-start | bytes 4194304 | tf_op jit(solution)/shard_map/all_to_all | solution.py:86
  70.1 2.1 convolution_convert_fusion
  72.2 46.1 %all-to-all-done.1 = bf16[4,32,16,512]{3,2,0,1:T(8,128)(2,1)S(1)} async-done(((bf16[4,32,16,512]{3,2,0,1:T(8,128)(2,1)}), bf16[4,32,16,512]{3,2,0,1:T(8,128)(2,1)S(1)}, u32[]{:S(2)}, u32[]{:S(2)}) %all-to-all-start.1) | async-done | bytes 2097184 | tf_op jit(solution)/shard_map/all_to_all | solution.py:86
  120.6 53.5 %all_to_all.35 = bf16[32,16,2048]{2,1,0:T(8,128)(2,1)S(1)} all-to-all(bf16[32,16,2048]{2,1,0:T(8,128)(2,1)S(1)} %bitcast.247), channel_id=1, replica_groups=mesh['grp'=4,'dev'=32,'split'=4] {'dev'}, dimensions={0} | all-to-all | bytes 4194304 | tf_op jit(solution)/shard_map/all_to_all | solution.py:90
  174.1 3.5 %all-gather.3.cloned.1.call-done = bf16[1536,2048]{1,0:T(8,128)(2,1)} async-done(((bf16[384,2048]{1,0:T(8,128)(2,1)}), bf16[1536,2048]{1,0:T(8,128)(2,1)}) %all-gather.3.cloned.1.call-update) | async-done | bytes 6291472 | tf_op jit(solution)/shard_map/all_gather | solution.py:59
  177.6 5.6 %fusion.127 = f32[4,2,192,512]{3,2,1,0:T(8,128)S(1)} fusion(bf16[4,2,192,2048]{3,2,1,0:T(8,128)(2,1)} %bitcast.285, bf16[512,2048,1,1]{1,0,3,2:T(8,128)(2,1)S(1)} %bitcast.256), kind=kOutput, calls=%fused_computation.227 | convolution fusion | flops 3221225472 | bytes 11534336 | tf_op jit(solution)/shard_map/dot_general | solution.py:94
  184.4 3.3 collective-permute-start.4
  187.8 3.7 %collective-permute-start.5 = (bf16[768,512]{1,0:T(8,128)(2,1)S(1)}, bf16[768,512]{1,0:T(8,128)(2,1)}, u32[]{:S(2)}, u32[]{:S(2)}) collective-permute-start(bf16[768,512]{1,0:T(8,128)(2,1)S(1)} %fusion), channel_id=1, source_target_pairs={{0,2},{1,3},{2,0},{3,1},{4,6},{5,7},{6,4},{7,5},{8,10},{9,11},{10,... | collective-permute-start | bytes 2359304 | tf_op jit(solution)/shard_map/ppermute | solution.py:103
  192.9 8.6 %all-to-all-start.3 = ((bf16[1,32,16,512]{3,2,0,1:T(8,128)(2,1)}), bf16[1,32,16,512]{3,2,0,1:T(8,128)(2,1)S(1)}, u32[]{:S(2)}, u32[]{:S(2)}) async-start(bf16[1,32,16,512]{3,2,0,1:T(8,128)(2,1)} %bitcast.46), calls=%async_computation.3 | async-start | bytes 1048576 | tf_op jit(solution)/shard_map/all_to_all | solution.py:119
  201.5 17.8 %collective-permute-done.4 = bf16[768,512]{1,0:T(8,128)(2,1)S(1)} collective-permute-done((bf16[768,512]{1,0:T(8,128)(2,1)S(1)}, bf16[768,512]{1,0:T(8,128)(2,1)S(1)}, u32[]{:S(2)}, u32[]{:S(2)}) %collective-permute-start.4) | collective-permute-done | bytes 786464 | tf_op jit(solution)/shard_map/ppermute | solution.py:102
  223.1 16.4 %all-to-all-start.4 = ((bf16[2,32,16,512]{3,2,0,1:T(8,128)(2,1)}), bf16[2,32,16,512]{3,2,0,1:T(8,128)(2,1)}, u32[]{:S(2)}, u32[]{:S(2)}) async-start(bf16[2,32,16,512]{3,2,0,1:T(8,128)(2,1)} %pad_maximum_fusion.1), calls=%async_computation.4 | async-start | bytes 2097152 | tf_op jit(solution)/shard_map/all_to_all | solution.py:119
  241.8 2.0 copy.99
  243.9 3.0 fusion.43
  246.8 2.1 collective-permute-start.6
  250.7 2.9 fusion.39
  253.5 2.1 convolution_bitcast_fusion.4
  257.5 6.6 %all-to-all-done.4 = bf16[2,32,16,512]{3,2,0,1:T(8,128)(2,1)} async-done(((bf16[2,32,16,512]{3,2,0,1:T(8,128)(2,1)}), bf16[2,32,16,512]{3,2,0,1:T(8,128)(2,1)}, u32[]{:S(2)}, u32[]{:S(2)}) %all-to-all-start.4) | async-done | bytes 1048608 | tf_op jit(solution)/shard_map/all_to_all | solution.py:119
  266.2 2.6 convolution_convert_fusion.1
  268.8 9.1 %all-to-all-start.5 = ((bf16[1,32,16,512]{3,2,0,1:T(8,128)(2,1)}), bf16[1,32,16,512]{3,2,0,1:T(8,128)(2,1)}, u32[]{:S(2)}, u32[]{:S(2)}) async-start(bf16[1,32,16,512]{3,2,0,1:T(8,128)(2,1)} %bitcast.261), calls=%async_computation.5 | async-start | bytes 1048576 | tf_op jit(solution)/shard_map/all_to_all | solution.py:119
  278.0 2.1 fusion.13
  283.7 6.1 %all-to-all-done.5 = bf16[1,32,16,512]{3,2,0,1:T(8,128)(2,1)} async-done(((bf16[1,32,16,512]{3,2,0,1:T(8,128)(2,1)}), bf16[1,32,16,512]{3,2,0,1:T(8,128)(2,1)}, u32[]{:S(2)}, u32[]{:S(2)}) %all-to-all-start.5) | async-done | bytes 524320 | tf_op jit(solution)/shard_map/all_to_all | solution.py:119
  294.5 10.8 %all-to-all-start.6 = ((f32[16,8,128]{2,1,0:T(8,128)}), f32[16,8,128]{2,1,0:T(8,128)}, u32[]{:S(2)}, u32[]{:S(2)}) async-start(f32[16,8,128]{2,1,0:T(8,128)} %bitcast.264), calls=%async_computation.6 | async-start | bytes 131072 | tf_op jit(solution)/shard_map/all_to_all | solution.py:135
  308.7 2.1 collective-permute-start.7
  310.8 7.4 %collective-permute-start.8 = (bf16[128,512]{1,0:T(8,128)(2,1)S(1)}, bf16[128,512]{1,0:T(8,128)(2,1)S(1)}, u32[]{:S(2)}, u32[]{:S(2)}) collective-permute-start(bf16[128,512]{1,0:T(8,128)(2,1)S(1)} %get-tuple-element.32), channel_id=1, source_target_pairs={{0,256},{128,384},{256,0},{384,128},{1,257},{129,385},{257,1},{385... | collective-permute-start | bytes 393224 | tf_op jit(solution)/shard_map/ppermute | solution.py:142
  318.2 2.3 collective-permute-start.9
  320.5 3.1 add_bitcast_fusion
  325.1 8.4 %collective-permute-done.9 = bf16[128,512]{1,0:T(8,128)(2,1)} collective-permute-done((bf16[128,512]{1,0:T(8,128)(2,1)S(1)}, bf16[128,512]{1,0:T(8,128)(2,1)}, u32[]{:S(2)}, u32[]{:S(2)}) %collective-permute-start.9) | collective-permute-done | bytes 131104 | tf_op jit(solution)/shard_map/ppermute | solution.py:142
  (139 shorter events, 47.9 us)
Async XLA Ops:
  7.2 184.3 %copy-start = (bf16[1,768,512]{2,1,0:T(8,128)(2,1)S(1)}, bf16[1,768,512]{2,1,0:T(8,128)(2,1)}, u32[]{:S(2)}) copy-start(bf16[1,768,512]{2,1,0:T(8,128)(2,1)} %param.13) | copy-start | bytes 2359300
  7.2 31.1 %copy-start.14 = (bf16[1,2048,192]{1,2,0:T(8,128)(2,1)S(1)}, bf16[1,2048,192]{1,2,0:T(8,128)(2,1)}, u32[]{:S(2)}) copy-start(bf16[1,2048,192]{1,2,0:T(8,128)(2,1)} %param.11) | copy-start | bytes 2359300
  7.2 31.1 %copy-start.13 = (bf16[1,2048,192]{1,2,0:T(8,128)(2,1)S(1)}, bf16[1,2048,192]{1,2,0:T(8,128)(2,1)}, u32[]{:S(2)}) copy-start(bf16[1,2048,192]{1,2,0:T(8,128)(2,1)} %param.12) | copy-start | bytes 2359300
  10.6 40.2 %all-to-all-start = ((bf16[4,144,512]{2,1,0:T(8,128)(2,1)}), bf16[4,144,512]{2,1,0:T(8,128)(2,1)S(1)}, u32[]{:S(2)}, u32[]{:S(2)}) async-start(bf16[4,144,512]{2,1,0:T(8,128)(2,1)} %broadcast_in_dim.119), calls=%async_computation | async-start | bytes 1179648 | tf_op jit(solution)/shard_map/all_to_all | solution.py:34
  20.9 156.7 %all-gather.3.cloned.1.call-start = ((), (), s32[]{:S(2)}) async-start(), calls=%async_computation.7 | async-start | bytes 7864320 | tf_op jit(solution)/shard_map/all_gather | solution.py:59
  20.9 18.7 %collective-permute-start = (bf16[128,512]{1,0:T(8,128)(2,1)}, bf16[128,512]{1,0:T(8,128)(2,1)S(1)}, u32[]{:S(2)}, u32[]{:S(2)}) collective-permute-start(bf16[128,512]{1,0:T(8,128)(2,1)} %param.7), channel_id=1, source_target_pairs={{0,0},{1,128},{2,256},{3,384},{128,1},{129,129},{130,257},{131,385... | collective-permute-start | bytes 393224 | tf_op jit(solution)/shard_map/ppermute | solution.py:42
  22.8 20.2 %collective-permute-start.1 = (bf16[128,512]{1,0:T(8,128)(2,1)}, bf16[128,512]{1,0:T(8,128)(2,1)S(1)}, u32[]{:S(2)}, u32[]{:S(2)}) collective-permute-start(bf16[128,512]{1,0:T(8,128)(2,1)} %param.7), channel_id=1, source_target_pairs={{0,128},{1,0},{2,384},{3,256},{128,129},{129,1},{130,385},{131,257... | collective-permute-start | bytes 393224 | tf_op jit(solution)/shard_map/ppermute | solution.py:42
  24.7 18.3 %collective-permute-start.2 = (bf16[128,512]{1,0:T(8,128)(2,1)}, bf16[128,512]{1,0:T(8,128)(2,1)S(1)}, u32[]{:S(2)}, u32[]{:S(2)}) collective-permute-start(bf16[128,512]{1,0:T(8,128)(2,1)} %param.7), channel_id=1, source_target_pairs={{0,256},{1,384},{2,0},{3,128},{128,257},{129,385},{130,1},{131,129... | collective-permute-start | bytes 393224 | tf_op jit(solution)/shard_map/ppermute | solution.py:42
  36.3 12.7 %collective-permute-start.3 = (bf16[128,512]{1,0:T(8,128)(2,1)}, bf16[128,512]{1,0:T(8,128)(2,1)S(1)}, u32[]{:S(2)}, u32[]{:S(2)}) collective-permute-start(bf16[128,512]{1,0:T(8,128)(2,1)} %param.7), channel_id=1, source_target_pairs={{0,384},{1,256},{2,128},{3,0},{128,385},{129,257},{130,129},{131,1... | collective-permute-start | bytes 393224 | tf_op jit(solution)/shard_map/ppermute | solution.py:42
  39.6 12.3 %copy-start.32 = (f32[32]{0:T(128)}, f32[32]{0:T(128)S(1)}, u32[]{:S(2)}) copy-start(f32[32]{0:T(128)S(1)} %iota_add_fusion) | copy-start | bytes 388
  43.0 6.0 %copy-start.25 = (bf16[128,512]{1,0:T(8,128)(2,1)}, bf16[128,512]{1,0:T(8,128)(2,1)S(1)}, u32[]{:S(2)}) copy-start(bf16[128,512]{1,0:T(8,128)(2,1)S(1)} %collective-permute-done.1) | copy-start | bytes 393220
  43.0 6.0 %copy-start.26 = (bf16[128,512]{1,0:T(8,128)(2,1)}, bf16[128,512]{1,0:T(8,128)(2,1)S(1)}, u32[]{:S(2)}) copy-start(bf16[128,512]{1,0:T(8,128)(2,1)S(1)} %collective-permute-done.2) | copy-start | bytes 393220
  56.4 61.9 %all-to-all-start.1 = ((bf16[4,32,16,512]{3,2,0,1:T(8,128)(2,1)}), bf16[4,32,16,512]{3,2,0,1:T(8,128)(2,1)S(1)}, u32[]{:S(2)}, u32[]{:S(2)}) async-start(bf16[4,32,16,512]{3,2,0,1:T(8,128)(2,1)} %copy.94), calls=%async_computation.1 | async-start | bytes 4194304 | tf_op jit(solution)/shard_map/all_to_all | solution.py:86
  183.9 7.6 %copy-start.8 = (bf16[4,1,192,512]{3,2,1,0:T(8,128)(2,1)}, bf16[4,1,192,512]{3,2,1,0:T(8,128)(2,1)S(1)}, u32[]{:S(2)}) copy-start(bf16[4,1,192,512]{3,2,1,0:T(8,128)(2,1)S(1)} %get-tuple-element.27) | copy-start | bytes 2359300
  184.4 34.9 %collective-permute-start.4 = (bf16[768,512]{1,0:T(8,128)(2,1)S(1)}, bf16[768,512]{1,0:T(8,128)(2,1)S(1)}, u32[]{:S(2)}, u32[]{:S(2)}) collective-permute-start(bf16[768,512]{1,0:T(8,128)(2,1)S(1)} %fusion), channel_id=1, source_target_pairs={{0,1},{1,0},{2,3},{3,2},{4,5},{5,4},{6,7},{7,6},{8,9},{9,8},{10,11... | collective-permute-start | bytes 2359304 | tf_op jit(solution)/shard_map/ppermute | solution.py:102
  187.8 31.8 %collective-permute-start.5 = (bf16[768,512]{1,0:T(8,128)(2,1)S(1)}, bf16[768,512]{1,0:T(8,128)(2,1)}, u32[]{:S(2)}, u32[]{:S(2)}) collective-permute-start(bf16[768,512]{1,0:T(8,128)(2,1)S(1)} %fusion), channel_id=1, source_target_pairs={{0,2},{1,3},{2,0},{3,1},{4,6},{5,7},{6,4},{7,5},{8,10},{9,11},{10,... | collective-permute-start | bytes 2359304 | tf_op jit(solution)/shard_map/ppermute | solution.py:103
  192.9 30.2 %all-to-all-start.3 = ((bf16[1,32,16,512]{3,2,0,1:T(8,128)(2,1)}), bf16[1,32,16,512]{3,2,0,1:T(8,128)(2,1)S(1)}, u32[]{:S(2)}, u32[]{:S(2)}) async-start(bf16[1,32,16,512]{3,2,0,1:T(8,128)(2,1)} %bitcast.46), calls=%async_computation.3 | async-start | bytes 1048576 | tf_op jit(solution)/shard_map/all_to_all | solution.py:119
  223.1 41.0 %all-to-all-start.4 = ((bf16[2,32,16,512]{3,2,0,1:T(8,128)(2,1)}), bf16[2,32,16,512]{3,2,0,1:T(8,128)(2,1)}, u32[]{:S(2)}, u32[]{:S(2)}) async-start(bf16[2,32,16,512]{3,2,0,1:T(8,128)(2,1)} %pad_maximum_fusion.1), calls=%async_computation.4 | async-start | bytes 2097152 | tf_op jit(solution)/shard_map/all_to_all | solution.py:119
  243.9 5.1 %copy-start.16 = (bf16[768,512]{1,0:T(8,128)(2,1)S(1)}, bf16[768,512]{1,0:T(8,128)(2,1)}, u32[]{:S(2)}) copy-start(bf16[768,512]{1,0:T(8,128)(2,1)} %copy-done.15) | copy-start | bytes 2359300
  246.8 19.4 %collective-permute-start.6 = (bf16[768,512]{1,0:T(8,128)(2,1)}, bf16[768,512]{1,0:T(8,128)(2,1)}, u32[]{:S(2)}, u32[]{:S(2)}) collective-permute-start(bf16[768,512]{1,0:T(8,128)(2,1)} %collective-permute-done.5), channel_id=1, source_target_pairs={{0,1},{1,0},{2,3},{3,2},{4,5},{5,4},{6,7},{7,6},{8,9},{9,8},{10,11... | collective-permute-start | bytes 2359304 | tf_op jit(solution)/shard_map/ppermute | solution.py:110
  266.2 11.8 %copy-start.3 = (f32[4,32,16,128]{3,1,2,0:T(8,128)S(1)}, f32[4,32,16,128]{3,1,2,0:T(8,128)}, u32[]{:S(2)}) copy-start(f32[4,32,16,128]{3,1,2,0:T(8,128)} %get-tuple-element.41) | copy-start | bytes 3145732
  268.8 11.3 %copy-start.18 = (bf16[1,128,512]{2,1,0:T(8,128)(2,1)S(1)}, bf16[1,128,512]{2,1,0:T(8,128)(2,1)}, u32[]{:S(2)}) copy-start(bf16[1,128,512]{2,1,0:T(8,128)(2,1)} %copy-done.17) | copy-start | bytes 393220
  268.8 20.9 %all-to-all-start.5 = ((bf16[1,32,16,512]{3,2,0,1:T(8,128)(2,1)}), bf16[1,32,16,512]{3,2,0,1:T(8,128)(2,1)}, u32[]{:S(2)}, u32[]{:S(2)}) async-start(bf16[1,32,16,512]{3,2,0,1:T(8,128)(2,1)} %bitcast.261), calls=%async_computation.5 | async-start | bytes 1048576 | tf_op jit(solution)/shard_map/all_to_all | solution.py:119
  282.6 7.2 %copy-start.22 = (bf16[1,128,512]{2,1,0:T(8,128)(2,1)S(1)}, bf16[1,128,512]{2,1,0:T(8,128)(2,1)}, u32[]{:S(2)}) copy-start(bf16[1,128,512]{2,1,0:T(8,128)(2,1)} %copy-done.21) | copy-start | bytes 393220
  289.8 30.7 %copy-start.6 = (f32[768,512]{1,0:T(8,128)S(1)}, f32[768,512]{1,0:T(8,128)}, u32[]{:S(2)}) copy-start(f32[768,512]{1,0:T(8,128)} %fusion.39) | copy-start | bytes 4718596
  291.4 17.1 %copy-start.20 = (bf16[1,128,512]{2,1,0:T(8,128)(2,1)S(1)}, bf16[1,128,512]{2,1,0:T(8,128)(2,1)}, u32[]{:S(2)}) copy-start(bf16[1,128,512]{2,1,0:T(8,128)(2,1)} %fusion.13) | copy-start | bytes 393220
  294.5 29.1 %all-to-all-start.6 = ((f32[16,8,128]{2,1,0:T(8,128)}), f32[16,8,128]{2,1,0:T(8,128)}, u32[]{:S(2)}, u32[]{:S(2)}) async-start(f32[16,8,128]{2,1,0:T(8,128)} %bitcast.264), calls=%async_computation.6 | async-start | bytes 131072 | tf_op jit(solution)/shard_map/all_to_all | solution.py:135
  305.3 15.2 %copy-start.5 = (f32[768,512]{1,0:T(8,128)S(1)}, f32[768,512]{1,0:T(8,128)}, u32[]{:S(2)}) copy-start(f32[768,512]{1,0:T(8,128)} %fusion.41) | copy-start | bytes 4718596
  306.9 13.6 %copy-start.4 = (f32[768,512]{1,0:T(8,128)S(1)}, f32[768,512]{1,0:T(8,128)}, u32[]{:S(2)}) copy-start(f32[768,512]{1,0:T(8,128)} %fusion.43) | copy-start | bytes 4718596
  308.7 16.4 %collective-permute-start.7 = (bf16[128,512]{1,0:T(8,128)(2,1)S(1)}, bf16[128,512]{1,0:T(8,128)(2,1)S(1)}, u32[]{:S(2)}, u32[]{:S(2)}) collective-permute-start(bf16[128,512]{1,0:T(8,128)(2,1)S(1)} %get-tuple-element.30), channel_id=1, source_target_pairs={{0,128},{128,0},{256,384},{384,256},{1,129},{129,1},{257,385},{385... | collective-permute-start | bytes 393224 | tf_op jit(solution)/shard_map/ppermute | solution.py:142
  310.8 14.3 %collective-permute-start.8 = (bf16[128,512]{1,0:T(8,128)(2,1)S(1)}, bf16[128,512]{1,0:T(8,128)(2,1)S(1)}, u32[]{:S(2)}, u32[]{:S(2)}) collective-permute-start(bf16[128,512]{1,0:T(8,128)(2,1)S(1)} %get-tuple-element.32), channel_id=1, source_target_pairs={{0,256},{128,384},{256,0},{384,128},{1,257},{129,385},{257,1},{385... | collective-permute-start | bytes 393224 | tf_op jit(solution)/shard_map/ppermute | solution.py:142
  318.2 15.3 %collective-permute-start.9 = (bf16[128,512]{1,0:T(8,128)(2,1)S(1)}, bf16[128,512]{1,0:T(8,128)(2,1)}, u32[]{:S(2)}, u32[]{:S(2)}) collective-permute-start(bf16[128,512]{1,0:T(8,128)(2,1)S(1)} %get-tuple-element.31), channel_id=1, source_target_pairs={{0,384},{128,256},{256,128},{384,0},{1,385},{129,257},{257,129},{3... | collective-permute-start | bytes 393224 | tf_op jit(solution)/shard_map/ppermute | solution.py:142
  (19 other events, 35.4 us)
Sparse Core Ops, SparseCore 0:
  51.1 126.4 all-gather.2

commit v4 on v3

--- a/solution.py
+++ b/solution.py
@@ -13,6 +13,10 @@
         pieces.append(top.astype(jnp.bfloat16))
         x = x - top
     return pieces
+
+
+def after(x, earlier):
+    return x + (earlier[(0,) * earlier.ndim].astype(jnp.float32) * 0.0).astype(x.dtype)
 
 
 def per_device(tokens, upstream, expert_ids, gate_probs, w_gate, w_up, w_down):
@@ -49,19 +53,29 @@
     )
 
     meta = jnp.concatenate([expert_ids.T.astype(bf16)] + bf16_pieces(gate_probs.T, 3), axis=0)
-    meta = meta.reshape(-1, feats)
-    meta_rows = meta.shape[0]
-    meta = jnp.pad(meta, ((0, SLOTS - meta_rows), (0, 0)))
-    near = spread(jnp.concatenate([upstream, meta], axis=0))
+    near = spread(meta)
     w_own = jnp.concatenate([w_gate[0].T, w_up[0].T], axis=0)
-    near, pieces, w_own = lax.optimization_barrier((near, pieces, w_own))
+    w_own = after(after(w_own, near), pieces)
 
-    w_all = lax.all_gather(w_own, "split", axis=0, tiled=False)
+    w_of = [w_own]
+    w_of.append(lax.ppermute(w_own, "split", flipped(split, 1)))
+    w_of.append(lax.ppermute(w_own, "split", flipped(split, 2)))
+    w_of[2] = after(w_of[2], w_of[1])
+    w_of.append(lax.ppermute(w_of[2], "split", flipped(split, 1)))
 
-    near_meta = relative(near[:, rows : rows + meta_rows].reshape(grp, 4, top, rows).astype(f32))
+    near_upstream = jnp.stack(
+        [upstream] + [lax.ppermute(upstream, "grp", flipped(grp, m)) for m in range(1, grp)]
+    )
+    near_upstream = jnp.stack(
+        [
+            lax.dynamic_index_in_dim(near_upstream, grp_me ^ split_me ^ j, 0, keepdims=False)
+            for j in range(grp)
+        ]
+    )
+
+    near_meta = relative(near.astype(f32).reshape(grp, 4, top, rows))
     near_ids = near_meta[:, 0]
     near_gates = near_meta[:, 1] + near_meta[:, 2] + near_meta[:, 3]
-    near_upstream = relative(near[:, :rows])
 
     mine = jnp.stack([lax.dynamic_index_in_dim(pieces, grp_me ^ f, 0, keepdims=False) for f in range(split)])
     mine = jnp.concatenate([mine[f] for f in range(split)], axis=1)
@@ -81,41 +95,34 @@
     weight = jnp.where(chosen, gate_of[:, :, None, :], 0.0).reshape(grp, dev * SLOTS, rows)
     gate_row = jnp.sum(weight, axis=2, keepdims=True)
 
-    scaled = jnp.einsum("grt,gtd->grd", pick, near_upstream, preferred_element_type=f32)
-    scaled = (scaled * gate_row).astype(bf16).reshape(grp, dev, SLOTS, feats)
-    scaled_rows = lax.all_to_all(scaled, "dev", split_axis=1, concat_axis=1, tiled=True)
-    scaled_rows = scaled_rows.reshape(grp, dev * SLOTS, feats)
     send = jnp.dot(pick[0], mine, preferred_element_type=f32).astype(bf16)
-    send, scaled_rows = lax.optimization_barrier((send, scaled_rows))
     arrived = lax.all_to_all(
         send.reshape(dev, SLOTS, split * feats), "dev", split_axis=0, concat_axis=0, tiled=True
     ).reshape(dev * SLOTS, split * feats)
+    scaled = jnp.einsum("grt,gtd->grd", pick, near_upstream, preferred_element_type=f32)
+    scaled = (scaled * after(gate_row, arrived)).astype(bf16).reshape(grp, dev, SLOTS, feats)
+    scaled_rows = lax.all_to_all(scaled, "dev", split_axis=1, concat_axis=1, tiled=True)
+    scaled_rows = scaled_rows.reshape(grp, dev * SLOTS, feats)
 
-    pre = lax.dot_general(
-        w_all.reshape(split * 2 * hidden_part, split * feats),
-        arrived,
-        (((1,), (1,)), ((), ())),
-        preferred_element_type=f32,
-    ).reshape(split, 2, hidden_part, dev * SLOTS)
-    hidden = (jax.nn.silu(pre[:, 0]) * pre[:, 1]).astype(bf16).reshape(split * hidden_part, dev * SLOTS)
+    hidden = []
+    for w in w_of:
+        pre = lax.dot_general(w, arrived, (((1,), (1,)), ((), ())), preferred_element_type=f32)
+        hidden.append((jax.nn.silu(pre[:hidden_part]) * pre[hidden_part:]).astype(bf16))
+    hidden = relative(jnp.stack(hidden)).reshape(split * hidden_part, dev * SLOTS)
     hidden_of = [hidden]
     hidden_of.append(lax.ppermute(hidden, "split", flipped(split, 1)))
     hidden_of.append(lax.ppermute(hidden, "split", flipped(split, 2)))
 
-    mixed, dots = [], []
+    mixed, dots, returned = [], [], scaled_rows
     for part_of in (slice(0, 1), slice(1, 3), slice(3, 4)):
         count = part_of.stop - part_of.start
         if part_of.start == 1:
-            returned, *hidden_of[1:] = lax.optimization_barrier((returned, *hidden_of[1:]))
             hidden_of.append(lax.ppermute(hidden_of[2], "split", flipped(split, 1)))
-        if part_of.start == 3:
-            returned, hidden_of[3] = lax.optimization_barrier((returned, hidden_of[3]))
-        out = jnp.stack(
-            [
-                lax.dot_general(h, w_down[0], (((0,), (0,)), ((), ())), preferred_element_type=f32).astype(bf16)
-                for h in hidden_of[part_of]
-            ]
-        )
+        out = [
+            lax.dot_general(h, w_down[0], (((0,), (0,)), ((), ())), preferred_element_type=f32)
+            for h in hidden_of[part_of]
+        ]
+        out = jnp.stack([after(x, returned).astype(bf16) for x in out])
         returned = lax.all_to_all(
             out.reshape(count, dev, SLOTS, feats), "dev", split_axis=1, concat_axis=1, tiled=True
         ).reshape(count, dev * SLOTS, feats)
@@ -130,17 +137,16 @@
     mixed = jnp.concatenate(mixed, axis=0)
     dots = jnp.concatenate(dots, axis=0)
     grads = jnp.stack([jnp.sum(jnp.where(e, dots, 0.0), axis=1) for e in equal], axis=1)
-    grads = relative(grads)
+    own_mixed = [
+        lax.dynamic_index_in_dim(mixed, grp_me ^ split_me ^ m, 0, keepdims=False) for m in range(grp)
+    ]
+    grads = after(relative(grads), own_mixed[1])
+    total = own_mixed[0].astype(f32)
+    for m in range(1, grp):
+        total = total + lax.ppermute(own_mixed[m], "grp", flipped(grp, m)).astype(f32)
     grads = jnp.broadcast_to(grads[:, None], (grp, split, top, rows)).reshape(grp * split, top, rows)
     grads = lax.all_to_all(grads, ("grp", "split"), split_axis=0, concat_axis=0, tiled=True)
     gate_grads = jnp.sum(grads, axis=0).T
-
-    total = 0.0
-    for m in range(grp):
-        piece = lax.dynamic_index_in_dim(mixed, grp_me ^ split_me ^ m, 0, keepdims=False)
-        if m > 0:
-            piece = lax.ppermute(piece, "grp", flipped(grp, m))
-        total = total + piece.astype(f32)
 
     grad_block = sum(
         jnp.dot(hidden_of[j], scaled_rows[j], preferred_element_type=f32) for j in range(grp)

time: 343 us -> 346 us (level)
  blocking collectives: 53.5 us -> 0 us
  waiting for transfers between devices: 99 us -> 143 us
  starting transfers between devices: 106 us -> 119 us
  between operations: 14.8 us -> 6.62 us
    ppermute x3 -> x9, waiting for transfers between devices: 8.39 us -> 65.9 us  [the longest x1 29.8 us: per_device(): w_of.append(lax.ppermute(w_own, 'split', flipped(split, 1)))]
    all_to_all x1 -> x0, blocking collectives: 53.5 us -> none  [per_device(): lax.all_to_all(send.reshape(dev, SLOTS, split * feats), 'dev', split_axis...]
    all_to_all x1, waiting for transfers between devices: 46.1 us -> 0.01 us  [per_device(): lax.all_to_all(scaled, 'dev', split_axis=1, concat_axis=1, tiled=True)]
    ppermute x1, waiting for transfers between devices: 0.28 us -> 26.5 us  [per_device(): hidden_of.append(lax.ppermute(hidden, 'split', flipped(split, 2)))]
    all_to_all x0 -> x1, waiting for transfers between devices: none -> 23 us  [per_device(): lax.all_to_all(send.reshape(dev, SLOTS, split * feats), 'dev', split_axis...]
    ppermute x3 -> x9, starting transfers between devices: 11.8 us -> 34.4 us  [the longest x3 15.8 us: per_device(): lax.ppermute(own_mixed[m], 'grp', flipped(grp, m)).astype(f32)]
    ppermute x1, waiting for transfers between devices: 17.8 us -> 0.01 us  [per_device(): hidden_of.append(lax.ppermute(hidden, 'split', flipped(split, 1)))]
    all_to_all x0 -> x1, starting transfers between devices: none -> 13 us  [per_device(): lax.all_to_all(send.reshape(dev, SLOTS, split * feats), 'dev', split_axis...]
  transfers between devices with their start and end apart: 17 -> 23, of which waited for: 10 -> 9; matrix products, arithmetic and copies ran while one was open for 13% -> 17% of each run, Pallas kernels for 0% -> 0%
where the time goes in v4:
time: 346 us; the launch traced here: 344 us
  waiting for transfers between devices  143 us (41%)
  starting transfers between devices  119 us (34%)
  matrix products  42.2 us (12%)
  local copies, waits for them, and re-layouts  17.8 us (5%)
  other arithmetic  15.1 us (4%)
  between operations  6.62 us (2%)
    ppermute x1, waiting for transfers between devices, per_device(): w_of.append(lax.ppermute(w_own, 'split', flipped(split, 1)))  29.8 us
    all_to_all x3, starting transfers between devices, per_device(): lax.all_to_all(out.reshape(count, dev, SLOTS, feats), 'dev', split_axis=1...  27.5 us
    ppermute x1, waiting for transfers between devices, per_device(): w_of.append(lax.ppermute(w_of[2], 'split', flipped(split, 1)))  27.4 us
    ppermute x1, waiting for transfers between devices, per_device(): hidden_of.append(lax.ppermute(hidden, 'split', flipped(split, 2)))  26.5 us
    all_to_all x1, waiting for transfers between devices, per_device(): lax.all_to_all(send.reshape(dev, SLOTS, split * feats), 'dev', split_axis...  23 us
    all_to_all x3, waiting for transfers between devices, per_device(): lax.all_to_all(out.reshape(count, dev, SLOTS, feats), 'dev', split_axis=1...  20.3 us
    ppermute x4, starting transfers between devices, per_device(): lax.ppermute(tokens, ('grp', 'split'), [(g * split + f, (f ^ m) * split +...  18.1 us
    ppermute x3, starting transfers between devices, per_device(): lax.ppermute(own_mixed[m], 'grp', flipped(grp, m)).astype(f32)  15.8 us
  transfers between devices with their start and end apart: 23, of which 9 were waited for; matrix products, arithmetic and copies ran while one was open for 17% of the time, Pallas kernels for 0%

profile of v4, /device:TPU:1, one launch (start us, length us, event | category | flops | bytes accessed | tf_op | source)
XLA Modules:
  0.0 344.0 jit_solution(1615422445638654079)
XLA Ops:
  0.6 4.2 %collective-permute-start.1 = (bf16[128,512]{1,0:T(8,128)(2,1)}, bf16[128,512]{1,0:T(8,128)(2,1)S(1)}, u32[]{:S(2)}, u32[]{:S(2)}) collective-permute-start(bf16[128,512]{1,0:T(8,128)(2,1)} %param.7), channel_id=1, source_target_pairs={{0,128},{1,0},{2,384},{3,256},{128,129},{129,1},{130,385},{131,257... | collective-permute-start | bytes 393224 | tf_op jit(solution)/shard_map/ppermute | solution.py:46
  4.8 8.3 %collective-permute-start = (bf16[128,512]{1,0:T(8,128)(2,1)}, bf16[128,512]{1,0:T(8,128)(2,1)S(1)}, u32[]{:S(2)}, u32[]{:S(2)}) collective-permute-start(bf16[128,512]{1,0:T(8,128)(2,1)} %param.7), channel_id=1, source_target_pairs={{0,0},{1,128},{2,256},{3,384},{128,1},{129,129},{130,257},{131,385... | collective-permute-start | bytes 393224 | tf_op jit(solution)/shard_map/ppermute | solution.py:46
  13.1 3.1 collective-permute-start.3
  16.2 2.5 collective-permute-start.2
  20.8 5.7 %all-to-all-start = ((bf16[4,32,128]{2,1,0:T(8,128)(2,1)}), bf16[4,32,128]{2,1,0:T(8,128)(2,1)S(1)}, u32[]{:S(2)}, u32[]{:S(2)}) async-start(bf16[4,32,128]{2,1,0:T(8,128)(2,1)} %broadcast_in_dim.119), calls=%async_computation | async-start | bytes 65536 | tf_op jit(solution)/shard_map/all_to_all | solution.py:38
  26.5 7.0 %all-to-all-done = bf16[4,32,128]{2,1,0:T(8,128)(2,1)S(1)} async-done(((bf16[4,32,128]{2,1,0:T(8,128)(2,1)}), bf16[4,32,128]{2,1,0:T(8,128)(2,1)S(1)}, u32[]{:S(2)}, u32[]{:S(2)}) %all-to-all-start) | async-done | bytes 32800 | tf_op jit(solution)/shard_map/all_to_all | solution.py:38
  37.0 13.0 %all-to-all-start.1 = ((bf16[32,16,2048]{2,1,0:T(8,128)(2,1)}), bf16[32,16,2048]{2,1,0:T(8,128)(2,1)S(1)}, u32[]{:S(2)}, u32[]{:S(2)}) async-start(bf16[32,16,2048]{2,1,0:T(8,128)(2,1)} %bitcast.39), calls=%async_computation.1 | async-start | bytes 4194304 | tf_op jit(solution)/shard_map/all_to_all | solution.py:99
  50.1 3.0 collective-permute-start.7
  55.0 7.2 %collective-permute-start.8 = (bf16[128,512]{1,0:T(8,128)(2,1)S(1)}, bf16[128,512]{1,0:T(8,128)(2,1)}, u32[]{:S(2)}, u32[]{:S(2)}) collective-permute-start(bf16[128,512]{1,0:T(8,128)(2,1)S(1)} %copy-done.14), channel_id=1, source_target_pairs={{0,256},{128,384},{256,0},{384,128},{1,257},{129,385},{257,1},{385... | collective-permute-start | bytes 393224 | tf_op jit(solution)/shard_map/ppermute | solution.py:67
  64.8 3.0 fusion
  69.8 2.6 collective-permute-start.4
  75.8 23.0 %all-to-all-done.1 = bf16[32,16,2048]{2,1,0:T(8,128)(2,1)S(1)} async-done(((bf16[32,16,2048]{2,1,0:T(8,128)(2,1)}), bf16[32,16,2048]{2,1,0:T(8,128)(2,1)S(1)}, u32[]{:S(2)}, u32[]{:S(2)}) %all-to-all-start.1) | async-done | bytes 2097184 | tf_op jit(solution)/shard_map/all_to_all | solution.py:99
  103.5 7.1 %all-to-all-start.2 = ((bf16[4,32,16,512]{3,2,0,1:T(8,128)(2,1)}), bf16[4,32,16,512]{3,2,0,1:T(8,128)(2,1)S(1)}, u32[]{:S(2)}, u32[]{:S(2)}) async-start(bf16[4,32,16,512]{3,2,0,1:T(8,128)(2,1)} %copy.71), calls=%async_computation.2 | async-start | bytes 4194304 | tf_op jit(solution)/shard_map/all_to_all | solution.py:104
  110.6 29.8 %collective-permute-done.4 = bf16[384,2048]{1,0:T(8,128)(2,1)} collective-permute-done((bf16[384,2048]{1,0:T(8,128)(2,1)}, bf16[384,2048]{1,0:T(8,128)(2,1)}, u32[]{:S(2)}, u32[]{:S(2)}) %collective-permute-start.4) | collective-permute-done | bytes 1572896 | tf_op jit(solution)/shard_map/ppermute | solution.py:61
  152.4 27.4 %collective-permute-done.6 = bf16[384,2048]{1,0:T(8,128)(2,1)S(1)} collective-permute-done((bf16[384,2048]{1,0:T(8,128)(2,1)S(1)}, bf16[384,2048]{1,0:T(8,128)(2,1)S(1)}, u32[]{:S(2)}, u32[]{:S(2)}) %collective-permute-start.6) | collective-permute-done | bytes 1572896 | tf_op jit(solution)/shard_map/ppermute | solution.py:64
  184.8 9.5 %all-to-all-start.3 = ((bf16[1,32,16,512]{3,2,0,1:T(8,128)(2,1)}), bf16[1,32,16,512]{3,2,0,1:T(8,128)(2,1)S(1)}, u32[]{:S(2)}, u32[]{:S(2)}) async-start(bf16[1,32,16,512]{3,2,0,1:T(8,128)(2,1)} %bitcast.272), calls=%async_computation.3 | async-start | bytes 1048576 | tf_op jit(solution)/shard_map/all_to_all | solution.py:126
  194.3 3.2 collective-permute-start.11
  197.5 3.3 collective-permute-start.10
  200.7 5.4 %all-to-all-done.3 = bf16[1,32,16,512]{3,2,0,1:T(8,128)(2,1)S(1)} async-done(((bf16[1,32,16,512]{3,2,0,1:T(8,128)(2,1)}), bf16[1,32,16,512]{3,2,0,1:T(8,128)(2,1)S(1)}, u32[]{:S(2)}, u32[]{:S(2)}) %all-to-all-start.3) | async-done | bytes 524320 | tf_op jit(solution)/shard_map/all_to_all | solution.py:126
  207.2 26.5 %collective-permute-done.11 = bf16[768,512]{1,0:T(8,128)(2,1)} collective-permute-done((bf16[768,512]{1,0:T(8,128)(2,1)}, bf16[768,512]{1,0:T(8,128)(2,1)}, u32[]{:S(2)}, u32[]{:S(2)}) %collective-permute-start.11) | collective-permute-done | bytes 786464 | tf_op jit(solution)/shard_map/ppermute | solution.py:114
  238.4 9.4 %all-to-all-start.4 = ((bf16[2,32,16,512]{3,2,0,1:T(8,128)(2,1)}), bf16[2,32,16,512]{3,2,0,1:T(8,128)(2,1)}, u32[]{:S(2)}, u32[]{:S(2)}) async-start(bf16[2,32,16,512]{3,2,0,1:T(8,128)(2,1)} %pad_maximum_fusion), calls=%async_computation.4 | async-start | bytes 2097152 | tf_op jit(solution)/shard_map/all_to_all | solution.py:126
  256.7 2.8 fusion.127
  259.5 3.0 fusion.126
  265.5 6.8 %all-to-all-done.4 = bf16[2,32,16,512]{3,2,0,1:T(8,128)(2,1)} async-done(((bf16[2,32,16,512]{3,2,0,1:T(8,128)(2,1)}), bf16[2,32,16,512]{3,2,0,1:T(8,128)(2,1)}, u32[]{:S(2)}, u32[]{:S(2)}) %all-to-all-start.4) | async-done | bytes 1048608 | tf_op jit(solution)/shard_map/all_to_all | solution.py:126
  274.9 2.6 fusion.4
  277.4 8.7 %all-to-all-start.5 = ((bf16[1,32,16,512]{3,2,0,1:T(8,128)(2,1)}), bf16[1,32,16,512]{3,2,0,1:T(8,128)(2,1)}, u32[]{:S(2)}, u32[]{:S(2)}) async-start(bf16[1,32,16,512]{3,2,0,1:T(8,128)(2,1)} %bitcast.271), calls=%async_computation.5 | async-start | bytes 1048576 | tf_op jit(solution)/shard_map/all_to_all | solution.py:126
  291.8 8.1 %all-to-all-done.5 = bf16[1,32,16,512]{3,2,0,1:T(8,128)(2,1)} async-done(((bf16[1,32,16,512]{3,2,0,1:T(8,128)(2,1)}), bf16[1,32,16,512]{3,2,0,1:T(8,128)(2,1)}, u32[]{:S(2)}, u32[]{:S(2)}) %all-to-all-start.5) | async-done | bytes 524320 | tf_op jit(solution)/shard_map/all_to_all | solution.py:126
  305.1 6.4 %collective-permute-start.13 = (bf16[128,512]{1,0:T(8,128)(2,1)}, bf16[128,512]{1,0:T(8,128)(2,1)}, u32[]{:S(2)}, u32[]{:S(2)}) collective-permute-start(bf16[128,512]{1,0:T(8,128)(2,1)} %get-tuple-element.19), channel_id=1, source_target_pairs={{0,128},{128,0},{256,384},{384,256},{1,129},{129,1},{257,385},{385... | collective-permute-start | bytes 393224 | tf_op jit(solution)/shard_map/ppermute | solution.py:146
  314.6 5.1 %all-to-all-start.6 = ((f32[16,8,128]{2,1,0:T(8,128)}), f32[16,8,128]{2,1,0:T(8,128)S(1)}, u32[]{:S(2)}, u32[]{:S(2)}) async-start(f32[16,8,128]{2,1,0:T(8,128)} %bitcast.105), calls=%async_computation.6 | async-start | bytes 131072 | tf_op jit(solution)/shard_map/all_to_all | solution.py:148
  319.7 7.4 %collective-permute-start.15 = (bf16[128,512]{1,0:T(8,128)(2,1)}, bf16[128,512]{1,0:T(8,128)(2,1)}, u32[]{:S(2)}, u32[]{:S(2)}) collective-permute-start(bf16[128,512]{1,0:T(8,128)(2,1)} %get-tuple-element.20), channel_id=1, source_target_pairs={{0,384},{128,256},{256,128},{384,0},{1,385},{129,257},{257,129},{3... | collective-permute-start | bytes 393224 | tf_op jit(solution)/shard_map/ppermute | solution.py:146
  329.1 3.8 %add_bitcast_fusion = f32[1,768,512]{2,1,0:T(8,128)} fusion(f32[768,512]{1,0:T(8,128)} %fusion.127, f32[768,512]{1,0:T(8,128)S(1)} %copy-done.2, f32[768,512]{1,0:T(8,128)} %fusion.126, bf16[768,512]{1,0:T(8,128)(2,1)} %collective-permute-done.12, bf16[512,512]{1,0:T(8,128)(2,1)S(1)} %bitcast.268), kind=kOutput, calls=%fused_computation.4 | convolution fusion | flops 403832832 | bytes 7602176 | tf_op jit(solution)/shard_map/dot_general | solution.py:152
  333.6 8.6 %collective-permute-done.14 = bf16[128,512]{1,0:T(8,128)(2,1)} collective-permute-done((bf16[128,512]{1,0:T(8,128)(2,1)}, bf16[128,512]{1,0:T(8,128)(2,1)}, u32[]{:S(2)}, u32[]{:S(2)}) %collective-permute-start.14) | collective-permute-done | bytes 131104 | tf_op jit(solution)/shard_map/ppermute | solution.py:146
  (156 shorter events, 69.7 us)
Async XLA Ops:
  0.6 182.8 %copy-start = (bf16[1,768,512]{2,1,0:T(8,128)(2,1)S(1)}, bf16[1,768,512]{2,1,0:T(8,128)(2,1)}, u32[]{:S(2)}) copy-start(bf16[1,768,512]{2,1,0:T(8,128)(2,1)} %param.13) | copy-start | bytes 2359300
  0.6 33.6 %collective-permute-start.1 = (bf16[128,512]{1,0:T(8,128)(2,1)}, bf16[128,512]{1,0:T(8,128)(2,1)S(1)}, u32[]{:S(2)}, u32[]{:S(2)}) collective-permute-start(bf16[128,512]{1,0:T(8,128)(2,1)} %param.7), channel_id=1, source_target_pairs={{0,128},{1,0},{2,384},{3,256},{128,129},{129,1},{130,385},{131,257... | collective-permute-start | bytes 393224 | tf_op jit(solution)/shard_map/ppermute | solution.py:46
  4.8 29.4 %collective-permute-start = (bf16[128,512]{1,0:T(8,128)(2,1)}, bf16[128,512]{1,0:T(8,128)(2,1)S(1)}, u32[]{:S(2)}, u32[]{:S(2)}) collective-permute-start(bf16[128,512]{1,0:T(8,128)(2,1)} %param.7), channel_id=1, source_target_pairs={{0,0},{1,128},{2,256},{3,384},{128,1},{129,129},{130,257},{131,385... | collective-permute-start | bytes 393224 | tf_op jit(solution)/shard_map/ppermute | solution.py:46
  13.1 21.1 %collective-permute-start.3 = (bf16[128,512]{1,0:T(8,128)(2,1)}, bf16[128,512]{1,0:T(8,128)(2,1)S(1)}, u32[]{:S(2)}, u32[]{:S(2)}) collective-permute-start(bf16[128,512]{1,0:T(8,128)(2,1)} %param.7), channel_id=1, source_target_pairs={{0,384},{1,256},{2,128},{3,0},{128,385},{129,257},{130,129},{131,1... | collective-permute-start | bytes 393224 | tf_op jit(solution)/shard_map/ppermute | solution.py:46
  16.2 18.0 %collective-permute-start.2 = (bf16[128,512]{1,0:T(8,128)(2,1)}, bf16[128,512]{1,0:T(8,128)(2,1)S(1)}, u32[]{:S(2)}, u32[]{:S(2)}) collective-permute-start(bf16[128,512]{1,0:T(8,128)(2,1)} %param.7), channel_id=1, source_target_pairs={{0,256},{1,384},{2,0},{3,128},{128,257},{129,385},{130,1},{131,129... | collective-permute-start | bytes 393224 | tf_op jit(solution)/shard_map/ppermute | solution.py:46
  20.8 12.8 %all-to-all-start = ((bf16[4,32,128]{2,1,0:T(8,128)(2,1)}), bf16[4,32,128]{2,1,0:T(8,128)(2,1)S(1)}, u32[]{:S(2)}, u32[]{:S(2)}) async-start(bf16[4,32,128]{2,1,0:T(8,128)(2,1)} %broadcast_in_dim.119), calls=%async_computation | async-start | bytes 65536 | tf_op jit(solution)/shard_map/all_to_all | solution.py:38
  26.5 36.9 %copy-start.27 = (f32[32]{0:T(128)}, f32[32]{0:T(128)S(1)}, u32[]{:S(2)}) copy-start(f32[32]{0:T(128)S(1)} %iota_add_fusion) | copy-start | bytes 388
  33.7 29.7 %copy-start.18 = (f32[4,128]{1,0:T(4,128)}, f32[4,128]{1,0:T(4,128)S(1)}, u32[]{:S(2)}) copy-start(f32[4,128]{1,0:T(4,128)S(1)} %get-tuple-element.69) | copy-start | bytes 6148
  33.7 29.7 %copy-start.20 = (f32[4,128]{1,0:T(4,128)}, f32[4,128]{1,0:T(4,128)S(1)}, u32[]{:S(2)}) copy-start(f32[4,128]{1,0:T(4,128)S(1)} %get-tuple-element.70) | copy-start | bytes 6148
  33.7 29.7 %copy-start.22 = (f32[4,128]{1,0:T(4,128)}, f32[4,128]{1,0:T(4,128)S(1)}, u32[]{:S(2)}) copy-start(f32[4,128]{1,0:T(4,128)S(1)} %get-tuple-element.71) | copy-start | bytes 6148
  33.7 29.7 %copy-start.24 = (f32[4,128]{1,0:T(4,128)}, f32[4,128]{1,0:T(4,128)S(1)}, u32[]{:S(2)}) copy-start(f32[4,128]{1,0:T(4,128)S(1)} %get-tuple-element.72) | copy-start | bytes 6148
  37.0 61.8 %all-to-all-start.1 = ((bf16[32,16,2048]{2,1,0:T(8,128)(2,1)}), bf16[32,16,2048]{2,1,0:T(8,128)(2,1)S(1)}, u32[]{:S(2)}, u32[]{:S(2)}) async-start(bf16[32,16,2048]{2,1,0:T(8,128)(2,1)} %bitcast.39), calls=%async_computation.1 | async-start | bytes 4194304 | tf_op jit(solution)/shard_map/all_to_all | solution.py:99
  50.1 23.9 %collective-permute-start.7 = (bf16[128,512]{1,0:T(8,128)(2,1)S(1)}, bf16[128,512]{1,0:T(8,128)(2,1)}, u32[]{:S(2)}, u32[]{:S(2)}) collective-permute-start(bf16[128,512]{1,0:T(8,128)(2,1)S(1)} %copy-done.14), channel_id=1, source_target_pairs={{0,128},{128,0},{256,384},{384,256},{1,129},{129,1},{257,385},{385... | collective-permute-start | bytes 393224 | tf_op jit(solution)/shard_map/ppermute | solution.py:67
  53.0 20.9 %collective-permute-start.9 = (bf16[128,512]{1,0:T(8,128)(2,1)S(1)}, bf16[128,512]{1,0:T(8,128)(2,1)}, u32[]{:S(2)}, u32[]{:S(2)}) collective-permute-start(bf16[128,512]{1,0:T(8,128)(2,1)S(1)} %copy-done.14), channel_id=1, source_target_pairs={{0,384},{128,256},{256,128},{384,0},{1,385},{129,257},{257,129},{3... | collective-permute-start | bytes 393224 | tf_op jit(solution)/shard_map/ppermute | solution.py:67
  55.0 19.0 %collective-permute-start.8 = (bf16[128,512]{1,0:T(8,128)(2,1)S(1)}, bf16[128,512]{1,0:T(8,128)(2,1)}, u32[]{:S(2)}, u32[]{:S(2)}) collective-permute-start(bf16[128,512]{1,0:T(8,128)(2,1)S(1)} %copy-done.14), channel_id=1, source_target_pairs={{0,256},{128,384},{256,0},{384,128},{1,257},{129,385},{257,1},{385... | collective-permute-start | bytes 393224 | tf_op jit(solution)/shard_map/ppermute | solution.py:67
  67.8 74.5 %collective-permute-start.5 = (bf16[384,2048]{1,0:T(8,128)(2,1)}, bf16[384,2048]{1,0:T(8,128)(2,1)}, u32[]{:S(2)}, u32[]{:S(2)}) collective-permute-start(bf16[384,2048]{1,0:T(8,128)(2,1)} %fusion), channel_id=1, source_target_pairs={{0,2},{1,3},{2,0},{3,1},{4,6},{5,7},{6,4},{7,5},{8,10},{9,11},{10,... | collective-permute-start | bytes 4718600 | tf_op jit(solution)/shard_map/ppermute | solution.py:62
  69.8 70.6 %collective-permute-start.4 = (bf16[384,2048]{1,0:T(8,128)(2,1)}, bf16[384,2048]{1,0:T(8,128)(2,1)}, u32[]{:S(2)}, u32[]{:S(2)}) collective-permute-start(bf16[384,2048]{1,0:T(8,128)(2,1)} %fusion), channel_id=1, source_target_pairs={{0,1},{1,0},{2,3},{3,2},{4,5},{5,4},{6,7},{7,6},{8,9},{9,8},{10,11... | collective-permute-start | bytes 4718600 | tf_op jit(solution)/shard_map/ppermute | solution.py:61
  75.8 26.2 %copy-start.12 = (bf16[1,128,512]{2,1,0:T(8,128)(2,1)}, bf16[1,128,512]{2,1,0:T(8,128)(2,1)S(1)}, u32[]{:S(2)}) copy-start(bf16[1,128,512]{2,1,0:T(8,128)(2,1)S(1)} %get-tuple-element.25) | copy-start | bytes 393220
  103.5 78.6 %all-to-all-start.2 = ((bf16[4,32,16,512]{3,2,0,1:T(8,128)(2,1)}), bf16[4,32,16,512]{3,2,0,1:T(8,128)(2,1)S(1)}, u32[]{:S(2)}, u32[]{:S(2)}) async-start(bf16[4,32,16,512]{3,2,0,1:T(8,128)(2,1)} %copy.71), calls=%async_computation.2 | async-start | bytes 4194304 | tf_op jit(solution)/shard_map/all_to_all | solution.py:104
  144.0 35.8 %collective-permute-start.6 = (bf16[384,2048]{1,0:T(8,128)(2,1)S(1)}, bf16[384,2048]{1,0:T(8,128)(2,1)S(1)}, u32[]{:S(2)}, u32[]{:S(2)}) collective-permute-start(bf16[384,2048]{1,0:T(8,128)(2,1)S(1)} %broadcast_add_fusion), channel_id=1, source_target_pairs={{0,1},{1,0},{2,3},{3,2},{4,5},{5,4},{6,7},{7,6},{8,9},{9,8},{10,11... | collective-permute-start | bytes 4718600 | tf_op jit(solution)/shard_map/ppermute | solution.py:64
  184.8 21.3 %all-to-all-start.3 = ((bf16[1,32,16,512]{3,2,0,1:T(8,128)(2,1)}), bf16[1,32,16,512]{3,2,0,1:T(8,128)(2,1)S(1)}, u32[]{:S(2)}, u32[]{:S(2)}) async-start(bf16[1,32,16,512]{3,2,0,1:T(8,128)(2,1)} %bitcast.272), calls=%async_computation.3 | async-start | bytes 1048576 | tf_op jit(solution)/shard_map/all_to_all | solution.py:126
  194.3 39.5 %collective-permute-start.11 = (bf16[768,512]{1,0:T(8,128)(2,1)}, bf16[768,512]{1,0:T(8,128)(2,1)}, u32[]{:S(2)}, u32[]{:S(2)}) collective-permute-start(bf16[768,512]{1,0:T(8,128)(2,1)} %bitcast.252), channel_id=1, source_target_pairs={{0,2},{1,3},{2,0},{3,1},{4,6},{5,7},{6,4},{7,5},{8,10},{9,11},{10,... | collective-permute-start | bytes 2359304 | tf_op jit(solution)/shard_map/ppermute | solution.py:114
  197.5 38.0 %collective-permute-start.10 = (bf16[768,512]{1,0:T(8,128)(2,1)}, bf16[768,512]{1,0:T(8,128)(2,1)}, u32[]{:S(2)}, u32[]{:S(2)}) collective-permute-start(bf16[768,512]{1,0:T(8,128)(2,1)} %bitcast.253), channel_id=1, source_target_pairs={{0,1},{1,0},{2,3},{3,2},{4,5},{5,4},{6,7},{7,6},{8,9},{9,8},{10,11... | collective-permute-start | bytes 2359304 | tf_op jit(solution)/shard_map/ppermute | solution.py:113
  238.4 34.0 %all-to-all-start.4 = ((bf16[2,32,16,512]{3,2,0,1:T(8,128)(2,1)}), bf16[2,32,16,512]{3,2,0,1:T(8,128)(2,1)}, u32[]{:S(2)}, u32[]{:S(2)}) async-start(bf16[2,32,16,512]{3,2,0,1:T(8,128)(2,1)} %pad_maximum_fusion), calls=%async_computation.4 | async-start | bytes 2097152 | tf_op jit(solution)/shard_map/all_to_all | solution.py:126
  251.9 22.9 %collective-permute-start.12 = (bf16[768,512]{1,0:T(8,128)(2,1)}, bf16[768,512]{1,0:T(8,128)(2,1)}, u32[]{:S(2)}, u32[]{:S(2)}) collective-permute-start(bf16[768,512]{1,0:T(8,128)(2,1)} %collective-permute-done.11), channel_id=1, source_target_pairs={{0,1},{1,0},{2,3},{3,2},{4,5},{5,4},{6,7},{7,6},{8,9},{9,8},{10,11... | collective-permute-start | bytes 2359304 | tf_op jit(solution)/shard_map/ppermute | solution.py:120
  277.4 22.4 %all-to-all-start.5 = ((bf16[1,32,16,512]{3,2,0,1:T(8,128)(2,1)}), bf16[1,32,16,512]{3,2,0,1:T(8,128)(2,1)}, u32[]{:S(2)}, u32[]{:S(2)}) async-start(bf16[1,32,16,512]{3,2,0,1:T(8,128)(2,1)} %bitcast.271), calls=%async_computation.5 | async-start | bytes 1048576 | tf_op jit(solution)/shard_map/all_to_all | solution.py:126
  303.0 26.1 %copy-start.2 = (f32[768,512]{1,0:T(8,128)S(1)}, f32[768,512]{1,0:T(8,128)}, u32[]{:S(2)}) copy-start(f32[768,512]{1,0:T(8,128)} %fusion.125) | copy-start | bytes 4718596
  303.0 26.1 %copy-start.8 = (bf16[1,32,16,512]{3,2,0,1:T(8,128)(2,1)S(1)}, bf16[1,32,16,512]{3,2,0,1:T(8,128)(2,1)}, u32[]{:S(2)}) copy-start(bf16[1,32,16,512]{3,2,0,1:T(8,128)(2,1)} %get-tuple-element.11) | copy-start | bytes 1572868
  305.1 37.2 %collective-permute-start.13 = (bf16[128,512]{1,0:T(8,128)(2,1)}, bf16[128,512]{1,0:T(8,128)(2,1)}, u32[]{:S(2)}, u32[]{:S(2)}) collective-permute-start(bf16[128,512]{1,0:T(8,128)(2,1)} %get-tuple-element.19), channel_id=1, source_target_pairs={{0,128},{128,0},{256,384},{384,256},{1,129},{129,1},{257,385},{385... | collective-permute-start | bytes 393224 | tf_op jit(solution)/shard_map/ppermute | solution.py:146
  314.6 18.4 %all-to-all-start.6 = ((f32[16,8,128]{2,1,0:T(8,128)}), f32[16,8,128]{2,1,0:T(8,128)S(1)}, u32[]{:S(2)}, u32[]{:S(2)}) async-start(f32[16,8,128]{2,1,0:T(8,128)} %bitcast.105), calls=%async_computation.6 | async-start | bytes 131072 | tf_op jit(solution)/shard_map/all_to_all | solution.py:148
  319.7 13.8 %collective-permute-start.15 = (bf16[128,512]{1,0:T(8,128)(2,1)}, bf16[128,512]{1,0:T(8,128)(2,1)}, u32[]{:S(2)}, u32[]{:S(2)}) collective-permute-start(bf16[128,512]{1,0:T(8,128)(2,1)} %get-tuple-element.20), channel_id=1, source_target_pairs={{0,384},{128,256},{256,128},{384,0},{1,385},{129,257},{257,129},{3... | collective-permute-start | bytes 393224 | tf_op jit(solution)/shard_map/ppermute | solution.py:146
  327.2 15.0 %collective-permute-start.14 = (bf16[128,512]{1,0:T(8,128)(2,1)}, bf16[128,512]{1,0:T(8,128)(2,1)}, u32[]{:S(2)}, u32[]{:S(2)}) collective-permute-start(bf16[128,512]{1,0:T(8,128)(2,1)} %get-tuple-element.21), channel_id=1, source_target_pairs={{0,256},{128,384},{256,0},{384,128},{1,257},{129,385},{257,1},{385... | collective-permute-start | bytes 393224 | tf_op jit(solution)/shard_map/ppermute | solution.py:146
  (20 other events, 134.8 us)

commit v5 on v4

--- a/solution.py
+++ b/solution.py
@@ -41,6 +41,9 @@
         parts = [lax.dynamic_index_in_dim(x, split_me ^ j, 0, keepdims=True) for j in range(grp)]
         return jnp.concatenate(parts, axis=0)
 
+    w_own = jnp.concatenate([w_gate[0].T, w_up[0].T], axis=0)
+    w_all = lax.all_gather(w_own, "split", axis=0, tiled=False)
+
     pieces = jnp.stack(
         [
             lax.ppermute(
@@ -54,15 +57,6 @@
 
     meta = jnp.concatenate([expert_ids.T.astype(bf16)] + bf16_pieces(gate_probs.T, 3), axis=0)
     near = spread(meta)
-    w_own = jnp.concatenate([w_gate[0].T, w_up[0].T], axis=0)
-    w_own = after(after(w_own, near), pieces)
-
-    w_of = [w_own]
-    w_of.append(lax.ppermute(w_own, "split", flipped(split, 1)))
-    w_of.append(lax.ppermute(w_own, "split", flipped(split, 2)))
-    w_of[2] = after(w_of[2], w_of[1])
-    w_of.append(lax.ppermute(w_of[2], "split", flipped(split, 1)))
-
     near_upstream = jnp.stack(
         [upstream] + [lax.ppermute(upstream, "grp", flipped(grp, m)) for m in range(1, grp)]
     )
@@ -104,11 +98,13 @@
     scaled_rows = lax.all_to_all(scaled, "dev", split_axis=1, concat_axis=1, tiled=True)
     scaled_rows = scaled_rows.reshape(grp, dev * SLOTS, feats)
 
-    hidden = []
-    for w in w_of:
-        pre = lax.dot_general(w, arrived, (((1,), (1,)), ((), ())), preferred_element_type=f32)
-        hidden.append((jax.nn.silu(pre[:hidden_part]) * pre[hidden_part:]).astype(bf16))
-    hidden = relative(jnp.stack(hidden)).reshape(split * hidden_part, dev * SLOTS)
+    pre = lax.dot_general(
+        w_all.reshape(split * 2 * hidden_part, split * feats),
+        arrived,
+        (((1,), (1,)), ((), ())),
+        preferred_element_type=f32,
+    ).reshape(split, 2, hidden_part, dev * SLOTS)
+    hidden = (jax.nn.silu(pre[:, 0]) * pre[:, 1]).astype(bf16).reshape(split * hidden_part, dev * SLOTS)
     hidden_of = [hidden]
     hidden_of.append(lax.ppermute(hidden, "split", flipped(split, 1)))
     hidden_of.append(lax.ppermute(hidden, "split", flipped(split, 2)))
@@ -119,10 +115,10 @@
         if part_of.start == 1:
             hidden_of.append(lax.ppermute(hidden_of[2], "split", flipped(split, 1)))
         out = [
-            lax.dot_general(h, w_down[0], (((0,), (0,)), ((), ())), preferred_element_type=f32)
+            lax.dot_general(h, w_down[0], (((0,), (0,)), ((), ())), preferred_element_type=f32).astype(bf16)
             for h in hidden_of[part_of]
         ]
-        out = jnp.stack([after(x, returned).astype(bf16) for x in out])
+        out = after(lax.optimization_barrier(jnp.stack(out)), returned)
         returned = lax.all_to_all(
             out.reshape(count, dev, SLOTS, feats), "dev", split_axis=1, concat_axis=1, tiled=True
         ).reshape(count, dev * SLOTS, feats)

time: 346 us -> 331 us (0.957)
  waiting for transfers between devices: 143 us -> 81.4 us
  blocking collectives: 0 us -> 54.2 us
  starting transfers between devices: 119 us -> 104 us
  between operations: 6.62 us -> 18.3 us
    ppermute x3 -> x0, waiting for transfers between devices: 57.2 us -> none  [the longest x1 29.8 us: per_device(): w_of.append(lax.ppermute(w_own, 'split', flipped(split, 1)))]
    all_to_all x0 -> x1, blocking collectives: none -> 54.2 us  [per_device(): lax.all_to_all(scaled, 'dev', split_axis=1, concat_axis=1, tiled=True)]
    all_to_all x3, waiting for transfers between devices: 20.3 us -> 6.15 us  [per_device(): lax.all_to_all(out.reshape(count, dev, SLOTS, feats), 'dev', split_axis=1...]
    ppermute x3, waiting for transfers between devices: 0.01 us -> 8.99 us  [per_device(): lax.ppermute(upstream, 'grp', flipped(grp, m))]
    ppermute x3, waiting for transfers between devices: 8.65 us -> 0.01 us  [per_device(): lax.ppermute(own_mixed[m], 'grp', flipped(grp, m)).astype(f32)]
    ppermute x1, waiting for transfers between devices: 0.01 us -> 8.6 us  [per_device(): hidden_of.append(lax.ppermute(hidden_of[2], 'split', flipped(split, 1)))]
    all_to_all x1 -> x0, starting transfers between devices: 7.1 us -> none  [per_device(): lax.all_to_all(scaled, 'dev', split_axis=1, concat_axis=1, tiled=True)]
    ppermute x3 -> x0, starting transfers between devices: 6.58 us -> none  [the longest x1 2.64 us: per_device(): w_of.append(lax.ppermute(w_own, 'split', flipped(split, 1)))]
  transfers between devices with their start and end apart: 23 -> 20, of which waited for: 9 -> 8; matrix products, arithmetic and copies ran while one was open for 17% -> 15% of each run, Pallas kernels for 0% -> 0%
where the time goes in v5:
time: 331 us; the launch traced here: 330 us
  starting transfers between devices  104 us (31%)
  waiting for transfers between devices  81.4 us (25%)
  blocking collectives  54.2 us (16%)
  matrix products  39.5 us (12%)
  between operations  18.3 us (6%)
  local copies, waits for them, and re-layouts  17.4 us (5%)
  other arithmetic  15.3 us (5%)
    all_to_all x1, blocking collectives, per_device(): lax.all_to_all(scaled, 'dev', split_axis=1, concat_axis=1, tiled=True)  54.2 us
    all_to_all x3, starting transfers between devices, per_device(): lax.all_to_all(out.reshape(count, dev, SLOTS, feats), 'dev', split_axis=1...  26.4 us
    all_to_all x1, waiting for transfers between devices, per_device(): lax.all_to_all(send.reshape(dev, SLOTS, split * feats), 'dev', split_axis...  24 us
    ppermute x1, waiting for transfers between devices, per_device(): hidden_of.append(lax.ppermute(hidden, 'split', flipped(split, 2)))  22.8 us
    ppermute x4, starting transfers between devices, per_device(): lax.ppermute(tokens, ('grp', 'split'), [(g * split + f, (f ^ m) * split +...  17 us
    ppermute x3, starting transfers between devices, per_device(): lax.ppermute(own_mixed[m], 'grp', flipped(grp, m)).astype(f32)  16.8 us
    all_to_all x1, starting transfers between devices, per_device(): lax.all_to_all(send.reshape(dev, SLOTS, split * feats), 'dev', split_axis...  13 us
    ppermute x3, starting transfers between devices, per_device(): lax.ppermute(upstream, 'grp', flipped(grp, m))  12.1 us
  transfers between devices with their start and end apart: 20, of which 8 were waited for; matrix products, arithmetic and copies ran while one was open for 15% of the time, Pallas kernels for 0%

profile of v5, /device:TPU:1, one launch (start us, length us, event | category | flops | bytes accessed | tf_op | source)
XLA Modules:
  0.0 329.7 jit_solution(8772009421357661182)
XLA Ops:
  7.2 7.6 %collective-permute-start.3 = (bf16[128,512]{1,0:T(8,128)(2,1)}, bf16[128,512]{1,0:T(8,128)(2,1)S(1)}, u32[]{:S(2)}, u32[]{:S(2)}) collective-permute-start(bf16[128,512]{1,0:T(8,128)(2,1)} %param.7), channel_id=1, source_target_pairs={{0,384},{1,256},{2,128},{3,0},{128,385},{129,257},{130,129},{131,1... | collective-permute-start | bytes 393224 | tf_op jit(solution)/shard_map/ppermute | solution.py:49
  14.9 3.1 collective-permute-start.2
  18.0 2.9 collective-permute-start.1
  20.9 3.3 collective-permute-start
  24.2 2.7 pad_maximum_fusion
  28.2 6.0 %all-to-all-start = ((bf16[4,32,128]{2,1,0:T(8,128)(2,1)}), bf16[4,32,128]{2,1,0:T(8,128)(2,1)S(1)}, u32[]{:S(2)}, u32[]{:S(2)}) async-start(bf16[4,32,128]{2,1,0:T(8,128)(2,1)} %broadcast_in_dim.119), calls=%async_computation | async-start | bytes 65536 | tf_op jit(solution)/shard_map/all_to_all | solution.py:38
  34.2 7.1 %all-to-all-done = bf16[4,32,128]{2,1,0:T(8,128)(2,1)S(1)} async-done(((bf16[4,32,128]{2,1,0:T(8,128)(2,1)}), bf16[4,32,128]{2,1,0:T(8,128)(2,1)S(1)}, u32[]{:S(2)}, u32[]{:S(2)}) %all-to-all-start) | async-done | bytes 32800 | tf_op jit(solution)/shard_map/all_to_all | solution.py:38
  42.8 2.1 convolution_convert_fusion
  44.9 13.0 %all-to-all-start.1 = ((bf16[32,16,2048]{2,1,0:T(8,128)(2,1)}), bf16[32,16,2048]{2,1,0:T(8,128)(2,1)S(1)}, u32[]{:S(2)}, u32[]{:S(2)}) async-start(bf16[32,16,2048]{2,1,0:T(8,128)(2,1)} %bitcast.38), calls=%async_computation.1 | async-start | bytes 4194304 | tf_op jit(solution)/shard_map/all_to_all | solution.py:93
  57.9 2.5 collective-permute-start.6
  60.4 7.7 %collective-permute-start.5 = (bf16[128,512]{1,0:T(8,128)(2,1)S(1)}, bf16[128,512]{1,0:T(8,128)(2,1)}, u32[]{:S(2)}, u32[]{:S(2)}) collective-permute-start(bf16[128,512]{1,0:T(8,128)(2,1)S(1)} %copy-done.15), channel_id=1, source_target_pairs={{0,256},{128,384},{256,0},{384,128},{1,257},{129,385},{257,1},{385... | collective-permute-start | bytes 393224 | tf_op jit(solution)/shard_map/ppermute | solution.py:61
  73.3 7.5 %collective-permute-done.5 = bf16[128,512]{1,0:T(8,128)(2,1)} collective-permute-done((bf16[128,512]{1,0:T(8,128)(2,1)S(1)}, bf16[128,512]{1,0:T(8,128)(2,1)}, u32[]{:S(2)}, u32[]{:S(2)}) %collective-permute-start.5) | collective-permute-done | bytes 131104 | tf_op jit(solution)/shard_map/ppermute | solution.py:61
  82.7 24.0 %all-to-all-done.1 = bf16[32,16,2048]{2,1,0:T(8,128)(2,1)S(1)} async-done(((bf16[32,16,2048]{2,1,0:T(8,128)(2,1)}), bf16[32,16,2048]{2,1,0:T(8,128)(2,1)S(1)}, u32[]{:S(2)}, u32[]{:S(2)}) %all-to-all-start.1) | async-done | bytes 2097184 | tf_op jit(solution)/shard_map/all_to_all | solution.py:93
  110.1 54.2 %all_to_all.35 = bf16[4,32,16,512]{3,2,0,1:T(8,128)(2,1)S(1)} all-to-all(bf16[4,32,16,512]{3,2,0,1:T(8,128)(2,1)S(1)} %copy.62), channel_id=1, replica_groups=mesh['grp'=4,'dev'=32,'split'=4] {'dev'}, dimensions={1} | all-to-all | bytes 4194304 | tf_op jit(solution)/shard_map/all_to_all | solution.py:98
  165.8 6.2 %fusion.116 = f32[4,2,192,512]{3,2,1,0:T(8,128)S(1)} fusion(bf16[4,2,192,2048]{3,2,1,0:T(8,128)(2,1)} %bitcast.298, bf16[512,2048,1,1]{1,0,3,2:T(8,128)(2,1)} %bitcast.265), kind=kOutput, calls=%fused_computation.222 | convolution fusion | flops 3221225472 | bytes 11534336 | tf_op jit(solution)/shard_map/dot_general | solution.py:101
  174.2 2.8 collective-permute-start.8
  177.0 2.5 collective-permute-start.7
  181.1 8.5 %all-to-all-start.3 = ((bf16[1,32,16,512]{3,2,0,1:T(8,128)(2,1)}), bf16[1,32,16,512]{3,2,0,1:T(8,128)(2,1)S(1)}, u32[]{:S(2)}, u32[]{:S(2)}) async-start(bf16[1,32,16,512]{3,2,0,1:T(8,128)(2,1)} %bitcast.269), calls=%async_computation.3 | async-start | bytes 1048576 | tf_op jit(solution)/shard_map/all_to_all | solution.py:122
  189.6 22.8 %collective-permute-done.8 = bf16[768,512]{1,0:T(8,128)(2,1)} collective-permute-done((bf16[768,512]{1,0:T(8,128)(2,1)}, bf16[768,512]{1,0:T(8,128)(2,1)}, u32[]{:S(2)}, u32[]{:S(2)}) %collective-permute-start.8) | collective-permute-done | bytes 786464 | tf_op jit(solution)/shard_map/ppermute | solution.py:110
  220.6 9.0 %all-to-all-start.4 = ((bf16[2,32,16,512]{3,2,0,1:T(8,128)(2,1)}), bf16[2,32,16,512]{3,2,0,1:T(8,128)(2,1)}, u32[]{:S(2)}, u32[]{:S(2)}) async-start(bf16[2,32,16,512]{3,2,0,1:T(8,128)(2,1)} %copy.68), calls=%async_computation.4 | async-start | bytes 2097152 | tf_op jit(solution)/shard_map/all_to_all | solution.py:122
  238.9 2.8 fusion.119
  241.7 3.0 fusion.118
  247.7 8.6 %collective-permute-done.9 = bf16[768,512]{1,0:T(8,128)(2,1)S(1)} collective-permute-done((bf16[768,512]{1,0:T(8,128)(2,1)}, bf16[768,512]{1,0:T(8,128)(2,1)S(1)}, u32[]{:S(2)}, u32[]{:S(2)}) %collective-permute-start.9) | collective-permute-done | bytes 786464 | tf_op jit(solution)/shard_map/ppermute | solution.py:116
  262.0 8.9 %all-to-all-start.5 = ((bf16[1,32,16,512]{3,2,0,1:T(8,128)(2,1)}), bf16[1,32,16,512]{3,2,0,1:T(8,128)(2,1)}, u32[]{:S(2)}, u32[]{:S(2)}) async-start(bf16[1,32,16,512]{3,2,0,1:T(8,128)(2,1)} %bitcast.268), calls=%async_computation.5 | async-start | bytes 1048576 | tf_op jit(solution)/shard_map/all_to_all | solution.py:122
  271.0 2.1 fusion.17
  276.6 6.1 %all-to-all-done.5 = bf16[1,32,16,512]{3,2,0,1:T(8,128)(2,1)} async-done(((bf16[1,32,16,512]{3,2,0,1:T(8,128)(2,1)}), bf16[1,32,16,512]{3,2,0,1:T(8,128)(2,1)}, u32[]{:S(2)}, u32[]{:S(2)}) %all-to-all-start.5) | async-done | bytes 524320 | tf_op jit(solution)/shard_map/all_to_all | solution.py:122
  286.8 7.7 %collective-permute-start.10 = (bf16[128,512]{1,0:T(8,128)(2,1)}, bf16[128,512]{1,0:T(8,128)(2,1)}, u32[]{:S(2)}, u32[]{:S(2)}) collective-permute-start(bf16[128,512]{1,0:T(8,128)(2,1)} %get-tuple-element.18), channel_id=1, source_target_pairs={{0,128},{128,0},{256,384},{384,256},{1,129},{129,1},{257,385},{385... | collective-permute-start | bytes 393224 | tf_op jit(solution)/shard_map/ppermute | solution.py:142
  295.8 4.2 %collective-permute-start.12 = (bf16[128,512]{1,0:T(8,128)(2,1)}, bf16[128,512]{1,0:T(8,128)(2,1)}, u32[]{:S(2)}, u32[]{:S(2)}) collective-permute-start(bf16[128,512]{1,0:T(8,128)(2,1)} %get-tuple-element.19), channel_id=1, source_target_pairs={{0,384},{128,256},{256,128},{384,0},{1,385},{129,257},{257,129},{3... | collective-permute-start | bytes 393224 | tf_op jit(solution)/shard_map/ppermute | solution.py:142
  300.1 4.8 %collective-permute-start.11 = (bf16[128,512]{1,0:T(8,128)(2,1)}, bf16[128,512]{1,0:T(8,128)(2,1)}, u32[]{:S(2)}, u32[]{:S(2)}) collective-permute-start(bf16[128,512]{1,0:T(8,128)(2,1)} %get-tuple-element.20), channel_id=1, source_target_pairs={{0,256},{128,384},{256,0},{384,128},{1,257},{129,385},{257,1},{385... | collective-permute-start | bytes 393224 | tf_op jit(solution)/shard_map/ppermute | solution.py:142
  308.0 4.8 %all-to-all-start.6 = ((f32[16,8,128]{2,1,0:T(8,128)}), f32[16,8,128]{2,1,0:T(8,128)S(1)}, u32[]{:S(2)}, u32[]{:S(2)}) async-start(f32[16,8,128]{2,1,0:T(8,128)} %bitcast.104), calls=%async_computation.6 | async-start | bytes 131072 | tf_op jit(solution)/shard_map/all_to_all | solution.py:144
  312.9 3.8 %add_bitcast_fusion = f32[1,768,512]{2,1,0:T(8,128)} fusion(f32[768,512]{1,0:T(8,128)} %fusion.119, f32[768,512]{1,0:T(8,128)S(1)} %copy-done.2, f32[768,512]{1,0:T(8,128)} %fusion.118, bf16[768,512]{1,0:T(8,128)(2,1)} %copy-done.11, bf16[512,512]{1,0:T(8,128)(2,1)S(1)} %bitcast.274), kind=kOutput, calls=%fused_computation.10 | convolution fusion | flops 403832832 | bytes 7602176 | tf_op jit(solution)/shard_map/dot_general | solution.py:148
  316.7 3.7 %all-to-all-done.6 = f32[16,8,128]{2,1,0:T(8,128)S(1)} async-done(((f32[16,8,128]{2,1,0:T(8,128)}), f32[16,8,128]{2,1,0:T(8,128)S(1)}, u32[]{:S(2)}, u32[]{:S(2)}) %all-to-all-start.6) | async-done | bytes 65568 | tf_op jit(solution)/shard_map/all_to_all | solution.py:144
  (150 shorter events, 55.0 us)
Async XLA Ops:
  7.2 172.4 %copy-start = (bf16[1,768,512]{2,1,0:T(8,128)(2,1)S(1)}, bf16[1,768,512]{2,1,0:T(8,128)(2,1)}, u32[]{:S(2)}) copy-start(bf16[1,768,512]{2,1,0:T(8,128)(2,1)} %param.13) | copy-start | bytes 2359300
  7.2 158.6 %all-gather.3.cloned.1.call-start = ((), (), s32[]{:S(2)}) async-start(), calls=%async_computation.7 | async-start | bytes 7864320 | tf_op jit(solution)/shard_map/all_gather | solution.py:45
  7.2 34.8 %collective-permute-start.3 = (bf16[128,512]{1,0:T(8,128)(2,1)}, bf16[128,512]{1,0:T(8,128)(2,1)S(1)}, u32[]{:S(2)}, u32[]{:S(2)}) collective-permute-start(bf16[128,512]{1,0:T(8,128)(2,1)} %param.7), channel_id=1, source_target_pairs={{0,384},{1,256},{2,128},{3,0},{128,385},{129,257},{130,129},{131,1... | collective-permute-start | bytes 393224 | tf_op jit(solution)/shard_map/ppermute | solution.py:49
  14.9 27.1 %collective-permute-start.2 = (bf16[128,512]{1,0:T(8,128)(2,1)}, bf16[128,512]{1,0:T(8,128)(2,1)S(1)}, u32[]{:S(2)}, u32[]{:S(2)}) collective-permute-start(bf16[128,512]{1,0:T(8,128)(2,1)} %param.7), channel_id=1, source_target_pairs={{0,256},{1,384},{2,0},{3,128},{128,257},{129,385},{130,1},{131,129... | collective-permute-start | bytes 393224 | tf_op jit(solution)/shard_map/ppermute | solution.py:49
  18.0 24.0 %collective-permute-start.1 = (bf16[128,512]{1,0:T(8,128)(2,1)}, bf16[128,512]{1,0:T(8,128)(2,1)S(1)}, u32[]{:S(2)}, u32[]{:S(2)}) collective-permute-start(bf16[128,512]{1,0:T(8,128)(2,1)} %param.7), channel_id=1, source_target_pairs={{0,128},{1,0},{2,384},{3,256},{128,129},{129,1},{130,385},{131,257... | collective-permute-start | bytes 393224 | tf_op jit(solution)/shard_map/ppermute | solution.py:49
  20.9 21.1 %collective-permute-start = (bf16[128,512]{1,0:T(8,128)(2,1)}, bf16[128,512]{1,0:T(8,128)(2,1)S(1)}, u32[]{:S(2)}, u32[]{:S(2)}) collective-permute-start(bf16[128,512]{1,0:T(8,128)(2,1)} %param.7), channel_id=1, source_target_pairs={{0,0},{1,128},{2,256},{3,384},{128,1},{129,129},{130,257},{131,385... | collective-permute-start | bytes 393224 | tf_op jit(solution)/shard_map/ppermute | solution.py:49
  28.2 13.1 %all-to-all-start = ((bf16[4,32,128]{2,1,0:T(8,128)(2,1)}), bf16[4,32,128]{2,1,0:T(8,128)(2,1)S(1)}, u32[]{:S(2)}, u32[]{:S(2)}) async-start(bf16[4,32,128]{2,1,0:T(8,128)(2,1)} %broadcast_in_dim.119), calls=%async_computation | async-start | bytes 65536 | tf_op jit(solution)/shard_map/all_to_all | solution.py:38
  34.2 36.2 %copy-start.30 = (f32[32]{0:T(128)}, f32[32]{0:T(128)S(1)}, u32[]{:S(2)}) copy-start(f32[32]{0:T(128)S(1)} %iota_add_fusion) | copy-start | bytes 388
  41.5 28.9 %copy-start.19 = (f32[4,128]{1,0:T(4,128)}, f32[4,128]{1,0:T(4,128)S(1)}, u32[]{:S(2)}) copy-start(f32[4,128]{1,0:T(4,128)S(1)} %get-tuple-element.68) | copy-start | bytes 6148
  41.5 28.9 %copy-start.21 = (f32[4,128]{1,0:T(4,128)}, f32[4,128]{1,0:T(4,128)S(1)}, u32[]{:S(2)}) copy-start(f32[4,128]{1,0:T(4,128)S(1)} %get-tuple-element.69) | copy-start | bytes 6148
  41.5 28.9 %copy-start.23 = (f32[4,128]{1,0:T(4,128)}, f32[4,128]{1,0:T(4,128)S(1)}, u32[]{:S(2)}) copy-start(f32[4,128]{1,0:T(4,128)S(1)} %get-tuple-element.70) | copy-start | bytes 6148
  41.5 28.9 %copy-start.25 = (f32[4,128]{1,0:T(4,128)}, f32[4,128]{1,0:T(4,128)S(1)}, u32[]{:S(2)}) copy-start(f32[4,128]{1,0:T(4,128)S(1)} %get-tuple-element.71) | copy-start | bytes 6148
  44.9 61.8 %all-to-all-start.1 = ((bf16[32,16,2048]{2,1,0:T(8,128)(2,1)}), bf16[32,16,2048]{2,1,0:T(8,128)(2,1)S(1)}, u32[]{:S(2)}, u32[]{:S(2)}) async-start(bf16[32,16,2048]{2,1,0:T(8,128)(2,1)} %bitcast.38), calls=%async_computation.1 | async-start | bytes 4194304 | tf_op jit(solution)/shard_map/all_to_all | solution.py:93
  57.9 15.4 %collective-permute-start.6 = (bf16[128,512]{1,0:T(8,128)(2,1)S(1)}, bf16[128,512]{1,0:T(8,128)(2,1)}, u32[]{:S(2)}, u32[]{:S(2)}) collective-permute-start(bf16[128,512]{1,0:T(8,128)(2,1)S(1)} %copy-done.15), channel_id=1, source_target_pairs={{0,384},{128,256},{256,128},{384,0},{1,385},{129,257},{257,129},{3... | collective-permute-start | bytes 393224 | tf_op jit(solution)/shard_map/ppermute | solution.py:61
  60.4 20.4 %collective-permute-start.5 = (bf16[128,512]{1,0:T(8,128)(2,1)S(1)}, bf16[128,512]{1,0:T(8,128)(2,1)}, u32[]{:S(2)}, u32[]{:S(2)}) collective-permute-start(bf16[128,512]{1,0:T(8,128)(2,1)S(1)} %copy-done.15), channel_id=1, source_target_pairs={{0,256},{128,384},{256,0},{384,128},{1,257},{129,385},{257,1},{385... | collective-permute-start | bytes 393224 | tf_op jit(solution)/shard_map/ppermute | solution.py:61
  68.1 12.7 %collective-permute-start.4 = (bf16[128,512]{1,0:T(8,128)(2,1)S(1)}, bf16[128,512]{1,0:T(8,128)(2,1)}, u32[]{:S(2)}, u32[]{:S(2)}) collective-permute-start(bf16[128,512]{1,0:T(8,128)(2,1)S(1)} %copy-done.15), channel_id=1, source_target_pairs={{0,128},{128,0},{256,384},{384,256},{1,129},{129,1},{257,385},{385... | collective-permute-start | bytes 393224 | tf_op jit(solution)/shard_map/ppermute | solution.py:61
  82.7 27.2 %copy-start.12 = (bf16[1,128,512]{2,1,0:T(8,128)(2,1)}, bf16[1,128,512]{2,1,0:T(8,128)(2,1)S(1)}, u32[]{:S(2)}) copy-start(bf16[1,128,512]{2,1,0:T(8,128)(2,1)S(1)} %get-tuple-element.24) | copy-start | bytes 393220
  174.2 38.1 %collective-permute-start.8 = (bf16[768,512]{1,0:T(8,128)(2,1)}, bf16[768,512]{1,0:T(8,128)(2,1)}, u32[]{:S(2)}, u32[]{:S(2)}) collective-permute-start(bf16[768,512]{1,0:T(8,128)(2,1)} %fusion), channel_id=1, source_target_pairs={{0,2},{1,3},{2,0},{3,1},{4,6},{5,7},{6,4},{7,5},{8,10},{9,11},{10,... | collective-permute-start | bytes 2359304 | tf_op jit(solution)/shard_map/ppermute | solution.py:110
  177.0 37.0 %collective-permute-start.7 = (bf16[768,512]{1,0:T(8,128)(2,1)}, bf16[768,512]{1,0:T(8,128)(2,1)}, u32[]{:S(2)}, u32[]{:S(2)}) collective-permute-start(bf16[768,512]{1,0:T(8,128)(2,1)} %fusion), channel_id=1, source_target_pairs={{0,1},{1,0},{2,3},{3,2},{4,5},{5,4},{6,7},{7,6},{8,9},{9,8},{10,11... | collective-permute-start | bytes 2359304 | tf_op jit(solution)/shard_map/ppermute | solution.py:109
  181.1 35.8 %all-to-all-start.3 = ((bf16[1,32,16,512]{3,2,0,1:T(8,128)(2,1)}), bf16[1,32,16,512]{3,2,0,1:T(8,128)(2,1)S(1)}, u32[]{:S(2)}, u32[]{:S(2)}) async-start(bf16[1,32,16,512]{3,2,0,1:T(8,128)(2,1)} %bitcast.269), calls=%async_computation.3 | async-start | bytes 1048576 | tf_op jit(solution)/shard_map/all_to_all | solution.py:122
  220.6 38.0 %all-to-all-start.4 = ((bf16[2,32,16,512]{3,2,0,1:T(8,128)(2,1)}), bf16[2,32,16,512]{3,2,0,1:T(8,128)(2,1)}, u32[]{:S(2)}, u32[]{:S(2)}) async-start(bf16[2,32,16,512]{3,2,0,1:T(8,128)(2,1)} %copy.68), calls=%async_computation.4 | async-start | bytes 2097152 | tf_op jit(solution)/shard_map/all_to_all | solution.py:122
  236.8 19.5 %collective-permute-start.9 = (bf16[768,512]{1,0:T(8,128)(2,1)}, bf16[768,512]{1,0:T(8,128)(2,1)S(1)}, u32[]{:S(2)}, u32[]{:S(2)}) collective-permute-start(bf16[768,512]{1,0:T(8,128)(2,1)} %collective-permute-done.8), channel_id=1, source_target_pairs={{0,1},{1,0},{2,3},{3,2},{4,5},{5,4},{6,7},{7,6},{8,9},{9,8},{10,11... | collective-permute-start | bytes 2359304 | tf_op jit(solution)/shard_map/ppermute | solution.py:116
  262.0 20.7 %all-to-all-start.5 = ((bf16[1,32,16,512]{3,2,0,1:T(8,128)(2,1)}), bf16[1,32,16,512]{3,2,0,1:T(8,128)(2,1)}, u32[]{:S(2)}, u32[]{:S(2)}) async-start(bf16[1,32,16,512]{3,2,0,1:T(8,128)(2,1)} %bitcast.268), calls=%async_computation.5 | async-start | bytes 1048576 | tf_op jit(solution)/shard_map/all_to_all | solution.py:122
  284.3 20.6 %copy-start.16 = (bf16[1,128,512]{2,1,0:T(8,128)(2,1)S(1)}, bf16[1,128,512]{2,1,0:T(8,128)(2,1)}, u32[]{:S(2)}) copy-start(bf16[1,128,512]{2,1,0:T(8,128)(2,1)} %get-tuple-element.22) | copy-start | bytes 393220
  285.9 20.6 %copy-start.18 = (f32[2,32,128]{2,1,0:T(8,128)S(1)}, f32[2,32,128]{2,1,0:T(8,128)}, u32[]{:S(2)}) copy-start(f32[2,32,128]{2,1,0:T(8,128)} %fusion.45) | copy-start | bytes 98308
  285.9 20.6 %copy-start.20 = (f32[4,128]{1,0:T(4,128)S(1)}, f32[4,128]{1,0:T(4,128)}, u32[]{:S(2)}) copy-start(f32[4,128]{1,0:T(4,128)} %copy-done.19) | copy-start | bytes 6148
  285.9 26.9 %copy-start.2 = (f32[768,512]{1,0:T(8,128)S(1)}, f32[768,512]{1,0:T(8,128)}, u32[]{:S(2)}) copy-start(f32[768,512]{1,0:T(8,128)} %fusion.117) | copy-start | bytes 4718596
  286.0 26.9 %copy-start.7 = (bf16[1,32,16,512]{3,2,0,1:T(8,128)(2,1)S(1)}, bf16[1,32,16,512]{3,2,0,1:T(8,128)(2,1)}, u32[]{:S(2)}) copy-start(bf16[1,32,16,512]{3,2,0,1:T(8,128)(2,1)} %get-tuple-element.14) | copy-start | bytes 1572868
  286.8 34.3 %collective-permute-start.10 = (bf16[128,512]{1,0:T(8,128)(2,1)}, bf16[128,512]{1,0:T(8,128)(2,1)}, u32[]{:S(2)}, u32[]{:S(2)}) collective-permute-start(bf16[128,512]{1,0:T(8,128)(2,1)} %get-tuple-element.18), channel_id=1, source_target_pairs={{0,128},{128,0},{256,384},{384,256},{1,129},{129,1},{257,385},{385... | collective-permute-start | bytes 393224 | tf_op jit(solution)/shard_map/ppermute | solution.py:142
  295.8 25.2 %collective-permute-start.12 = (bf16[128,512]{1,0:T(8,128)(2,1)}, bf16[128,512]{1,0:T(8,128)(2,1)}, u32[]{:S(2)}, u32[]{:S(2)}) collective-permute-start(bf16[128,512]{1,0:T(8,128)(2,1)} %get-tuple-element.19), channel_id=1, source_target_pairs={{0,384},{128,256},{256,128},{384,0},{1,385},{129,257},{257,129},{3... | collective-permute-start | bytes 393224 | tf_op jit(solution)/shard_map/ppermute | solution.py:142
  300.1 21.0 %collective-permute-start.11 = (bf16[128,512]{1,0:T(8,128)(2,1)}, bf16[128,512]{1,0:T(8,128)(2,1)}, u32[]{:S(2)}, u32[]{:S(2)}) collective-permute-start(bf16[128,512]{1,0:T(8,128)(2,1)} %get-tuple-element.20), channel_id=1, source_target_pairs={{0,256},{128,384},{256,0},{384,128},{1,257},{129,385},{257,1},{385... | collective-permute-start | bytes 393224 | tf_op jit(solution)/shard_map/ppermute | solution.py:142
  308.0 12.4 %all-to-all-start.6 = ((f32[16,8,128]{2,1,0:T(8,128)}), f32[16,8,128]{2,1,0:T(8,128)S(1)}, u32[]{:S(2)}, u32[]{:S(2)}) async-start(f32[16,8,128]{2,1,0:T(8,128)} %bitcast.104), calls=%async_computation.6 | async-start | bytes 131072 | tf_op jit(solution)/shard_map/all_to_all | solution.py:144
  (20 other events, 159.9 us)
Sparse Core Ops, SparseCore 0:
  27.1 135.9 all-gather.2

commit v6 on v5

--- a/solution.py
+++ b/solution.py
@@ -1,6 +1,8 @@
 import jax
 import jax.numpy as jnp
 from jax import lax
+from jax.experimental import pallas as pl
+from jax.experimental.pallas import tpu as pltpu
 from jax.sharding import PartitionSpec as P
 
 SLOTS = 16
@@ -17,6 +19,34 @@
 
 def after(x, earlier):
     return x + (earlier[(0,) * earlier.ndim].astype(jnp.float32) * 0.0).astype(x.dtype)
+
+
+def expert_out(hidden_of, w_down, dev):
+    count = len(hidden_of)
+    hidden, feats = w_down.shape
+    rows = hidden_of[0].shape[1]
+
+    def kernel(*refs):
+        w_ref, out_ref = refs[count], refs[-1]
+        for c in range(count):
+            rows_out = lax.dot_general(
+                refs[c][...], w_ref[...], (((0,), (0,)), ((), ())), preferred_element_type=jnp.float32
+            )
+            out_ref[:, c] = rows_out.astype(jnp.bfloat16).reshape(dev, rows // dev, feats)
+
+    vmem = pl.BlockSpec(memory_space=pltpu.VMEM)
+    return pl.pallas_call(
+        kernel,
+        out_shape=jax.ShapeDtypeStruct((dev, count, rows // dev, feats), jnp.bfloat16),
+        in_specs=[vmem] * (count + 1),
+        out_specs=vmem,
+        cost_estimate=pl.CostEstimate(
+            flops=(1 if count == 1 else 32) * 2 * count * rows * hidden * feats,
+            bytes_accessed=2 * (count * rows * (hidden + feats) + hidden * feats),
+            transcendentals=0,
+        ),
+        compiler_params=pltpu.CompilerParams(vmem_limit_bytes=32 * 1024 * 1024),
+    )(*hidden_of, w_down)
 
 
 def per_device(tokens, upstream, expert_ids, gate_probs, w_gate, w_up, w_down):
@@ -33,10 +63,6 @@
     def flipped(size, bits):
         return [(i, i ^ bits) for i in range(size)]
 
-    def spread(x):
-        x = jnp.broadcast_to(x[None], (grp,) + x.shape)
-        return lax.all_to_all(x, "grp", split_axis=0, concat_axis=0, tiled=True)
-
     def relative(x):
         parts = [lax.dynamic_index_in_dim(x, split_me ^ j, 0, keepdims=True) for j in range(grp)]
         return jnp.concatenate(parts, axis=0)
@@ -44,52 +70,59 @@
     w_own = jnp.concatenate([w_gate[0].T, w_up[0].T], axis=0)
     w_all = lax.all_gather(w_own, "split", axis=0, tiled=False)
 
+    meta = jnp.concatenate([expert_ids.T.astype(bf16)] + bf16_pieces(gate_probs.T, 3), axis=0)
+    meta = meta.reshape(-1, feats)
+    meta_rows = meta.shape[0]
+    meta = jnp.pad(meta, ((0, SLOTS - meta_rows), (0, 0)))
+    token_rows = jnp.concatenate([tokens, meta], axis=0)
+    upstream_rows = jnp.concatenate([upstream, meta], axis=0)
+
     pieces = jnp.stack(
         [
             lax.ppermute(
-                tokens,
+                token_rows,
                 ("grp", "split"),
                 [(g * split + f, (f ^ m) * split + g) for g in range(grp) for f in range(split)],
             )
             for m in range(split)
         ]
     )
-
-    meta = jnp.concatenate([expert_ids.T.astype(bf16)] + bf16_pieces(gate_probs.T, 3), axis=0)
-    near = spread(meta)
-    near_upstream = jnp.stack(
-        [upstream] + [lax.ppermute(upstream, "grp", flipped(grp, m)) for m in range(1, grp)]
-    )
-    near_upstream = jnp.stack(
-        [
-            lax.dynamic_index_in_dim(near_upstream, grp_me ^ split_me ^ j, 0, keepdims=False)
-            for j in range(grp)
-        ]
-    )
-
-    near_meta = relative(near.astype(f32).reshape(grp, 4, top, rows))
-    near_ids = near_meta[:, 0]
-    near_gates = near_meta[:, 1] + near_meta[:, 2] + near_meta[:, 3]
-
-    mine = jnp.stack([lax.dynamic_index_in_dim(pieces, grp_me ^ f, 0, keepdims=False) for f in range(split)])
-    mine = jnp.concatenate([mine[f] for f in range(split)], axis=1)
+    mine = [lax.dynamic_index_in_dim(pieces[:, :rows], grp_me ^ f, 0, keepdims=False) for f in range(split)]
+    mine = jnp.concatenate(mine, axis=1)
+
+    near = jnp.stack(
+        [upstream_rows] + [lax.ppermute(upstream_rows, "grp", flipped(grp, m)) for m in range(1, grp)]
+    )
+    near = jnp.stack(
+        [lax.dynamic_index_in_dim(near, grp_me ^ split_me ^ j, 0, keepdims=False) for j in range(grp)]
+    )
+    near_upstream = near[:, :rows]
 
     expert = (grp_me * dev).astype(f32) + lax.broadcasted_iota(f32, (1, dev, 1), 1)
-    equal = [near_ids[:, k][:, None, :] == expert for k in range(top)]
-    member = sum(e.astype(f32) for e in equal)
-    gate_of = sum(jnp.where(e, near_gates[:, k][:, None, :], 0.0) for k, e in enumerate(equal))
     before = (
         lax.broadcasted_iota(jnp.int32, (rows, rows), 0) < lax.broadcasted_iota(jnp.int32, (rows, rows), 1)
     ).astype(bf16)
-    place = jnp.dot(member.astype(bf16).reshape(grp * dev, rows), before, preferred_element_type=f32)
-    place = jnp.where(member > 0, place.reshape(grp, dev, rows), -1.0)
     slot = lax.broadcasted_iota(f32, (1, 1, SLOTS, 1), 2)
-    chosen = place[:, :, None, :] == slot
+
+    def route(meta):
+        count = meta.shape[0]
+        meta = meta.astype(f32).reshape(count, 4, top, rows)
+        equal = [meta[:, 0, k][:, None, :] == expert for k in range(top)]
+        member = sum(e.astype(f32) for e in equal)
+        place = jnp.dot(member.astype(bf16).reshape(count * dev, rows), before, preferred_element_type=f32)
+        place = jnp.where(member > 0, place.reshape(count, dev, rows), -1.0)
+        gates = meta[:, 1] + meta[:, 2] + meta[:, 3]
+        return equal, gates, place[:, :, None, :] == slot
+
+    _, _, chosen_mine = route(pieces[:1, rows : rows + meta_rows])
+    equal, near_gates, chosen = route(near[:, rows : rows + meta_rows])
+    gate_of = sum(jnp.where(e, near_gates[:, k][:, None, :], 0.0) for k, e in enumerate(equal))
     pick = chosen.astype(bf16).reshape(grp, dev * SLOTS, rows)
     weight = jnp.where(chosen, gate_of[:, :, None, :], 0.0).reshape(grp, dev * SLOTS, rows)
     gate_row = jnp.sum(weight, axis=2, keepdims=True)
 
-    send = jnp.dot(pick[0], mine, preferred_element_type=f32).astype(bf16)
+    pick_mine = chosen_mine.astype(bf16).reshape(dev * SLOTS, rows)
+    send = jnp.dot(pick_mine, mine, preferred_element_type=f32).astype(bf16)
     arrived = lax.all_to_all(
         send.reshape(dev, SLOTS, split * feats), "dev", split_axis=0, concat_axis=0, tiled=True
     ).reshape(dev * SLOTS, split * feats)
@@ -114,21 +147,16 @@
         count = part_of.stop - part_of.start
         if part_of.start == 1:
             hidden_of.append(lax.ppermute(hidden_of[2], "split", flipped(split, 1)))
-        out = [
-            lax.dot_general(h, w_down[0], (((0,), (0,)), ((), ())), preferred_element_type=f32).astype(bf16)
-            for h in hidden_of[part_of]
-        ]
-        out = after(lax.optimization_barrier(jnp.stack(out)), returned)
-        returned = lax.all_to_all(
-            out.reshape(count, dev, SLOTS, feats), "dev", split_axis=1, concat_axis=1, tiled=True
-        ).reshape(count, dev * SLOTS, feats)
+        out = after(expert_out(hidden_of[part_of], w_down[0], dev), returned)
+        returned = lax.all_to_all(out, "dev", split_axis=0, concat_axis=0, tiled=True)
+        sent = jnp.swapaxes(returned, 0, 1).reshape(count, dev * SLOTS, feats)
         mixed.append(
             sum(
-                jnp.einsum("grt,grd->gtd", piece, returned, preferred_element_type=f32)
+                jnp.einsum("grt,grd->gtd", piece, sent, preferred_element_type=f32)
                 for piece in bf16_pieces(weight[part_of], 2)
             ).astype(bf16)
         )
-        part = jnp.einsum("grd,gtd->grt", returned, near_upstream[part_of], preferred_element_type=f32)
+        part = jnp.einsum("grd,gtd->grt", sent, near_upstream[part_of], preferred_element_type=f32)
         dots.append(jnp.where(chosen[part_of], part.reshape(count, dev, SLOTS, rows), 0.0).sum(axis=2))
     mixed = jnp.concatenate(mixed, axis=0)
     dots = jnp.concatenate(dots, axis=0)

time: 331 us -> 318 us (0.961)
  blocking collectives: 54.2 us -> 0 us
  starting transfers between devices: 104 us -> 129 us
  waiting for transfers between devices: 81.4 us -> 104 us
  matrix products: 39.5 us -> 28.8 us
    all_to_all x1 -> x0, blocking collectives: 54.2 us -> none  [per_device(): lax.all_to_all(scaled, 'dev', split_axis=1, concat_axis=1, tiled=True)]
    all_gather x1, waiting for transfers between devices: 0.02 us -> 46.1 us  [per_device(): w_all = lax.all_gather(w_own, 'split', axis=0, tiled=False)]
    all_to_all x1, waiting for transfers between devices: 24 us -> 2.59 us  [per_device(): lax.all_to_all(send.reshape(dev, SLOTS, split * feats), 'dev', split_axis...]
    all_to_all x4, waiting for transfers between devices: 13.3 us -> 4.05 us  [the longest x3 4.05 us: per_device(): lax.all_to_all(out, 'dev', split_axis=0, concat_axis=0, tiled=True)]
    all_to_all x4, starting transfers between devices: 32.3 us -> 41.3 us  [the longest x3 30.6 us: per_device(): lax.all_to_all(out, 'dev', split_axis=0, concat_axis=0, tiled=True)]
    ppermute x7, waiting for transfers between devices: 9 us -> 17.9 us  [the longest x3 9.5 us: per_device(): lax.ppermute(upstream_rows, 'grp', flipped(grp, m))]
    ppermute x7, starting transfers between devices: 29.1 us -> 37.7 us  [the longest x3 21.4 us: per_device(): lax.ppermute(upstream_rows, 'grp', flipped(grp, m))]
    ppermute x1, waiting for transfers between devices: 22.8 us -> 15.5 us  [per_device(): hidden_of.append(lax.ppermute(hidden, 'split', flipped(split, 2)))]
  transfers between devices with their start and end apart: 20 -> 20, of which waited for: 8 -> 10; matrix products, arithmetic and copies ran while one was open for 15% -> 15% of each run, Pallas kernels for 0% -> 1%
where the time goes in v6:
time: 318 us; the launch traced here: 316 us
  starting transfers between devices  129 us (41%)
  waiting for transfers between devices  104 us (33%)
  matrix products  28.8 us (9%)
  local copies, waits for them, and re-layouts  18.6 us (6%)
  between operations  18.5 us (6%)
  other arithmetic  14.6 us (5%)
    all_gather x1, waiting for transfers between devices, per_device(): w_all = lax.all_gather(w_own, 'split', axis=0, tiled=False)  46.1 us
    all_to_all x3, starting transfers between devices, per_device(): lax.all_to_all(out, 'dev', split_axis=0, concat_axis=0, tiled=True)  30.6 us
    ppermute x3, starting transfers between devices, per_device(): lax.ppermute(upstream_rows, 'grp', flipped(grp, m))  21.4 us
    ppermute x3, starting transfers between devices, per_device(): lax.ppermute(own_mixed[m], 'grp', flipped(grp, m)).astype(f32)  17.2 us
    ppermute x4, starting transfers between devices, per_device(): lax.ppermute(token_rows, ('grp', 'split'), [(g * split + f, (f ^ m) * spl...  16.3 us
    ppermute x1, waiting for transfers between devices, per_device(): hidden_of.append(lax.ppermute(hidden, 'split', flipped(split, 2)))  15.5 us
    all_to_all x1, starting transfers between devices, per_device(): lax.all_to_all(send.reshape(dev, SLOTS, split * feats), 'dev', split_axis...  14.9 us
    ppermute x1, waiting for transfers between devices, per_device(): hidden_of.append(lax.ppermute(hidden_of[2], 'split', flipped(split, 1)))  11.8 us
  transfers between devices with their start and end apart: 20, of which 10 were waited for; matrix products, arithmetic and copies ran while one was open for 15% of the time, Pallas kernels for 1%

profile of v6, /device:TPU:1, one launch (start us, length us, event | category | flops | bytes accessed | tf_op | source)
XLA Modules:
  0.0 316.4 jit_solution(10165294792477157466)
XLA Ops:
  7.2 2.7 pad_maximum_fusion
  10.9 4.6 %collective-permute-start.3 = (bf16[144,512]{1,0:T(8,128)(2,1)S(1)}, bf16[144,512]{1,0:T(8,128)(2,1)S(1)}, u32[]{:S(2)}, u32[]{:S(2)}) collective-permute-start(bf16[144,512]{1,0:T(8,128)(2,1)S(1)} %get-tuple-element.72), channel_id=1, source_target_pairs={{0,0},{1,128},{2,256},{3,384},{128,1},{129,129},{130,257},{131,385... | collective-permute-start | bytes 442376 | tf_op jit(solution)/shard_map/ppermute | solution.py:82
  15.5 5.8 %collective-permute-start.6 = (bf16[144,512]{1,0:T(8,128)(2,1)S(1)}, bf16[144,512]{1,0:T(8,128)(2,1)S(1)}, u32[]{:S(2)}, u32[]{:S(2)}) collective-permute-start(bf16[144,512]{1,0:T(8,128)(2,1)S(1)} %get-tuple-element.72), channel_id=1, source_target_pairs={{0,384},{1,256},{2,128},{3,0},{128,385},{129,257},{130,129},{131,1... | collective-permute-start | bytes 442376 | tf_op jit(solution)/shard_map/ppermute | solution.py:82
  21.3 2.1 collective-permute-start.5
  23.4 3.8 %collective-permute-start.4 = (bf16[144,512]{1,0:T(8,128)(2,1)S(1)}, bf16[144,512]{1,0:T(8,128)(2,1)S(1)}, u32[]{:S(2)}, u32[]{:S(2)}) collective-permute-start(bf16[144,512]{1,0:T(8,128)(2,1)S(1)} %get-tuple-element.72), channel_id=1, source_target_pairs={{0,128},{1,0},{2,384},{3,256},{128,129},{129,1},{130,385},{131,257... | collective-permute-start | bytes 442376 | tf_op jit(solution)/shard_map/ppermute | solution.py:82
  27.8 4.7 %collective-permute-done.6 = bf16[144,512]{1,0:T(8,128)(2,1)S(1)} collective-permute-done((bf16[144,512]{1,0:T(8,128)(2,1)S(1)}, bf16[144,512]{1,0:T(8,128)(2,1)S(1)}, u32[]{:S(2)}, u32[]{:S(2)}) %collective-permute-start.6) | collective-permute-done | bytes 147488 | tf_op jit(solution)/shard_map/ppermute | solution.py:82
  32.5 3.7 %collective-permute-done.4 = bf16[144,512]{1,0:T(8,128)(2,1)S(1)} collective-permute-done((bf16[144,512]{1,0:T(8,128)(2,1)S(1)}, bf16[144,512]{1,0:T(8,128)(2,1)S(1)}, u32[]{:S(2)}, u32[]{:S(2)}) %collective-permute-start.4) | collective-permute-done | bytes 147488 | tf_op jit(solution)/shard_map/ppermute | solution.py:82
  36.2 2.1 convolution_convert_fusion
  38.3 14.9 %all-to-all-start = ((bf16[32,16,2048]{2,1,0:T(8,128)(2,1)}), bf16[32,16,2048]{2,1,0:T(8,128)(2,1)S(1)}, u32[]{:S(2)}, u32[]{:S(2)}) async-start(bf16[32,16,2048]{2,1,0:T(8,128)(2,1)} %bitcast.47), calls=%async_computation | async-start | bytes 4194304 | tf_op jit(solution)/shard_map/all_to_all | solution.py:126
  53.2 8.3 %collective-permute-start.2 = (bf16[144,512]{1,0:T(8,128)(2,1)S(1)}, bf16[144,512]{1,0:T(8,128)(2,1)S(1)}, u32[]{:S(2)}, u32[]{:S(2)}) collective-permute-start(bf16[144,512]{1,0:T(8,128)(2,1)S(1)} %get-tuple-element.34), channel_id=1, source_target_pairs={{0,384},{128,256},{256,128},{384,0},{1,385},{129,257},{257,129},{3... | collective-permute-start | bytes 442376 | tf_op jit(solution)/shard_map/ppermute | solution.py:94
  61.5 11.2 %collective-permute-start.1 = (bf16[144,512]{1,0:T(8,128)(2,1)S(1)}, bf16[144,512]{1,0:T(8,128)(2,1)S(1)}, u32[]{:S(2)}, u32[]{:S(2)}) collective-permute-start(bf16[144,512]{1,0:T(8,128)(2,1)S(1)} %get-tuple-element.34), channel_id=1, source_target_pairs={{0,256},{128,384},{256,0},{384,128},{1,257},{129,385},{257,1},{385... | collective-permute-start | bytes 442376 | tf_op jit(solution)/shard_map/ppermute | solution.py:94
  74.7 9.5 %collective-permute-done.1 = bf16[144,512]{1,0:T(8,128)(2,1)S(1)} collective-permute-done((bf16[144,512]{1,0:T(8,128)(2,1)S(1)}, bf16[144,512]{1,0:T(8,128)(2,1)S(1)}, u32[]{:S(2)}, u32[]{:S(2)}) %collective-permute-start.1) | collective-permute-done | bytes 147488 | tf_op jit(solution)/shard_map/ppermute | solution.py:94
  87.1 2.6 all-to-all-done
  93.4 10.6 %all-to-all-start.1 = ((bf16[4,32,16,512]{3,2,0,1:T(8,128)(2,1)}), bf16[4,32,16,512]{3,2,0,1:T(8,128)(2,1)}, u32[]{:S(2)}, u32[]{:S(2)}) async-start(bf16[4,32,16,512]{3,2,0,1:T(8,128)(2,1)} %copy.82), calls=%async_computation.1 | async-start | bytes 4194304 | tf_op jit(solution)/shard_map/all_to_all | solution.py:131
  104.1 46.1 %all-gather.3.cloned.1.call-done = bf16[1536,2048]{1,0:T(8,128)(2,1)} async-done(((bf16[384,2048]{1,0:T(8,128)(2,1)}), bf16[1536,2048]{1,0:T(8,128)(2,1)}) %all-gather.3.cloned.1.call-update) | async-done | bytes 6291472 | tf_op jit(solution)/shard_map/all_gather | solution.py:71
  150.2 5.6 %fusion.98 = f32[4,2,192,512]{3,2,1,0:T(8,128)S(1)} fusion(bf16[4,2,192,2048]{3,2,1,0:T(8,128)(2,1)} %bitcast.288, bf16[512,2048,1,1]{1,0,3,2:T(8,128)(2,1)S(1)} %bitcast.231), kind=kOutput, calls=%fused_computation.207 | convolution fusion | flops 3221225472 | bytes 11534336 | tf_op jit(solution)/shard_map/dot_general | solution.py:134
  157.9 6.6 %collective-permute-start.8 = (bf16[768,512]{1,0:T(8,128)(2,1)S(1)}, bf16[768,512]{1,0:T(8,128)(2,1)S(1)}, u32[]{:S(2)}, u32[]{:S(2)}) collective-permute-start(bf16[768,512]{1,0:T(8,128)(2,1)S(1)} %fusion.refs_0_), channel_id=1, source_target_pairs={{0,2},{1,3},{2,0},{3,1},{4,6},{5,7},{6,4},{7,5},{8,10},{9,11},{10,... | collective-permute-start | bytes 2359304 | tf_op jit(solution)/shard_map/ppermute | solution.py:143
  170.8 12.3 %all-to-all-start.2 = ((bf16[32,1,16,512]{3,2,1,0:T(8,128)(2,1)}), bf16[32,1,16,512]{3,2,1,0:T(8,128)(2,1)}, u32[]{:S(2)}, u32[]{:S(2)}) async-start(bf16[32,1,16,512]{3,2,1,0:T(8,128)(2,1)} %broadcast_add_fusion.2), calls=%async_computation.2 | async-start | bytes 1048576 | tf_op jit(solution)/shard_map/all_to_all | solution.py:151
  183.1 15.5 %collective-permute-done.8.refs_1_ = bf16[768,512]{1,0:T(8,128)(2,1)S(1)} collective-permute-done((bf16[768,512]{1,0:T(8,128)(2,1)S(1)}, bf16[768,512]{1,0:T(8,128)(2,1)S(1)}, u32[]{:S(2)}, u32[]{:S(2)}) %collective-permute-start.8) | collective-permute-done | bytes 786464 | tf_op jit(solution)/shard_map/ppermute | solution.py:143
  198.6 2.7 collective-permute-done.7.refs_0_
  207.3 9.6 %all-to-all-start.3 = ((bf16[32,2,16,512]{3,2,1,0:T(8,128)(2,1)}), bf16[32,2,16,512]{3,2,1,0:T(8,128)(2,1)}, u32[]{:S(2)}, u32[]{:S(2)}) async-start(bf16[32,2,16,512]{3,2,1,0:T(8,128)(2,1)} %broadcast_add_fusion), calls=%async_computation.3 | async-start | bytes 2097152 | tf_op jit(solution)/shard_map/all_to_all | solution.py:151
  220.4 2.6 fusion.95
  224.8 2.2 collective-permute-start.9
  232.5 11.8 %collective-permute-done.9.refs_0_ = bf16[768,512]{1,0:T(8,128)(2,1)S(1)} collective-permute-done((bf16[768,512]{1,0:T(8,128)(2,1)S(1)}, bf16[768,512]{1,0:T(8,128)(2,1)S(1)}, u32[]{:S(2)}, u32[]{:S(2)}) %collective-permute-start.9) | collective-permute-done | bytes 786464 | tf_op jit(solution)/shard_map/ppermute | solution.py:149
  247.7 8.8 %all-to-all-start.4 = ((bf16[32,1,16,512]{3,2,1,0:T(8,128)(2,1)}), bf16[32,1,16,512]{3,2,1,0:T(8,128)(2,1)S(1)}, u32[]{:S(2)}, u32[]{:S(2)}) async-start(bf16[32,1,16,512]{3,2,1,0:T(8,128)(2,1)} %broadcast_add_fusion.1), calls=%async_computation.4 | async-start | bytes 1048576 | tf_op jit(solution)/shard_map/all_to_all | solution.py:151
  264.2 4.0 %all-to-all-done.4 = bf16[32,1,16,512]{3,2,1,0:T(8,128)(2,1)S(1)} async-done(((bf16[32,1,16,512]{3,2,1,0:T(8,128)(2,1)}), bf16[32,1,16,512]{3,2,1,0:T(8,128)(2,1)S(1)}, u32[]{:S(2)}, u32[]{:S(2)}) %all-to-all-start.4) | async-done | bytes 524320 | tf_op jit(solution)/shard_map/all_to_all | solution.py:151
  270.7 7.7 %collective-permute-start.10 = (bf16[128,512]{1,0:T(8,128)(2,1)}, bf16[128,512]{1,0:T(8,128)(2,1)S(1)}, u32[]{:S(2)}, u32[]{:S(2)}) collective-permute-start(bf16[128,512]{1,0:T(8,128)(2,1)} %get-tuple-element.26), channel_id=1, source_target_pairs={{0,128},{128,0},{256,384},{384,256},{1,129},{129,1},{257,385},{385... | collective-permute-start | bytes 393224 | tf_op jit(solution)/shard_map/ppermute | solution.py:170
  279.7 7.4 %collective-permute-start.12 = (bf16[128,512]{1,0:T(8,128)(2,1)}, bf16[128,512]{1,0:T(8,128)(2,1)}, u32[]{:S(2)}, u32[]{:S(2)}) collective-permute-start(bf16[128,512]{1,0:T(8,128)(2,1)} %get-tuple-element.27), channel_id=1, source_target_pairs={{0,384},{128,256},{256,128},{384,0},{1,385},{129,257},{257,129},{3... | collective-permute-start | bytes 393224 | tf_op jit(solution)/shard_map/ppermute | solution.py:170
  287.1 2.0 collective-permute-start.11
  292.1 7.6 %all-to-all-start.5 = ((f32[16,8,128]{2,1,0:T(8,128)}), f32[16,8,128]{2,1,0:T(8,128)S(1)}, u32[]{:S(2)}, u32[]{:S(2)}) async-start(f32[16,8,128]{2,1,0:T(8,128)} %bitcast.95), calls=%async_computation.5 | async-start | bytes 131072 | tf_op jit(solution)/shard_map/all_to_all | solution.py:172
  299.7 3.8 %add_bitcast_fusion = f32[1,768,512]{2,1,0:T(8,128)} fusion(f32[768,512]{1,0:T(8,128)} %fusion.103, f32[768,512]{1,0:T(8,128)S(1)} %copy-done.4, f32[768,512]{1,0:T(8,128)} %fusion.102, bf16[768,512]{1,0:T(8,128)(2,1)S(1)} %collective-permute-done.9.refs_0_, bf16[512,512]{1,0:T(8,128)(2,1)} %bitcast.238), kind=kOutput, calls=%fused_computation.10 | convolution fusion | flops 403832832 | bytes 7602176 | tf_op jit(solution)/shard_map/dot_general | solution.py:176
  303.4 3.8 %all-to-all-done.5 = f32[16,8,128]{2,1,0:T(8,128)S(1)} async-done(((f32[16,8,128]{2,1,0:T(8,128)}), f32[16,8,128]{2,1,0:T(8,128)S(1)}, u32[]{:S(2)}, u32[]{:S(2)}) %all-to-all-start.5) | async-done | bytes 65568 | tf_op jit(solution)/shard_map/all_to_all | solution.py:172
  (169 shorter events, 51.5 us)
Async XLA Ops:
  7.2 143.0 %all-gather.3.cloned.1.call-start = ((), (), s32[]{:S(2)}) async-start(), calls=%async_computation.6 | async-start | bytes 7864320 | tf_op jit(solution)/shard_map/all_gather | solution.py:71
  10.9 16.4 %collective-permute-start.3 = (bf16[144,512]{1,0:T(8,128)(2,1)S(1)}, bf16[144,512]{1,0:T(8,128)(2,1)S(1)}, u32[]{:S(2)}, u32[]{:S(2)}) collective-permute-start(bf16[144,512]{1,0:T(8,128)(2,1)S(1)} %get-tuple-element.72), channel_id=1, source_target_pairs={{0,0},{1,128},{2,256},{3,384},{128,1},{129,129},{130,257},{131,385... | collective-permute-start | bytes 442376 | tf_op jit(solution)/shard_map/ppermute | solution.py:82
  15.5 16.9 %collective-permute-start.6 = (bf16[144,512]{1,0:T(8,128)(2,1)S(1)}, bf16[144,512]{1,0:T(8,128)(2,1)S(1)}, u32[]{:S(2)}, u32[]{:S(2)}) collective-permute-start(bf16[144,512]{1,0:T(8,128)(2,1)S(1)} %get-tuple-element.72), channel_id=1, source_target_pairs={{0,384},{1,256},{2,128},{3,0},{128,385},{129,257},{130,129},{131,1... | collective-permute-start | bytes 442376 | tf_op jit(solution)/shard_map/ppermute | solution.py:82
  21.3 11.2 %collective-permute-start.5 = (bf16[144,512]{1,0:T(8,128)(2,1)S(1)}, bf16[144,512]{1,0:T(8,128)(2,1)S(1)}, u32[]{:S(2)}, u32[]{:S(2)}) collective-permute-start(bf16[144,512]{1,0:T(8,128)(2,1)S(1)} %get-tuple-element.72), channel_id=1, source_target_pairs={{0,256},{1,384},{2,0},{3,128},{128,257},{129,385},{130,1},{131,129... | collective-permute-start | bytes 442376 | tf_op jit(solution)/shard_map/ppermute | solution.py:82
  23.4 12.7 %collective-permute-start.4 = (bf16[144,512]{1,0:T(8,128)(2,1)S(1)}, bf16[144,512]{1,0:T(8,128)(2,1)S(1)}, u32[]{:S(2)}, u32[]{:S(2)}) collective-permute-start(bf16[144,512]{1,0:T(8,128)(2,1)S(1)} %get-tuple-element.72), channel_id=1, source_target_pairs={{0,128},{1,0},{2,384},{3,256},{128,129},{129,1},{130,385},{131,257... | collective-permute-start | bytes 442376 | tf_op jit(solution)/shard_map/ppermute | solution.py:82
  27.4 58.4 %copy-start.40 = (f32[32]{0:T(128)}, f32[32]{0:T(128)S(1)}, u32[]{:S(2)}) copy-start(f32[32]{0:T(128)S(1)} %iota_add_fusion) | copy-start | bytes 388
  38.3 51.4 %all-to-all-start = ((bf16[32,16,2048]{2,1,0:T(8,128)(2,1)}), bf16[32,16,2048]{2,1,0:T(8,128)(2,1)S(1)}, u32[]{:S(2)}, u32[]{:S(2)}) async-start(bf16[32,16,2048]{2,1,0:T(8,128)(2,1)} %bitcast.47), calls=%async_computation | async-start | bytes 4194304 | tf_op jit(solution)/shard_map/all_to_all | solution.py:126
  53.2 21.5 %collective-permute-start.2 = (bf16[144,512]{1,0:T(8,128)(2,1)S(1)}, bf16[144,512]{1,0:T(8,128)(2,1)S(1)}, u32[]{:S(2)}, u32[]{:S(2)}) collective-permute-start(bf16[144,512]{1,0:T(8,128)(2,1)S(1)} %get-tuple-element.34), channel_id=1, source_target_pairs={{0,384},{128,256},{256,128},{384,0},{1,385},{129,257},{257,129},{3... | collective-permute-start | bytes 442376 | tf_op jit(solution)/shard_map/ppermute | solution.py:94
  61.5 22.7 %collective-permute-start.1 = (bf16[144,512]{1,0:T(8,128)(2,1)S(1)}, bf16[144,512]{1,0:T(8,128)(2,1)S(1)}, u32[]{:S(2)}, u32[]{:S(2)}) collective-permute-start(bf16[144,512]{1,0:T(8,128)(2,1)S(1)} %get-tuple-element.34), channel_id=1, source_target_pairs={{0,256},{128,384},{256,0},{384,128},{1,257},{129,385},{257,1},{385... | collective-permute-start | bytes 442376 | tf_op jit(solution)/shard_map/ppermute | solution.py:94
  72.7 11.5 %collective-permute-start = (bf16[144,512]{1,0:T(8,128)(2,1)S(1)}, bf16[144,512]{1,0:T(8,128)(2,1)S(1)}, u32[]{:S(2)}, u32[]{:S(2)}) collective-permute-start(bf16[144,512]{1,0:T(8,128)(2,1)S(1)} %get-tuple-element.34), channel_id=1, source_target_pairs={{0,128},{128,0},{256,384},{384,256},{1,129},{129,1},{257,385},{385... | collective-permute-start | bytes 442376 | tf_op jit(solution)/shard_map/ppermute | solution.py:94
  93.4 73.0 %all-to-all-start.1 = ((bf16[4,32,16,512]{3,2,0,1:T(8,128)(2,1)}), bf16[4,32,16,512]{3,2,0,1:T(8,128)(2,1)}, u32[]{:S(2)}, u32[]{:S(2)}) async-start(bf16[4,32,16,512]{3,2,0,1:T(8,128)(2,1)} %copy.82), calls=%async_computation.1 | async-start | bytes 4194304 | tf_op jit(solution)/shard_map/all_to_all | solution.py:131
  157.9 40.7 %collective-permute-start.8 = (bf16[768,512]{1,0:T(8,128)(2,1)S(1)}, bf16[768,512]{1,0:T(8,128)(2,1)S(1)}, u32[]{:S(2)}, u32[]{:S(2)}) collective-permute-start(bf16[768,512]{1,0:T(8,128)(2,1)S(1)} %fusion.refs_0_), channel_id=1, source_target_pairs={{0,2},{1,3},{2,0},{3,1},{4,6},{5,7},{6,4},{7,5},{8,10},{9,11},{10,... | collective-permute-start | bytes 2359304 | tf_op jit(solution)/shard_map/ppermute | solution.py:143
  164.5 36.8 %collective-permute-start.7 = (bf16[768,512]{1,0:T(8,128)(2,1)S(1)}, bf16[768,512]{1,0:T(8,128)(2,1)S(1)}, u32[]{:S(2)}, u32[]{:S(2)}) collective-permute-start(bf16[768,512]{1,0:T(8,128)(2,1)S(1)} %fusion.refs_0_), channel_id=1, source_target_pairs={{0,1},{1,0},{2,3},{3,2},{4,5},{5,4},{6,7},{7,6},{8,9},{9,8},{10,11... | collective-permute-start | bytes 2359304 | tf_op jit(solution)/shard_map/ppermute | solution.py:142
  170.8 33.5 %all-to-all-start.2 = ((bf16[32,1,16,512]{3,2,1,0:T(8,128)(2,1)}), bf16[32,1,16,512]{3,2,1,0:T(8,128)(2,1)}, u32[]{:S(2)}, u32[]{:S(2)}) async-start(bf16[32,1,16,512]{3,2,1,0:T(8,128)(2,1)} %broadcast_add_fusion.2), calls=%async_computation.2 | async-start | bytes 1048576 | tf_op jit(solution)/shard_map/all_to_all | solution.py:151
  207.3 37.6 %all-to-all-start.3 = ((bf16[32,2,16,512]{3,2,1,0:T(8,128)(2,1)}), bf16[32,2,16,512]{3,2,1,0:T(8,128)(2,1)}, u32[]{:S(2)}, u32[]{:S(2)}) async-start(bf16[32,2,16,512]{3,2,1,0:T(8,128)(2,1)} %broadcast_add_fusion), calls=%async_computation.3 | async-start | bytes 2097152 | tf_op jit(solution)/shard_map/all_to_all | solution.py:151
  224.8 19.5 %collective-permute-start.9 = (bf16[768,512]{1,0:T(8,128)(2,1)S(1)}, bf16[768,512]{1,0:T(8,128)(2,1)S(1)}, u32[]{:S(2)}, u32[]{:S(2)}) collective-permute-start(bf16[768,512]{1,0:T(8,128)(2,1)S(1)} %collective-permute-done.8.refs_1_), channel_id=1, source_target_pairs={{0,1},{1,0},{2,3},{3,2},{4,5},{5,4},{6,7},{7,6},{8,9},{9,8},{10,11... | collective-permute-start | bytes 2359304 | tf_op jit(solution)/shard_map/ppermute | solution.py:149
  247.7 20.6 %all-to-all-start.4 = ((bf16[32,1,16,512]{3,2,1,0:T(8,128)(2,1)}), bf16[32,1,16,512]{3,2,1,0:T(8,128)(2,1)S(1)}, u32[]{:S(2)}, u32[]{:S(2)}) async-start(bf16[32,1,16,512]{3,2,1,0:T(8,128)(2,1)} %broadcast_add_fusion.1), calls=%async_computation.4 | async-start | bytes 1048576 | tf_op jit(solution)/shard_map/all_to_all | solution.py:151
  269.7 21.4 %copy-start.20 = (f32[2,32,128]{2,1,0:T(8,128)S(1)}, f32[2,32,128]{2,1,0:T(8,128)}, u32[]{:S(2)}) copy-start(f32[2,32,128]{2,1,0:T(8,128)} %select_reduce_fusion) | copy-start | bytes 98308
  269.7 21.4 %copy-start.22 = (f32[4,1,1,128]{3,2,1,0:T(1,128)S(1)}, f32[4,1,1,128]{3,2,1,0:T(1,128)}, u32[]{:S(2)}) copy-start(f32[4,1,1,128]{3,2,1,0:T(1,128)} %copy-done.21) | copy-start | bytes 6148
  269.8 21.4 %copy-start.24 = (f32[4,1,1,128]{3,2,1,0:T(1,128)S(1)}, f32[4,1,1,128]{3,2,1,0:T(1,128)}, u32[]{:S(2)}) copy-start(f32[4,1,1,128]{3,2,1,0:T(1,128)} %copy-done.23) | copy-start | bytes 6148
  269.8 21.4 %copy-start.26 = (f32[4,1,1,128]{3,2,1,0:T(1,128)S(1)}, f32[4,1,1,128]{3,2,1,0:T(1,128)}, u32[]{:S(2)}) copy-start(f32[4,1,1,128]{3,2,1,0:T(1,128)} %copy-done.25) | copy-start | bytes 6148
  269.8 21.4 %copy-start.28 = (f32[4,1,1,128]{3,2,1,0:T(1,128)S(1)}, f32[4,1,1,128]{3,2,1,0:T(1,128)}, u32[]{:S(2)}) copy-start(f32[4,1,1,128]{3,2,1,0:T(1,128)} %copy-done.27) | copy-start | bytes 6148
  269.8 21.4 %copy-start.30 = (f32[4,1,1,128]{3,2,1,0:T(1,128)S(1)}, f32[4,1,1,128]{3,2,1,0:T(1,128)}, u32[]{:S(2)}) copy-start(f32[4,1,1,128]{3,2,1,0:T(1,128)} %copy-done.29) | copy-start | bytes 6148
  269.8 21.4 %copy-start.32 = (f32[4,1,1,128]{3,2,1,0:T(1,128)S(1)}, f32[4,1,1,128]{3,2,1,0:T(1,128)}, u32[]{:S(2)}) copy-start(f32[4,1,1,128]{3,2,1,0:T(1,128)} %copy-done.31) | copy-start | bytes 6148
  269.8 21.4 %copy-start.34 = (f32[4,1,1,128]{3,2,1,0:T(1,128)S(1)}, f32[4,1,1,128]{3,2,1,0:T(1,128)}, u32[]{:S(2)}) copy-start(f32[4,1,1,128]{3,2,1,0:T(1,128)} %copy-done.33) | copy-start | bytes 6148
  269.8 21.4 %copy-start.36 = (f32[4,1,1,128]{3,2,1,0:T(1,128)S(1)}, f32[4,1,1,128]{3,2,1,0:T(1,128)}, u32[]{:S(2)}) copy-start(f32[4,1,1,128]{3,2,1,0:T(1,128)} %copy-done.35) | copy-start | bytes 6148
  269.8 21.4 %copy-start.37 = (f32[32,128]{1,0:T(8,128)S(1)}, f32[32,128]{1,0:T(8,128)}, u32[]{:S(2)}) copy-start(f32[32,128]{1,0:T(8,128)} %fusion.10) | copy-start | bytes 49156
  269.8 29.8 %copy-start.4 = (f32[768,512]{1,0:T(8,128)S(1)}, f32[768,512]{1,0:T(8,128)}, u32[]{:S(2)}) copy-start(f32[768,512]{1,0:T(8,128)} %fusion.101) | copy-start | bytes 4718596
  270.7 37.2 %collective-permute-start.10 = (bf16[128,512]{1,0:T(8,128)(2,1)}, bf16[128,512]{1,0:T(8,128)(2,1)S(1)}, u32[]{:S(2)}, u32[]{:S(2)}) collective-permute-start(bf16[128,512]{1,0:T(8,128)(2,1)} %get-tuple-element.26), channel_id=1, source_target_pairs={{0,128},{128,0},{256,384},{384,256},{1,129},{129,1},{257,385},{385... | collective-permute-start | bytes 393224 | tf_op jit(solution)/shard_map/ppermute | solution.py:170
  279.7 28.1 %collective-permute-start.12 = (bf16[128,512]{1,0:T(8,128)(2,1)}, bf16[128,512]{1,0:T(8,128)(2,1)}, u32[]{:S(2)}, u32[]{:S(2)}) collective-permute-start(bf16[128,512]{1,0:T(8,128)(2,1)} %get-tuple-element.27), channel_id=1, source_target_pairs={{0,384},{128,256},{256,128},{384,0},{1,385},{129,257},{257,129},{3... | collective-permute-start | bytes 393224 | tf_op jit(solution)/shard_map/ppermute | solution.py:170
  287.1 20.7 %collective-permute-start.11 = (bf16[128,512]{1,0:T(8,128)(2,1)}, bf16[128,512]{1,0:T(8,128)(2,1)}, u32[]{:S(2)}, u32[]{:S(2)}) collective-permute-start(bf16[128,512]{1,0:T(8,128)(2,1)} %get-tuple-element.28), channel_id=1, source_target_pairs={{0,256},{128,384},{256,0},{384,128},{1,257},{129,385},{257,1},{385... | collective-permute-start | bytes 393224 | tf_op jit(solution)/shard_map/ppermute | solution.py:170
  292.1 15.2 %all-to-all-start.5 = ((f32[16,8,128]{2,1,0:T(8,128)}), f32[16,8,128]{2,1,0:T(8,128)S(1)}, u32[]{:S(2)}, u32[]{:S(2)}) async-start(f32[16,8,128]{2,1,0:T(8,128)} %bitcast.95), calls=%async_computation.5 | async-start | bytes 131072 | tf_op jit(solution)/shard_map/all_to_all | solution.py:172
  (30 other events, 163.3 us)
Sparse Core Ops, SparseCore 0:
  10.7 139.4 all-gather.2

commit v7 on v6

--- a/solution.py
+++ b/solution.py
@@ -77,21 +77,22 @@
     token_rows = jnp.concatenate([tokens, meta], axis=0)
     upstream_rows = jnp.concatenate([upstream, meta], axis=0)
 
-    pieces = jnp.stack(
-        [
-            lax.ppermute(
-                token_rows,
-                ("grp", "split"),
-                [(g * split + f, (f ^ m) * split + g) for g in range(grp) for f in range(split)],
-            )
-            for m in range(split)
-        ]
-    )
+    core = flipped(grp, 1)
+    pieces = [None] * split
+    for m in (0, 2):
+        pieces[m] = lax.ppermute(
+            token_rows,
+            ("grp", "split"),
+            [(g * split + f, (f ^ m) * split + g) for g in range(grp) for f in range(split)],
+        )
+        pieces[m + 1] = lax.ppermute(pieces[m], "grp", core)
+    pieces = jnp.stack(pieces)
     mine = [lax.dynamic_index_in_dim(pieces[:, :rows], grp_me ^ f, 0, keepdims=False) for f in range(split)]
     mine = jnp.concatenate(mine, axis=1)
 
+    far = lax.ppermute(upstream_rows, "grp", flipped(grp, 2))
     near = jnp.stack(
-        [upstream_rows] + [lax.ppermute(upstream_rows, "grp", flipped(grp, m)) for m in range(1, grp)]
+        [upstream_rows, lax.ppermute(upstream_rows, "grp", core), far, lax.ppermute(far, "grp", core)]
     )
     near = jnp.stack(
         [lax.dynamic_index_in_dim(near, grp_me ^ split_me ^ j, 0, keepdims=False) for j in range(grp)]
@@ -165,9 +166,10 @@
         lax.dynamic_index_in_dim(mixed, grp_me ^ split_me ^ m, 0, keepdims=False) for m in range(grp)
     ]
     grads = after(relative(grads), own_mixed[1])
-    total = own_mixed[0].astype(f32)
-    for m in range(1, grp):
-        total = total + lax.ppermute(own_mixed[m], "grp", flipped(grp, m)).astype(f32)
+    other = lax.ppermute(jnp.stack([own_mixed[1], own_mixed[3]]), "grp", core).astype(f32)
+    far_sum = (own_mixed[2].astype(f32) + other[1]).astype(bf16)
+    total = own_mixed[0].astype(f32) + other[0]
+    total = total + lax.ppermute(far_sum, "grp", flipped(grp, 2)).astype(f32)
     grads = jnp.broadcast_to(grads[:, None], (grp, split, top, rows)).reshape(grp * split, top, rows)
     grads = lax.all_to_all(grads, ("grp", "split"), split_axis=0, concat_axis=0, tiled=True)
     gate_grads = jnp.sum(grads, axis=0).T

time: 318 us -> 304 us (0.956)
  starting transfers between devices: 129 us -> 113 us
    all_to_all x1, waiting for transfers between devices: 2.59 us -> 25.1 us  [per_device(): lax.all_to_all(send.reshape(dev, SLOTS, split * feats), 'dev', split_axis...]
    all_gather x1, waiting for transfers between devices: 46.1 us -> 36 us  [per_device(): w_all = lax.all_gather(w_own, 'split', axis=0, tiled=False)]
    ppermute x4 -> x2, starting transfers between devices: 16.3 us -> 10.5 us  [per_device(): lax.ppermute(token_rows, ('grp', 'split'), [(g * split + f, (f ^ m) * spl...]
    ppermute x4 -> x2, waiting for transfers between devices: 8.38 us -> 3.9 us  [per_device(): lax.ppermute(token_rows, ('grp', 'split'), [(g * split + f, (f ^ m) * spl...]
    all_to_all x1, waiting for transfers between devices: 3.82 us -> 0.01 us  [per_device(): lax.all_to_all(grads, ('grp', 'split'), split_axis=0, concat_axis=0, tile...]
    ppermute x6 -> x7, starting transfers between devices: 38.6 us -> 36.6 us  [the longest x1 9.8 us: per_device(): lax.ppermute(jnp.stack([own_mixed[1], own_mixed[3]]), 'grp', core)]
    ppermute x6 -> x7, waiting for transfers between devices: 9.51 us -> 7.64 us  [the longest x1 6.06 us: per_device(): far = lax.ppermute(upstream_rows, 'grp', flipped(grp, 2))]
  transfers between devices with their start and end apart: 20 -> 19, of which waited for: 10 -> 9; matrix products, arithmetic and copies ran while one was open for 15% -> 16% of each run, Pallas kernels for 1% -> 1%
where the time goes in v7:
time: 304 us; the launch traced here: 300 us
  starting transfers between devices  113 us (37%)
  waiting for transfers between devices  104 us (34%)
  matrix products  28.8 us (9%)
  between operations  18.4 us (6%)
  local copies, waits for them, and re-layouts  17.8 us (6%)
  other arithmetic  16.5 us (5%)
    all_gather x1, waiting for transfers between devices, per_device(): w_all = lax.all_gather(w_own, 'split', axis=0, tiled=False)  36 us
    all_to_all x3, starting transfers between devices, per_device(): lax.all_to_all(out, 'dev', split_axis=0, concat_axis=0, tiled=True)  29.2 us
    all_to_all x1, waiting for transfers between devices, per_device(): lax.all_to_all(send.reshape(dev, SLOTS, split * feats), 'dev', split_axis...  25.1 us
    ppermute x1, waiting for transfers between devices, per_device(): hidden_of.append(lax.ppermute(hidden, 'split', flipped(split, 2)))  17.9 us
    all_to_all x1, starting transfers between devices, per_device(): lax.all_to_all(send.reshape(dev, SLOTS, split * feats), 'dev', split_axis...  12.9 us
    ppermute x2, starting transfers between devices, per_device(): lax.ppermute(token_rows, ('grp', 'split'), [(g * split + f, (f ^ m) * spl...  10.5 us
    ppermute x1, starting transfers between devices, per_device(): lax.ppermute(jnp.stack([own_mixed[1], own_mixed[3]]), 'grp', core)  9.8 us
    ppermute x1, waiting for transfers between devices, per_device(): hidden_of.append(lax.ppermute(hidden_of[2], 'split', flipped(split, 1)))  9.34 us
  transfers between devices with their start and end apart: 19, of which 9 were waited for; matrix products, arithmetic and copies ran while one was open for 16% of the time, Pallas kernels for 1%

profile of v7, /device:TPU:1, one launch (start us, length us, event | category | flops | bytes accessed | tf_op | source)
XLA Modules:
  0.0 300.2 jit_solution(9332991844306961618)
XLA Ops:
  7.2 2.7 pad_maximum_fusion
  10.9 4.6 %collective-permute-start.3 = (bf16[144,512]{1,0:T(8,128)(2,1)S(1)}, bf16[144,512]{1,0:T(8,128)(2,1)S(1)}, u32[]{:S(2)}, u32[]{:S(2)}) collective-permute-start(bf16[144,512]{1,0:T(8,128)(2,1)S(1)} %get-tuple-element.71), channel_id=1, source_target_pairs={{0,0},{1,128},{2,256},{3,384},{128,1},{129,129},{130,257},{131,385... | collective-permute-start | bytes 442376 | tf_op jit(solution)/shard_map/ppermute | solution.py:83
  15.5 5.9 %collective-permute-start.5 = (bf16[144,512]{1,0:T(8,128)(2,1)S(1)}, bf16[144,512]{1,0:T(8,128)(2,1)S(1)}, u32[]{:S(2)}, u32[]{:S(2)}) collective-permute-start(bf16[144,512]{1,0:T(8,128)(2,1)S(1)} %get-tuple-element.71), channel_id=1, source_target_pairs={{0,256},{1,384},{2,0},{3,128},{128,257},{129,385},{130,1},{131,129... | collective-permute-start | bytes 442376 | tf_op jit(solution)/shard_map/ppermute | solution.py:83
  21.6 2.9 collective-permute-start.4
  24.5 3.9 %collective-permute-done.5 = bf16[144,512]{1,0:T(8,128)(2,1)S(1)} collective-permute-done((bf16[144,512]{1,0:T(8,128)(2,1)S(1)}, bf16[144,512]{1,0:T(8,128)(2,1)S(1)}, u32[]{:S(2)}, u32[]{:S(2)}) %collective-permute-start.5) | collective-permute-done | bytes 147488 | tf_op jit(solution)/shard_map/ppermute | solution.py:83
  28.4 3.2 %collective-permute-start.6 = (bf16[144,512]{1,0:T(8,128)(2,1)S(1)}, bf16[144,512]{1,0:T(8,128)(2,1)S(1)}, u32[]{:S(2)}, u32[]{:S(2)}) collective-permute-start(bf16[144,512]{1,0:T(8,128)(2,1)S(1)} %collective-permute-done.5), channel_id=1, source_target_pairs={{0,128},{128,0},{256,384},{384,256},{1,129},{129,1},{257,385},{385... | collective-permute-start | bytes 442376 | tf_op jit(solution)/shard_map/ppermute | solution.py:88
  32.8 2.1 convolution_convert_fusion
  34.8 12.9 %all-to-all-start = ((bf16[32,16,2048]{2,1,0:T(8,128)(2,1)}), bf16[32,16,2048]{2,1,0:T(8,128)(2,1)S(1)}, u32[]{:S(2)}, u32[]{:S(2)}) async-start(bf16[32,16,2048]{2,1,0:T(8,128)(2,1)} %bitcast.47), calls=%async_computation | async-start | bytes 4194304 | tf_op jit(solution)/shard_map/all_to_all | solution.py:127
  47.7 7.0 %collective-permute-start.1 = (bf16[144,512]{1,0:T(8,128)(2,1)S(1)}, bf16[144,512]{1,0:T(8,128)(2,1)S(1)}, u32[]{:S(2)}, u32[]{:S(2)}) collective-permute-start(bf16[144,512]{1,0:T(8,128)(2,1)S(1)} %get-tuple-element.33), channel_id=1, source_target_pairs={{0,256},{128,384},{256,0},{384,128},{1,257},{129,385},{257,1},{385... | collective-permute-start | bytes 442376 | tf_op jit(solution)/shard_map/ppermute | solution.py:93
  54.8 2.8 collective-permute-start
  57.6 6.1 %collective-permute-done.1 = bf16[144,512]{1,0:T(8,128)(2,1)S(1)} collective-permute-done((bf16[144,512]{1,0:T(8,128)(2,1)S(1)}, bf16[144,512]{1,0:T(8,128)(2,1)S(1)}, u32[]{:S(2)}, u32[]{:S(2)}) %collective-permute-start.1) | collective-permute-done | bytes 147488 | tf_op jit(solution)/shard_map/ppermute | solution.py:93
  63.7 3.6 %collective-permute-start.2 = (bf16[144,512]{1,0:T(8,128)(2,1)S(1)}, bf16[144,512]{1,0:T(8,128)(2,1)S(1)}, u32[]{:S(2)}, u32[]{:S(2)}) collective-permute-start(bf16[144,512]{1,0:T(8,128)(2,1)S(1)} %collective-permute-done.1), channel_id=1, source_target_pairs={{0,128},{128,0},{256,384},{384,256},{1,129},{129,1},{257,385},{385... | collective-permute-start | bytes 442376 | tf_op jit(solution)/shard_map/ppermute | solution.py:95
  71.2 25.1 %all-to-all-done = bf16[32,16,2048]{2,1,0:T(8,128)(2,1)S(1)} async-done(((bf16[32,16,2048]{2,1,0:T(8,128)(2,1)}), bf16[32,16,2048]{2,1,0:T(8,128)(2,1)S(1)}, u32[]{:S(2)}, u32[]{:S(2)}) %all-to-all-start) | async-done | bytes 2097184 | tf_op jit(solution)/shard_map/all_to_all | solution.py:127
  100.0 7.8 %all-to-all-start.1 = ((bf16[4,32,16,512]{3,2,0,1:T(8,128)(2,1)}), bf16[4,32,16,512]{3,2,0,1:T(8,128)(2,1)}, u32[]{:S(2)}, u32[]{:S(2)}) async-start(bf16[4,32,16,512]{3,2,0,1:T(8,128)(2,1)} %copy.82), calls=%async_computation.1 | async-start | bytes 4194304 | tf_op jit(solution)/shard_map/all_to_all | solution.py:132
  107.8 36.0 %all-gather.3.cloned.1.call-done = bf16[1536,2048]{1,0:T(8,128)(2,1)} async-done(((bf16[384,2048]{1,0:T(8,128)(2,1)}), bf16[1536,2048]{1,0:T(8,128)(2,1)}) %all-gather.3.cloned.1.call-update) | async-done | bytes 6291472 | tf_op jit(solution)/shard_map/all_gather | solution.py:71
  143.8 5.6 %fusion.100 = f32[4,2,192,512]{3,2,1,0:T(8,128)S(1)} fusion(bf16[4,2,192,2048]{3,2,1,0:T(8,128)(2,1)} %bitcast.289, bf16[512,2048,1,1]{1,0,3,2:T(8,128)(2,1)S(1)} %bitcast.231), kind=kOutput, calls=%fused_computation.210 | convolution fusion | flops 3221225472 | bytes 11534336 | tf_op jit(solution)/shard_map/dot_general | solution.py:135
  151.5 3.8 %collective-permute-start.8 = (bf16[768,512]{1,0:T(8,128)(2,1)S(1)}, bf16[768,512]{1,0:T(8,128)(2,1)S(1)}, u32[]{:S(2)}, u32[]{:S(2)}) collective-permute-start(bf16[768,512]{1,0:T(8,128)(2,1)S(1)} %fusion.refs_0_), channel_id=1, source_target_pairs={{0,2},{1,3},{2,0},{3,1},{4,6},{5,7},{6,4},{7,5},{8,10},{9,11},{10,... | collective-permute-start | bytes 2359304 | tf_op jit(solution)/shard_map/ppermute | solution.py:144
  161.6 10.2 %all-to-all-start.2 = ((bf16[32,1,16,512]{3,2,1,0:T(8,128)(2,1)}), bf16[32,1,16,512]{3,2,1,0:T(8,128)(2,1)}, u32[]{:S(2)}, u32[]{:S(2)}) async-start(bf16[32,1,16,512]{3,2,1,0:T(8,128)(2,1)} %broadcast_add_fusion.2), calls=%async_computation.2 | async-start | bytes 1048576 | tf_op jit(solution)/shard_map/all_to_all | solution.py:152
  171.8 17.9 %collective-permute-done.8.refs_1_ = bf16[768,512]{1,0:T(8,128)(2,1)S(1)} collective-permute-done((bf16[768,512]{1,0:T(8,128)(2,1)S(1)}, bf16[768,512]{1,0:T(8,128)(2,1)S(1)}, u32[]{:S(2)}, u32[]{:S(2)}) %collective-permute-start.8) | collective-permute-done | bytes 786464 | tf_op jit(solution)/shard_map/ppermute | solution.py:144
  195.8 10.2 %all-to-all-start.3 = ((bf16[32,2,16,512]{3,2,1,0:T(8,128)(2,1)}), bf16[32,2,16,512]{3,2,1,0:T(8,128)(2,1)}, u32[]{:S(2)}, u32[]{:S(2)}) async-start(bf16[32,2,16,512]{3,2,1,0:T(8,128)(2,1)} %broadcast_add_fusion), calls=%async_computation.3 | async-start | bytes 2097152 | tf_op jit(solution)/shard_map/all_to_all | solution.py:152
  209.5 2.6 fusion.97
  213.8 3.1 %collective-permute-start.9 = (bf16[768,512]{1,0:T(8,128)(2,1)S(1)}, bf16[768,512]{1,0:T(8,128)(2,1)S(1)}, u32[]{:S(2)}, u32[]{:S(2)}) collective-permute-start(bf16[768,512]{1,0:T(8,128)(2,1)S(1)} %collective-permute-done.8.refs_1_), channel_id=1, source_target_pairs={{0,1},{1,0},{2,3},{3,2},{4,5},{5,4},{6,7},{7,6},{8,9},{9,8},{10,11... | collective-permute-start | bytes 2359304 | tf_op jit(solution)/shard_map/ppermute | solution.py:150
  220.4 2.0 fusion.101
  222.4 9.3 %collective-permute-done.9.refs_0_ = bf16[768,512]{1,0:T(8,128)(2,1)S(1)} collective-permute-done((bf16[768,512]{1,0:T(8,128)(2,1)S(1)}, bf16[768,512]{1,0:T(8,128)(2,1)S(1)}, u32[]{:S(2)}, u32[]{:S(2)}) %collective-permute-start.9) | collective-permute-done | bytes 786464 | tf_op jit(solution)/shard_map/ppermute | solution.py:150
  235.1 8.8 %all-to-all-start.4 = ((bf16[32,1,16,512]{3,2,1,0:T(8,128)(2,1)}), bf16[32,1,16,512]{3,2,1,0:T(8,128)(2,1)S(1)}, u32[]{:S(2)}, u32[]{:S(2)}) async-start(bf16[32,1,16,512]{3,2,1,0:T(8,128)(2,1)} %broadcast_add_fusion.1), calls=%async_computation.4 | async-start | bytes 1048576 | tf_op jit(solution)/shard_map/all_to_all | solution.py:152
  243.9 2.0 fusion.10
  246.0 2.0 fusion.12
  251.7 3.8 %all-to-all-done.4 = bf16[32,1,16,512]{3,2,1,0:T(8,128)(2,1)S(1)} async-done(((bf16[32,1,16,512]{3,2,1,0:T(8,128)(2,1)}), bf16[32,1,16,512]{3,2,1,0:T(8,128)(2,1)S(1)}, u32[]{:S(2)}, u32[]{:S(2)}) %all-to-all-start.4) | async-done | bytes 524320 | tf_op jit(solution)/shard_map/all_to_all | solution.py:152
  257.9 9.8 %collective-permute-start.10 = (bf16[2,128,512]{2,1,0:T(8,128)(2,1)S(1)}, bf16[2,128,512]{2,1,0:T(8,128)(2,1)}, u32[]{:S(2)}, u32[]{:S(2)}) collective-permute-start(bf16[2,128,512]{2,1,0:T(8,128)(2,1)S(1)} %pad_maximum_fusion.14), channel_id=1, source_target_pairs={{0,128},{128,0},{256,384},{384,256},{1,129},{129,1},{257,385},{385... | collective-permute-start | bytes 786440 | tf_op jit(solution)/shard_map/ppermute | solution.py:169
  271.1 7.1 %all-to-all-start.5 = ((f32[16,8,128]{2,1,0:T(8,128)}), f32[16,8,128]{2,1,0:T(8,128)S(1)}, u32[]{:S(2)}, u32[]{:S(2)}) async-start(f32[16,8,128]{2,1,0:T(8,128)} %bitcast.94), calls=%async_computation.5 | async-start | bytes 131072 | tf_op jit(solution)/shard_map/all_to_all | solution.py:174
  280.2 7.2 %collective-permute-start.11 = (bf16[128,512]{1,0:T(8,128)(2,1)S(1)}, bf16[128,512]{1,0:T(8,128)(2,1)S(1)}, u32[]{:S(2)}, u32[]{:S(2)}) collective-permute-start(bf16[128,512]{1,0:T(8,128)(2,1)S(1)} %fusion.41), channel_id=1, source_target_pairs={{0,256},{128,384},{256,0},{384,128},{1,257},{129,385},{257,1},{385... | collective-permute-start | bytes 393224 | tf_op jit(solution)/shard_map/ppermute | solution.py:172
  287.4 3.8 %add_bitcast_fusion = f32[1,768,512]{2,1,0:T(8,128)} fusion(f32[768,512]{1,0:T(8,128)} %fusion.105, f32[768,512]{1,0:T(8,128)S(1)} %copy-done.4, f32[768,512]{1,0:T(8,128)} %fusion.104, bf16[768,512]{1,0:T(8,128)(2,1)S(1)} %collective-permute-done.9.refs_0_, bf16[512,512]{1,0:T(8,128)(2,1)} %bitcast.238), kind=kOutput, calls=%fused_computation.10 | convolution fusion | flops 403832832 | bytes 7602176 | tf_op jit(solution)/shard_map/dot_general | solution.py:178
  (172 shorter events, 46.2 us)
Async XLA Ops:
  7.2 136.6 %all-gather.3.cloned.1.call-start = ((), (), s32[]{:S(2)}) async-start(), calls=%async_computation.6 | async-start | bytes 7864320 | tf_op jit(solution)/shard_map/all_gather | solution.py:71
  10.9 10.7 %collective-permute-start.3 = (bf16[144,512]{1,0:T(8,128)(2,1)S(1)}, bf16[144,512]{1,0:T(8,128)(2,1)S(1)}, u32[]{:S(2)}, u32[]{:S(2)}) collective-permute-start(bf16[144,512]{1,0:T(8,128)(2,1)S(1)} %get-tuple-element.71), channel_id=1, source_target_pairs={{0,0},{1,128},{2,256},{3,384},{128,1},{129,129},{130,257},{131,385... | collective-permute-start | bytes 442376 | tf_op jit(solution)/shard_map/ppermute | solution.py:83
  15.5 12.9 %collective-permute-start.5 = (bf16[144,512]{1,0:T(8,128)(2,1)S(1)}, bf16[144,512]{1,0:T(8,128)(2,1)S(1)}, u32[]{:S(2)}, u32[]{:S(2)}) collective-permute-start(bf16[144,512]{1,0:T(8,128)(2,1)S(1)} %get-tuple-element.71), channel_id=1, source_target_pairs={{0,256},{1,384},{2,0},{3,128},{128,257},{129,385},{130,1},{131,129... | collective-permute-start | bytes 442376 | tf_op jit(solution)/shard_map/ppermute | solution.py:83
  21.6 48.3 %copy-start.41 = (f32[32]{0:T(128)}, f32[32]{0:T(128)S(1)}, u32[]{:S(2)}) copy-start(f32[32]{0:T(128)S(1)} %iota_add_fusion) | copy-start | bytes 388
  21.6 11.0 %collective-permute-start.4 = (bf16[144,512]{1,0:T(8,128)(2,1)S(1)}, bf16[144,512]{1,0:T(8,128)(2,1)S(1)}, u32[]{:S(2)}, u32[]{:S(2)}) collective-permute-start(bf16[144,512]{1,0:T(8,128)(2,1)S(1)} %collective-permute-done.3), channel_id=1, source_target_pairs={{0,128},{128,0},{256,384},{384,256},{1,129},{129,1},{257,385},{385... | collective-permute-start | bytes 442376 | tf_op jit(solution)/shard_map/ppermute | solution.py:88
  28.4 4.2 %collective-permute-start.6 = (bf16[144,512]{1,0:T(8,128)(2,1)S(1)}, bf16[144,512]{1,0:T(8,128)(2,1)S(1)}, u32[]{:S(2)}, u32[]{:S(2)}) collective-permute-start(bf16[144,512]{1,0:T(8,128)(2,1)S(1)} %collective-permute-done.5), channel_id=1, source_target_pairs={{0,128},{128,0},{256,384},{384,256},{1,129},{129,1},{257,385},{385... | collective-permute-start | bytes 442376 | tf_op jit(solution)/shard_map/ppermute | solution.py:88
  34.8 61.5 %all-to-all-start = ((bf16[32,16,2048]{2,1,0:T(8,128)(2,1)}), bf16[32,16,2048]{2,1,0:T(8,128)(2,1)S(1)}, u32[]{:S(2)}, u32[]{:S(2)}) async-start(bf16[32,16,2048]{2,1,0:T(8,128)(2,1)} %bitcast.47), calls=%async_computation | async-start | bytes 4194304 | tf_op jit(solution)/shard_map/all_to_all | solution.py:127
  47.7 15.9 %collective-permute-start.1 = (bf16[144,512]{1,0:T(8,128)(2,1)S(1)}, bf16[144,512]{1,0:T(8,128)(2,1)S(1)}, u32[]{:S(2)}, u32[]{:S(2)}) collective-permute-start(bf16[144,512]{1,0:T(8,128)(2,1)S(1)} %get-tuple-element.33), channel_id=1, source_target_pairs={{0,256},{128,384},{256,0},{384,128},{1,257},{129,385},{257,1},{385... | collective-permute-start | bytes 442376 | tf_op jit(solution)/shard_map/ppermute | solution.py:93
  54.8 12.5 %collective-permute-start = (bf16[144,512]{1,0:T(8,128)(2,1)S(1)}, bf16[144,512]{1,0:T(8,128)(2,1)S(1)}, u32[]{:S(2)}, u32[]{:S(2)}) collective-permute-start(bf16[144,512]{1,0:T(8,128)(2,1)S(1)} %get-tuple-element.33), channel_id=1, source_target_pairs={{0,128},{128,0},{256,384},{384,256},{1,129},{129,1},{257,385},{385... | collective-permute-start | bytes 442376 | tf_op jit(solution)/shard_map/ppermute | solution.py:95
  63.7 4.6 %collective-permute-start.2 = (bf16[144,512]{1,0:T(8,128)(2,1)S(1)}, bf16[144,512]{1,0:T(8,128)(2,1)S(1)}, u32[]{:S(2)}, u32[]{:S(2)}) collective-permute-start(bf16[144,512]{1,0:T(8,128)(2,1)S(1)} %collective-permute-done.1), channel_id=1, source_target_pairs={{0,128},{128,0},{256,384},{384,256},{1,129},{129,1},{257,385},{385... | collective-permute-start | bytes 442376 | tf_op jit(solution)/shard_map/ppermute | solution.py:95
  69.2 28.5 %copy-start.11 = (bf16[1,144,512]{2,1,0:T(8,128)(2,1)}, bf16[1,144,512]{2,1,0:T(8,128)(2,1)S(1)}, u32[]{:S(2)}) copy-start(bf16[1,144,512]{2,1,0:T(8,128)(2,1)S(1)} %get-tuple-element.25) | copy-start | bytes 442372
  69.3 29.2 %copy-start.22 = (f32[4,1,1,128]{3,2,1,0:T(1,128)}, f32[4,1,1,128]{3,2,1,0:T(1,128)S(1)}, u32[]{:S(2)}) copy-start(f32[4,1,1,128]{3,2,1,0:T(1,128)S(1)} %get-tuple-element.40) | copy-start | bytes 6148
  69.3 29.2 %copy-start.24 = (f32[4,1,1,128]{3,2,1,0:T(1,128)}, f32[4,1,1,128]{3,2,1,0:T(1,128)S(1)}, u32[]{:S(2)}) copy-start(f32[4,1,1,128]{3,2,1,0:T(1,128)S(1)} %get-tuple-element.41) | copy-start | bytes 6148
  69.3 29.2 %copy-start.26 = (f32[4,1,1,128]{3,2,1,0:T(1,128)}, f32[4,1,1,128]{3,2,1,0:T(1,128)S(1)}, u32[]{:S(2)}) copy-start(f32[4,1,1,128]{3,2,1,0:T(1,128)S(1)} %get-tuple-element.42) | copy-start | bytes 6148
  69.3 29.2 %copy-start.28 = (f32[4,1,1,128]{3,2,1,0:T(1,128)}, f32[4,1,1,128]{3,2,1,0:T(1,128)S(1)}, u32[]{:S(2)}) copy-start(f32[4,1,1,128]{3,2,1,0:T(1,128)S(1)} %get-tuple-element.43) | copy-start | bytes 6148
  69.3 29.2 %copy-start.30 = (f32[4,1,1,128]{3,2,1,0:T(1,128)}, f32[4,1,1,128]{3,2,1,0:T(1,128)S(1)}, u32[]{:S(2)}) copy-start(f32[4,1,1,128]{3,2,1,0:T(1,128)S(1)} %get-tuple-element.44) | copy-start | bytes 6148
  69.3 29.2 %copy-start.32 = (f32[4,1,1,128]{3,2,1,0:T(1,128)}, f32[4,1,1,128]{3,2,1,0:T(1,128)S(1)}, u32[]{:S(2)}) copy-start(f32[4,1,1,128]{3,2,1,0:T(1,128)S(1)} %get-tuple-element.45) | copy-start | bytes 6148
  69.3 29.2 %copy-start.34 = (f32[4,1,1,128]{3,2,1,0:T(1,128)}, f32[4,1,1,128]{3,2,1,0:T(1,128)S(1)}, u32[]{:S(2)}) copy-start(f32[4,1,1,128]{3,2,1,0:T(1,128)S(1)} %get-tuple-element.46) | copy-start | bytes 6148
  69.3 29.2 %copy-start.36 = (f32[4,1,1,128]{3,2,1,0:T(1,128)}, f32[4,1,1,128]{3,2,1,0:T(1,128)S(1)}, u32[]{:S(2)}) copy-start(f32[4,1,1,128]{3,2,1,0:T(1,128)S(1)} %get-tuple-element.47) | copy-start | bytes 6148
  69.6 28.9 %copy-start.13 = (f32[4,32,128]{2,1,0:T(8,128)}, f32[4,32,128]{2,1,0:T(8,128)S(1)}, u32[]{:S(2)}) copy-start(f32[4,32,128]{2,1,0:T(8,128)S(1)} %convolution_select_fusion) | copy-start | bytes 196612
  100.0 57.2 %all-to-all-start.1 = ((bf16[4,32,16,512]{3,2,0,1:T(8,128)(2,1)}), bf16[4,32,16,512]{3,2,0,1:T(8,128)(2,1)}, u32[]{:S(2)}, u32[]{:S(2)}) async-start(bf16[4,32,16,512]{3,2,0,1:T(8,128)(2,1)} %copy.82), calls=%async_computation.1 | async-start | bytes 4194304 | tf_op jit(solution)/shard_map/all_to_all | solution.py:132
  151.5 38.2 %collective-permute-start.8 = (bf16[768,512]{1,0:T(8,128)(2,1)S(1)}, bf16[768,512]{1,0:T(8,128)(2,1)S(1)}, u32[]{:S(2)}, u32[]{:S(2)}) collective-permute-start(bf16[768,512]{1,0:T(8,128)(2,1)S(1)} %fusion.refs_0_), channel_id=1, source_target_pairs={{0,2},{1,3},{2,0},{3,1},{4,6},{5,7},{6,4},{7,5},{8,10},{9,11},{10,... | collective-permute-start | bytes 2359304 | tf_op jit(solution)/shard_map/ppermute | solution.py:144
  155.3 34.4 %collective-permute-start.7 = (bf16[768,512]{1,0:T(8,128)(2,1)S(1)}, bf16[768,512]{1,0:T(8,128)(2,1)S(1)}, u32[]{:S(2)}, u32[]{:S(2)}) collective-permute-start(bf16[768,512]{1,0:T(8,128)(2,1)S(1)} %fusion.refs_0_), channel_id=1, source_target_pairs={{0,1},{1,0},{2,3},{3,2},{4,5},{5,4},{6,7},{7,6},{8,9},{9,8},{10,11... | collective-permute-start | bytes 2359304 | tf_op jit(solution)/shard_map/ppermute | solution.py:143
  161.6 31.2 %all-to-all-start.2 = ((bf16[32,1,16,512]{3,2,1,0:T(8,128)(2,1)}), bf16[32,1,16,512]{3,2,1,0:T(8,128)(2,1)}, u32[]{:S(2)}, u32[]{:S(2)}) async-start(bf16[32,1,16,512]{3,2,1,0:T(8,128)(2,1)} %broadcast_add_fusion.2), calls=%async_computation.2 | async-start | bytes 1048576 | tf_op jit(solution)/shard_map/all_to_all | solution.py:152
  195.8 36.6 %all-to-all-start.3 = ((bf16[32,2,16,512]{3,2,1,0:T(8,128)(2,1)}), bf16[32,2,16,512]{3,2,1,0:T(8,128)(2,1)}, u32[]{:S(2)}, u32[]{:S(2)}) async-start(bf16[32,2,16,512]{3,2,1,0:T(8,128)(2,1)} %broadcast_add_fusion), calls=%async_computation.3 | async-start | bytes 2097152 | tf_op jit(solution)/shard_map/all_to_all | solution.py:152
  213.8 17.9 %collective-permute-start.9 = (bf16[768,512]{1,0:T(8,128)(2,1)S(1)}, bf16[768,512]{1,0:T(8,128)(2,1)S(1)}, u32[]{:S(2)}, u32[]{:S(2)}) collective-permute-start(bf16[768,512]{1,0:T(8,128)(2,1)S(1)} %collective-permute-done.8.refs_1_), channel_id=1, source_target_pairs={{0,1},{1,0},{2,3},{3,2},{4,5},{5,4},{6,7},{7,6},{8,9},{9,8},{10,11... | collective-permute-start | bytes 2359304 | tf_op jit(solution)/shard_map/ppermute | solution.py:150
  232.3 13.6 %copy-start.9 = (f32[128,512]{1,0:T(8,128)S(1)}, f32[128,512]{1,0:T(8,128)}, u32[]{:S(2)}) copy-start(f32[128,512]{1,0:T(8,128)} %fusion.101) | copy-start | bytes 786436
  235.1 20.3 %all-to-all-start.4 = ((bf16[32,1,16,512]{3,2,1,0:T(8,128)(2,1)}), bf16[32,1,16,512]{3,2,1,0:T(8,128)(2,1)S(1)}, u32[]{:S(2)}, u32[]{:S(2)}) async-start(bf16[32,1,16,512]{3,2,1,0:T(8,128)(2,1)} %broadcast_add_fusion.1), calls=%async_computation.4 | async-start | bytes 1048576 | tf_op jit(solution)/shard_map/all_to_all | solution.py:152
  257.9 29.5 %copy-start.4 = (f32[768,512]{1,0:T(8,128)S(1)}, f32[768,512]{1,0:T(8,128)}, u32[]{:S(2)}) copy-start(f32[768,512]{1,0:T(8,128)} %fusion.103) | copy-start | bytes 4718596
  257.9 20.3 %collective-permute-start.10 = (bf16[2,128,512]{2,1,0:T(8,128)(2,1)S(1)}, bf16[2,128,512]{2,1,0:T(8,128)(2,1)}, u32[]{:S(2)}, u32[]{:S(2)}) collective-permute-start(bf16[2,128,512]{2,1,0:T(8,128)(2,1)S(1)} %pad_maximum_fusion.14), channel_id=1, source_target_pairs={{0,128},{128,0},{256,384},{384,256},{1,129},{129,1},{257,385},{385... | collective-permute-start | bytes 786440 | tf_op jit(solution)/shard_map/ppermute | solution.py:169
  271.1 20.0 %all-to-all-start.5 = ((f32[16,8,128]{2,1,0:T(8,128)}), f32[16,8,128]{2,1,0:T(8,128)S(1)}, u32[]{:S(2)}, u32[]{:S(2)}) async-start(f32[16,8,128]{2,1,0:T(8,128)} %bitcast.94), calls=%async_computation.5 | async-start | bytes 131072 | tf_op jit(solution)/shard_map/all_to_all | solution.py:174
  280.2 11.6 %collective-permute-start.11 = (bf16[128,512]{1,0:T(8,128)(2,1)S(1)}, bf16[128,512]{1,0:T(8,128)(2,1)S(1)}, u32[]{:S(2)}, u32[]{:S(2)}) collective-permute-start(bf16[128,512]{1,0:T(8,128)(2,1)S(1)} %fusion.41), channel_id=1, source_target_pairs={{0,256},{128,384},{256,0},{384,128},{1,257},{129,385},{257,1},{385... | collective-permute-start | bytes 393224 | tf_op jit(solution)/shard_map/ppermute | solution.py:172
  (30 other events, 202.1 us)
Sparse Core Ops, SparseCore 0:
  10.7 133.0 all-gather.2

commit v8 on v7

--- a/solution.py
+++ b/solution.py
@@ -19,6 +19,51 @@
 
 def after(x, earlier):
     return x + (earlier[(0,) * earlier.ndim].astype(jnp.float32) * 0.0).astype(x.dtype)
+
+
+def held(x, earlier):
+    def kernel(x_ref, earlier_ref, out_ref):
+        del x_ref, earlier_ref, out_ref
+
+    anywhere = pl.BlockSpec(memory_space=pl.ANY)
+    return pl.pallas_call(
+        kernel,
+        out_shape=jax.ShapeDtypeStruct(x.shape, x.dtype),
+        in_specs=[anywhere, anywhere],
+        out_specs=anywhere,
+        input_output_aliases={0: 0},
+        cost_estimate=pl.CostEstimate(flops=0, bytes_accessed=0, transcendentals=0),
+    )(x, earlier)
+
+
+def hidden_units(w_all, arrived):
+    parts, both, width = w_all.shape
+    half = both // 2
+    rows = arrived.shape[0]
+
+    def kernel(w_ref, x_ref, out_ref):
+        pre = lax.dot_general(
+            w_ref[0], x_ref[...], (((1,), (1,)), ((), ())), preferred_element_type=jnp.float32
+        )
+        gate, up = pre[:half], pre[half:]
+        out_ref[...] = (gate / (1.0 + jnp.exp(-gate)) * up).astype(jnp.bfloat16)
+
+    return pl.pallas_call(
+        kernel,
+        grid=(parts,),
+        out_shape=jax.ShapeDtypeStruct((parts * half, rows), jnp.bfloat16),
+        in_specs=[
+            pl.BlockSpec((1, both, width), lambda q: (q, 0, 0)),
+            pl.BlockSpec((rows, width), lambda q: (0, 0)),
+        ],
+        out_specs=pl.BlockSpec((half, rows), lambda q: (q, 0)),
+        cost_estimate=pl.CostEstimate(
+            flops=2 * parts * both * width * rows,
+            bytes_accessed=2 * (parts * both * width + rows * width + parts * half * rows),
+            transcendentals=parts * half * rows,
+        ),
+        compiler_params=pltpu.CompilerParams(vmem_limit_bytes=32 * 1024 * 1024),
+    )(w_all, arrived)
 
 
 def expert_out(hidden_of, w_down, dev):
@@ -132,13 +177,7 @@
     scaled_rows = lax.all_to_all(scaled, "dev", split_axis=1, concat_axis=1, tiled=True)
     scaled_rows = scaled_rows.reshape(grp, dev * SLOTS, feats)
 
-    pre = lax.dot_general(
-        w_all.reshape(split * 2 * hidden_part, split * feats),
-        arrived,
-        (((1,), (1,)), ((), ())),
-        preferred_element_type=f32,
-    ).reshape(split, 2, hidden_part, dev * SLOTS)
-    hidden = (jax.nn.silu(pre[:, 0]) * pre[:, 1]).astype(bf16).reshape(split * hidden_part, dev * SLOTS)
+    hidden = hidden_units(w_all, arrived)
     hidden_of = [hidden]
     hidden_of.append(lax.ppermute(hidden, "split", flipped(split, 1)))
     hidden_of.append(lax.ppermute(hidden, "split", flipped(split, 2)))
@@ -148,7 +187,7 @@
         count = part_of.stop - part_of.start
         if part_of.start == 1:
             hidden_of.append(lax.ppermute(hidden_of[2], "split", flipped(split, 1)))
-        out = after(expert_out(hidden_of[part_of], w_down[0], dev), returned)
+        out = held(expert_out(hidden_of[part_of], w_down[0], dev), returned)
         returned = lax.all_to_all(out, "dev", split_axis=0, concat_axis=0, tiled=True)
         sent = jnp.swapaxes(returned, 0, 1).reshape(count, dev * SLOTS, feats)
         mixed.append(

time: 304 us -> 298 us (0.980)
  matrix products: 28.8 us -> 19.5 us
  other arithmetic: 16.5 us -> 12.1 us
  local copies, waits for them, and re-layouts: 17.8 us -> 22.2 us
  Pallas kernels: 2.19 us -> 6.32 us
    dot_general x1 -> x0, matrix products: 5.57 us -> none  [per_device(): lax.dot_general(w_all.reshape(split * 2 * hidden_part, split * feats), ar...]
    pallas_call x0 -> x4, Pallas kernels: none -> 4.13 us  [the longest x1 4.13 us: hidden_units(): pl.pallas_call(kernel, grid=(parts,), out_shape=jax.ShapeDtypeStruct((par...]
    slice x2, local copies, waits for them, and re-layouts: 0.23 us -> 3.91 us  [per_device(): weight[part_of]]
    slice x5 -> x2, local copies, waits for them, and re-layouts: 4.15 us -> 1.02 us  [after(): earlier[(0,) * earlier.ndim].astype(jnp.float32) * 0.0]
    unnamed x86 -> x34, local copies, waits for them, and re-layouts: 5.24 us -> 7.67 us
  transfers between devices with their start and end apart: 19 -> 19, of which waited for: 9 -> 9; matrix products, arithmetic and copies ran while one was open for 16% -> 14% of each run, Pallas kernels for 1% -> 2%
where the time goes in v8:
time: 298 us; the launch traced here: 295 us
  starting transfers between devices  112 us (38%)
  waiting for transfers between devices  106 us (36%)
  local copies, waits for them, and re-layouts  22.2 us (7%)
  matrix products  19.5 us (7%)
  between operations  16 us (5%)
  other arithmetic  12.1 us (4%)
  Pallas kernels  6.32 us (2%)
    all_gather x1, waiting for transfers between devices, per_device(): w_all = lax.all_gather(w_own, 'split', axis=0, tiled=False)  36.2 us
    all_to_all x3, starting transfers between devices, per_device(): lax.all_to_all(out, 'dev', split_axis=0, concat_axis=0, tiled=True)  29.2 us
    all_to_all x1, waiting for transfers between devices, per_device(): lax.all_to_all(send.reshape(dev, SLOTS, split * feats), 'dev', split_axis...  25.2 us
    ppermute x1, waiting for transfers between devices, per_device(): hidden_of.append(lax.ppermute(hidden, 'split', flipped(split, 2)))  17.8 us
    all_to_all x1, starting transfers between devices, per_device(): lax.all_to_all(send.reshape(dev, SLOTS, split * feats), 'dev', split_axis...  12.9 us
    ppermute x2, starting transfers between devices, per_device(): lax.ppermute(token_rows, ('grp', 'split'), [(g * split + f, (f ^ m) * spl...  10.5 us
    ppermute x1, waiting for transfers between devices, per_device(): hidden_of.append(lax.ppermute(hidden_of[2], 'split', flipped(split, 1)))  10.2 us
    ppermute x1, starting transfers between devices, per_device(): lax.ppermute(jnp.stack([own_mixed[1], own_mixed[3]]), 'grp', core)  9.78 us
  transfers between devices with their start and end apart: 19, of which 9 were waited for; matrix products, arithmetic and copies ran while one was open for 14% of the time, Pallas kernels for 2%

profile of v8, /device:TPU:1, one launch (start us, length us, event | category | flops | bytes accessed | tf_op | source)
XLA Modules:
  0.0 294.5 jit_solution(4455701151726539372)
XLA Ops:
  7.2 2.7 pad_maximum_fusion
  10.9 4.6 %collective-permute-start.3 = (bf16[144,512]{1,0:T(8,128)(2,1)S(1)}, bf16[144,512]{1,0:T(8,128)(2,1)S(1)}, u32[]{:S(2)}, u32[]{:S(2)}) collective-permute-start(bf16[144,512]{1,0:T(8,128)(2,1)S(1)} %get-tuple-element.68), channel_id=1, source_target_pairs={{0,0},{1,128},{2,256},{3,384},{128,1},{129,129},{130,257},{131,385... | collective-permute-start | bytes 442376 | tf_op jit(solution)/shard_map/ppermute | solution.py:128
  15.5 5.9 %collective-permute-start.5 = (bf16[144,512]{1,0:T(8,128)(2,1)S(1)}, bf16[144,512]{1,0:T(8,128)(2,1)S(1)}, u32[]{:S(2)}, u32[]{:S(2)}) collective-permute-start(bf16[144,512]{1,0:T(8,128)(2,1)S(1)} %get-tuple-element.68), channel_id=1, source_target_pairs={{0,256},{1,384},{2,0},{3,128},{128,257},{129,385},{130,1},{131,129... | collective-permute-start | bytes 442376 | tf_op jit(solution)/shard_map/ppermute | solution.py:128
  21.6 2.9 collective-permute-start.4
  24.5 3.9 %collective-permute-done.5 = bf16[144,512]{1,0:T(8,128)(2,1)S(1)} collective-permute-done((bf16[144,512]{1,0:T(8,128)(2,1)S(1)}, bf16[144,512]{1,0:T(8,128)(2,1)S(1)}, u32[]{:S(2)}, u32[]{:S(2)}) %collective-permute-start.5) | collective-permute-done | bytes 147488 | tf_op jit(solution)/shard_map/ppermute | solution.py:128
  28.4 3.2 %collective-permute-start.6 = (bf16[144,512]{1,0:T(8,128)(2,1)S(1)}, bf16[144,512]{1,0:T(8,128)(2,1)S(1)}, u32[]{:S(2)}, u32[]{:S(2)}) collective-permute-start(bf16[144,512]{1,0:T(8,128)(2,1)S(1)} %collective-permute-done.5), channel_id=1, source_target_pairs={{0,128},{128,0},{256,384},{384,256},{1,129},{129,1},{257,385},{385... | collective-permute-start | bytes 442376 | tf_op jit(solution)/shard_map/ppermute | solution.py:133
  32.8 2.0 convolution_convert_fusion
  34.8 12.9 %all-to-all-start = ((bf16[32,16,2048]{2,1,0:T(8,128)(2,1)}), bf16[32,16,2048]{2,1,0:T(8,128)(2,1)S(1)}, u32[]{:S(2)}, u32[]{:S(2)}) async-start(bf16[32,16,2048]{2,1,0:T(8,128)(2,1)} %bitcast.203), calls=%async_computation | async-start | bytes 4194304 | tf_op jit(solution)/shard_map/all_to_all | solution.py:172
  47.7 7.0 %collective-permute-start.1 = (bf16[144,512]{1,0:T(8,128)(2,1)S(1)}, bf16[144,512]{1,0:T(8,128)(2,1)S(1)}, u32[]{:S(2)}, u32[]{:S(2)}) collective-permute-start(bf16[144,512]{1,0:T(8,128)(2,1)S(1)} %get-tuple-element.30), channel_id=1, source_target_pairs={{0,256},{128,384},{256,0},{384,128},{1,257},{129,385},{257,1},{385... | collective-permute-start | bytes 442376 | tf_op jit(solution)/shard_map/ppermute | solution.py:138
  54.7 2.8 collective-permute-start
  57.6 6.1 %collective-permute-done.1 = bf16[144,512]{1,0:T(8,128)(2,1)S(1)} collective-permute-done((bf16[144,512]{1,0:T(8,128)(2,1)S(1)}, bf16[144,512]{1,0:T(8,128)(2,1)S(1)}, u32[]{:S(2)}, u32[]{:S(2)}) %collective-permute-start.1) | collective-permute-done | bytes 147488 | tf_op jit(solution)/shard_map/ppermute | solution.py:138
  63.6 3.6 %collective-permute-start.2 = (bf16[144,512]{1,0:T(8,128)(2,1)S(1)}, bf16[144,512]{1,0:T(8,128)(2,1)S(1)}, u32[]{:S(2)}, u32[]{:S(2)}) collective-permute-start(bf16[144,512]{1,0:T(8,128)(2,1)S(1)} %collective-permute-done.1), channel_id=1, source_target_pairs={{0,128},{128,0},{256,384},{384,256},{1,129},{129,1},{257,385},{385... | collective-permute-start | bytes 442376 | tf_op jit(solution)/shard_map/ppermute | solution.py:140
  71.0 25.2 %all-to-all-done = bf16[32,16,2048]{2,1,0:T(8,128)(2,1)S(1)} async-done(((bf16[32,16,2048]{2,1,0:T(8,128)(2,1)}), bf16[32,16,2048]{2,1,0:T(8,128)(2,1)S(1)}, u32[]{:S(2)}, u32[]{:S(2)}) %all-to-all-start) | async-done | bytes 2097184 | tf_op jit(solution)/shard_map/all_to_all | solution.py:172
  99.9 7.7 %all-to-all-start.1 = ((bf16[4,32,16,512]{3,2,0,1:T(8,128)(2,1)}), bf16[4,32,16,512]{3,2,0,1:T(8,128)(2,1)}, u32[]{:S(2)}, u32[]{:S(2)}) async-start(bf16[4,32,16,512]{3,2,0,1:T(8,128)(2,1)} %copy.69), calls=%async_computation.1 | async-start | bytes 4194304 | tf_op jit(solution)/shard_map/all_to_all | solution.py:177
  107.6 36.2 %all-gather.3.cloned.1.call-done = bf16[1536,2048]{1,0:T(8,128)(2,1)} async-done(((bf16[384,2048]{1,0:T(8,128)(2,1)}), bf16[1536,2048]{1,0:T(8,128)(2,1)}) %all-gather.3.cloned.1.call-update) | async-done | bytes 6291472 | tf_op jit(solution)/shard_map/all_gather | solution.py:116
  143.8 2.8 copy-done.4
  146.6 4.1 %shard_map.94.refs_0_ = bf16[768,512]{1,0:T(8,128)(2,1)S(1)} custom-call(bf16[4,384,2048]{2,1,0:T(8,128)(2,1)S(1)} %bitcast.199, bf16[512,2048]{1,0:T(8,128)(2,1)S(1)} %bitcast.198), custom_call_target="tpu_custom_call" | custom-call | flops 3221225472 | bytes 9175040 | tf_op jit(solution)/shard_map/pallas_call | solution.py:51
  150.7 3.8 %collective-permute-start.8 = (bf16[768,512]{1,0:T(8,128)(2,1)S(1)}, bf16[768,512]{1,0:T(8,128)(2,1)S(1)}, u32[]{:S(2)}, u32[]{:S(2)}) collective-permute-start(bf16[768,512]{1,0:T(8,128)(2,1)S(1)} %shard_map.94.refs_0_), channel_id=1, source_target_pairs={{0,2},{1,3},{2,0},{3,1},{4,6},{5,7},{6,4},{7,5},{8,10},{9,11},{10,... | collective-permute-start | bytes 2359304 | tf_op jit(solution)/shard_map/ppermute | solution.py:183
  156.4 3.2 %copy.70 = bf16[4,32,16,512]{3,2,1,0:T(8,128)(2,1)} copy(bf16[4,32,16,512]{3,2,0,1:T(8,128)(2,1)} %all-to-all-done.1) | data formatting | bytes 4194304 | tf_op jit(solution)/shard_map/all_to_all | solution.py:177
  161.0 10.2 %all-to-all-start.2 = ((bf16[32,1,16,512]{3,2,1,0:T(8,128)(2,1)}), bf16[32,1,16,512]{3,2,1,0:T(8,128)(2,1)}, u32[]{:S(2)}, u32[]{:S(2)}) async-start(bf16[32,1,16,512]{3,2,1,0:T(8,128)(2,1)} %shard_map.96), calls=%async_computation.2 | async-start | bytes 1048576 | tf_op jit(solution)/shard_map/all_to_all | solution.py:191
  171.2 17.8 %collective-permute-done.8.refs_1_ = bf16[768,512]{1,0:T(8,128)(2,1)S(1)} collective-permute-done((bf16[768,512]{1,0:T(8,128)(2,1)S(1)}, bf16[768,512]{1,0:T(8,128)(2,1)S(1)}, u32[]{:S(2)}, u32[]{:S(2)}) %collective-permute-start.8) | collective-permute-done | bytes 786464 | tf_op jit(solution)/shard_map/ppermute | solution.py:183
  191.0 10.0 %all-to-all-start.3 = ((bf16[32,2,16,512]{3,2,1,0:T(8,128)(2,1)}), bf16[32,2,16,512]{3,2,1,0:T(8,128)(2,1)}, u32[]{:S(2)}, u32[]{:S(2)}) async-start(bf16[32,2,16,512]{3,2,1,0:T(8,128)(2,1)} %shard_map.98), calls=%async_computation.3 | async-start | bytes 2097152 | tf_op jit(solution)/shard_map/all_to_all | solution.py:191
  202.9 2.0 copy.71
  207.6 2.5 fusion.93
  211.8 2.7 collective-permute-start.9
  219.3 10.2 %collective-permute-done.9.refs_0_ = bf16[768,512]{1,0:T(8,128)(2,1)S(1)} collective-permute-done((bf16[768,512]{1,0:T(8,128)(2,1)S(1)}, bf16[768,512]{1,0:T(8,128)(2,1)S(1)}, u32[]{:S(2)}, u32[]{:S(2)}) %collective-permute-start.9) | collective-permute-done | bytes 786464 | tf_op jit(solution)/shard_map/ppermute | solution.py:189
  230.9 9.1 %all-to-all-start.4 = ((bf16[32,1,16,512]{3,2,1,0:T(8,128)(2,1)}), bf16[32,1,16,512]{3,2,1,0:T(8,128)(2,1)S(1)}, u32[]{:S(2)}, u32[]{:S(2)}) async-start(bf16[32,1,16,512]{3,2,1,0:T(8,128)(2,1)} %shard_map.100), calls=%async_computation.4 | async-start | bytes 1048576 | tf_op jit(solution)/shard_map/all_to_all | solution.py:191
  246.4 5.0 %all-to-all-done.4 = bf16[32,1,16,512]{3,2,1,0:T(8,128)(2,1)S(1)} async-done(((bf16[32,1,16,512]{3,2,1,0:T(8,128)(2,1)}), bf16[32,1,16,512]{3,2,1,0:T(8,128)(2,1)S(1)}, u32[]{:S(2)}, u32[]{:S(2)}) %all-to-all-start.4) | async-done | bytes 524320 | tf_op jit(solution)/shard_map/all_to_all | solution.py:191
  252.8 9.8 %collective-permute-start.10 = (bf16[2,128,512]{2,1,0:T(8,128)(2,1)}, bf16[2,128,512]{2,1,0:T(8,128)(2,1)}, u32[]{:S(2)}, u32[]{:S(2)}) collective-permute-start(bf16[2,128,512]{2,1,0:T(8,128)(2,1)} %pad_maximum_fusion.14), channel_id=1, source_target_pairs={{0,128},{128,0},{256,384},{384,256},{1,129},{129,1},{257,385},{385... | collective-permute-start | bytes 786440 | tf_op jit(solution)/shard_map/ppermute | solution.py:208
  265.8 7.0 %all-to-all-start.5 = ((f32[16,8,128]{2,1,0:T(8,128)}), f32[16,8,128]{2,1,0:T(8,128)S(1)}, u32[]{:S(2)}, u32[]{:S(2)}) async-start(f32[16,8,128]{2,1,0:T(8,128)} %bitcast.87), calls=%async_computation.5 | async-start | bytes 131072 | tf_op jit(solution)/shard_map/all_to_all | solution.py:213
  274.5 7.2 %collective-permute-start.11 = (bf16[128,512]{1,0:T(8,128)(2,1)}, bf16[128,512]{1,0:T(8,128)(2,1)}, u32[]{:S(2)}, u32[]{:S(2)}) collective-permute-start(bf16[128,512]{1,0:T(8,128)(2,1)} %fusion.37), channel_id=1, source_target_pairs={{0,256},{128,384},{256,0},{384,128},{1,257},{129,385},{257,1},{385... | collective-permute-start | bytes 393224 | tf_op jit(solution)/shard_map/ppermute | solution.py:211
  281.7 3.8 %add_bitcast_fusion = f32[1,768,512]{2,1,0:T(8,128)} fusion(f32[768,512]{1,0:T(8,128)} %fusion.100, f32[768,512]{1,0:T(8,128)S(1)} %copy-done.5, f32[768,512]{1,0:T(8,128)} %fusion.99, bf16[768,512]{1,0:T(8,128)(2,1)S(1)} %collective-permute-done.9.refs_0_, bf16[512,512]{1,0:T(8,128)(2,1)} %bitcast.212), kind=kOutput, calls=%fused_computation.3 | convolution fusion | flops 403832832 | bytes 7602176 | tf_op jit(solution)/shard_map/dot_general | solution.py:217
  (115 shorter events, 40.5 us)
Async XLA Ops:
  7.2 136.6 %all-gather.3.cloned.1.call-start = ((), (), s32[]{:S(2)}) async-start(), calls=%async_computation.6 | async-start | bytes 7864320 | tf_op jit(solution)/shard_map/all_gather | solution.py:116
  9.9 0.9 copy-start.13
  9.9 1.0 copy-start.14
  10.9 10.7 %collective-permute-start.3 = (bf16[144,512]{1,0:T(8,128)(2,1)S(1)}, bf16[144,512]{1,0:T(8,128)(2,1)S(1)}, u32[]{:S(2)}, u32[]{:S(2)}) collective-permute-start(bf16[144,512]{1,0:T(8,128)(2,1)S(1)} %get-tuple-element.68), channel_id=1, source_target_pairs={{0,0},{1,128},{2,256},{3,384},{128,1},{129,129},{130,257},{131,385... | collective-permute-start | bytes 442376 | tf_op jit(solution)/shard_map/ppermute | solution.py:128
  15.5 12.9 %collective-permute-start.5 = (bf16[144,512]{1,0:T(8,128)(2,1)S(1)}, bf16[144,512]{1,0:T(8,128)(2,1)S(1)}, u32[]{:S(2)}, u32[]{:S(2)}) collective-permute-start(bf16[144,512]{1,0:T(8,128)(2,1)S(1)} %get-tuple-element.68), channel_id=1, source_target_pairs={{0,256},{1,384},{2,0},{3,128},{128,257},{129,385},{130,1},{131,129... | collective-permute-start | bytes 442376 | tf_op jit(solution)/shard_map/ppermute | solution.py:128
  21.6 11.0 %collective-permute-start.4 = (bf16[144,512]{1,0:T(8,128)(2,1)S(1)}, bf16[144,512]{1,0:T(8,128)(2,1)S(1)}, u32[]{:S(2)}, u32[]{:S(2)}) collective-permute-start(bf16[144,512]{1,0:T(8,128)(2,1)S(1)} %collective-permute-done.3), channel_id=1, source_target_pairs={{0,128},{128,0},{256,384},{384,256},{1,129},{129,1},{257,385},{385... | collective-permute-start | bytes 442376 | tf_op jit(solution)/shard_map/ppermute | solution.py:133
  28.4 4.2 %collective-permute-start.6 = (bf16[144,512]{1,0:T(8,128)(2,1)S(1)}, bf16[144,512]{1,0:T(8,128)(2,1)S(1)}, u32[]{:S(2)}, u32[]{:S(2)}) collective-permute-start(bf16[144,512]{1,0:T(8,128)(2,1)S(1)} %collective-permute-done.5), channel_id=1, source_target_pairs={{0,128},{128,0},{256,384},{384,256},{1,129},{129,1},{257,385},{385... | collective-permute-start | bytes 442376 | tf_op jit(solution)/shard_map/ppermute | solution.py:133
  34.8 61.5 %all-to-all-start = ((bf16[32,16,2048]{2,1,0:T(8,128)(2,1)}), bf16[32,16,2048]{2,1,0:T(8,128)(2,1)S(1)}, u32[]{:S(2)}, u32[]{:S(2)}) async-start(bf16[32,16,2048]{2,1,0:T(8,128)(2,1)} %bitcast.203), calls=%async_computation | async-start | bytes 4194304 | tf_op jit(solution)/shard_map/all_to_all | solution.py:172
  47.7 15.9 %collective-permute-start.1 = (bf16[144,512]{1,0:T(8,128)(2,1)S(1)}, bf16[144,512]{1,0:T(8,128)(2,1)S(1)}, u32[]{:S(2)}, u32[]{:S(2)}) collective-permute-start(bf16[144,512]{1,0:T(8,128)(2,1)S(1)} %get-tuple-element.30), channel_id=1, source_target_pairs={{0,256},{128,384},{256,0},{384,128},{1,257},{129,385},{257,1},{385... | collective-permute-start | bytes 442376 | tf_op jit(solution)/shard_map/ppermute | solution.py:138
  54.7 12.6 %collective-permute-start = (bf16[144,512]{1,0:T(8,128)(2,1)S(1)}, bf16[144,512]{1,0:T(8,128)(2,1)S(1)}, u32[]{:S(2)}, u32[]{:S(2)}) collective-permute-start(bf16[144,512]{1,0:T(8,128)(2,1)S(1)} %get-tuple-element.30), channel_id=1, source_target_pairs={{0,128},{128,0},{256,384},{384,256},{1,129},{129,1},{257,385},{385... | collective-permute-start | bytes 442376 | tf_op jit(solution)/shard_map/ppermute | solution.py:140
  63.6 4.6 %collective-permute-start.2 = (bf16[144,512]{1,0:T(8,128)(2,1)S(1)}, bf16[144,512]{1,0:T(8,128)(2,1)S(1)}, u32[]{:S(2)}, u32[]{:S(2)}) collective-permute-start(bf16[144,512]{1,0:T(8,128)(2,1)S(1)} %collective-permute-done.1), channel_id=1, source_target_pairs={{0,128},{128,0},{256,384},{384,256},{1,129},{129,1},{257,385},{385... | collective-permute-start | bytes 442376 | tf_op jit(solution)/shard_map/ppermute | solution.py:140
  68.3 0.8 copy-start.7
  99.9 56.6 %all-to-all-start.1 = ((bf16[4,32,16,512]{3,2,0,1:T(8,128)(2,1)}), bf16[4,32,16,512]{3,2,0,1:T(8,128)(2,1)}, u32[]{:S(2)}, u32[]{:S(2)}) async-start(bf16[4,32,16,512]{3,2,0,1:T(8,128)(2,1)} %copy.69), calls=%async_computation.1 | async-start | bytes 4194304 | tf_op jit(solution)/shard_map/all_to_all | solution.py:177
  143.8 2.8 copy-start.4
  150.7 8.9 %copy-start.3 = (bf16[1,768,512]{2,1,0:T(8,128)(2,1)S(1)}, bf16[1,768,512]{2,1,0:T(8,128)(2,1)}, u32[]{:S(2)}) copy-start(bf16[1,768,512]{2,1,0:T(8,128)(2,1)} %param.13) | copy-start | bytes 2359300
  150.7 38.3 %collective-permute-start.8 = (bf16[768,512]{1,0:T(8,128)(2,1)S(1)}, bf16[768,512]{1,0:T(8,128)(2,1)S(1)}, u32[]{:S(2)}, u32[]{:S(2)}) collective-permute-start(bf16[768,512]{1,0:T(8,128)(2,1)S(1)} %shard_map.94.refs_0_), channel_id=1, source_target_pairs={{0,2},{1,3},{2,0},{3,1},{4,6},{5,7},{6,4},{7,5},{8,10},{9,11},{10,... | collective-permute-start | bytes 2359304 | tf_op jit(solution)/shard_map/ppermute | solution.py:183
  154.5 34.5 %collective-permute-start.7 = (bf16[768,512]{1,0:T(8,128)(2,1)S(1)}, bf16[768,512]{1,0:T(8,128)(2,1)S(1)}, u32[]{:S(2)}, u32[]{:S(2)}) collective-permute-start(bf16[768,512]{1,0:T(8,128)(2,1)S(1)} %shard_map.94.refs_0_), channel_id=1, source_target_pairs={{0,1},{1,0},{2,3},{3,2},{4,5},{5,4},{6,7},{7,6},{8,9},{9,8},{10,11... | collective-permute-start | bytes 2359304 | tf_op jit(solution)/shard_map/ppermute | solution.py:182
  161.0 30.0 %all-to-all-start.2 = ((bf16[32,1,16,512]{3,2,1,0:T(8,128)(2,1)}), bf16[32,1,16,512]{3,2,1,0:T(8,128)(2,1)}, u32[]{:S(2)}, u32[]{:S(2)}) async-start(bf16[32,1,16,512]{3,2,1,0:T(8,128)(2,1)} %shard_map.96), calls=%async_computation.2 | async-start | bytes 1048576 | tf_op jit(solution)/shard_map/all_to_all | solution.py:191
  190.0 1.0 copy-start.2
  191.0 39.9 %all-to-all-start.3 = ((bf16[32,2,16,512]{3,2,1,0:T(8,128)(2,1)}), bf16[32,2,16,512]{3,2,1,0:T(8,128)(2,1)}, u32[]{:S(2)}, u32[]{:S(2)}) async-start(bf16[32,2,16,512]{3,2,1,0:T(8,128)(2,1)} %shard_map.98), calls=%async_computation.3 | async-start | bytes 2097152 | tf_op jit(solution)/shard_map/all_to_all | solution.py:191
  211.8 17.7 %collective-permute-start.9 = (bf16[768,512]{1,0:T(8,128)(2,1)S(1)}, bf16[768,512]{1,0:T(8,128)(2,1)S(1)}, u32[]{:S(2)}, u32[]{:S(2)}) collective-permute-start(bf16[768,512]{1,0:T(8,128)(2,1)S(1)} %collective-permute-done.8.refs_1_), channel_id=1, source_target_pairs={{0,1},{1,0},{2,3},{3,2},{4,5},{5,4},{6,7},{7,6},{8,9},{9,8},{10,11... | collective-permute-start | bytes 2359304 | tf_op jit(solution)/shard_map/ppermute | solution.py:189
  230.9 9.1 %copy-start.12 = (pred[4,32,16,128]{3,2,1,0:T(8,128)(4,1)S(1)}, pred[4,32,16,128]{3,2,1,0:T(8,128)(4,1)}, u32[]{:S(2)}) copy-start(pred[4,32,16,128]{3,2,1,0:T(8,128)(4,1)} %iota_compare_fusion) | copy-start | bytes 786436
  230.9 10.5 %copy-start.10 = (bf16[1,32,16,128]{3,2,1,0:T(8,128)(2,1)S(1)}, bf16[1,32,16,128]{3,2,1,0:T(8,128)(2,1)}, u32[]{:S(2)}) copy-start(bf16[1,32,16,128]{3,2,1,0:T(8,128)(2,1)} %get-tuple-element.15) | copy-start | bytes 393220
  230.9 20.5 %all-to-all-start.4 = ((bf16[32,1,16,512]{3,2,1,0:T(8,128)(2,1)}), bf16[32,1,16,512]{3,2,1,0:T(8,128)(2,1)S(1)}, u32[]{:S(2)}, u32[]{:S(2)}) async-start(bf16[32,1,16,512]{3,2,1,0:T(8,128)(2,1)} %shard_map.100), calls=%async_computation.4 | async-start | bytes 1048576 | tf_op jit(solution)/shard_map/all_to_all | solution.py:191
  244.7 1.0 copy-start.6
  246.0 5.4 %copy-start.8 = (bf16[1,32,16,128]{3,2,1,0:T(8,128)(2,1)S(1)}, bf16[1,32,16,128]{3,2,1,0:T(8,128)(2,1)}, u32[]{:S(2)}) copy-start(bf16[1,32,16,128]{3,2,1,0:T(8,128)(2,1)} %get-tuple-element.16) | copy-start | bytes 393220
  246.0 5.6 %copy-start.9 = (bf16[1,32,16,128]{3,2,1,0:T(8,128)(2,1)S(1)}, bf16[1,32,16,128]{3,2,1,0:T(8,128)(2,1)}, u32[]{:S(2)}) copy-start(bf16[1,32,16,128]{3,2,1,0:T(8,128)(2,1)} %get-tuple-element.17) | copy-start | bytes 393220
  246.3 5.6 %copy-start.11 = (bf16[1,128,512]{2,1,0:T(8,128)(2,1)S(1)}, bf16[1,128,512]{2,1,0:T(8,128)(2,1)}, u32[]{:S(2)}) copy-start(bf16[1,128,512]{2,1,0:T(8,128)(2,1)} %fusion.8) | copy-start | bytes 393220
  252.0 29.7 %copy-start.5 = (f32[768,512]{1,0:T(8,128)S(1)}, f32[768,512]{1,0:T(8,128)}, u32[]{:S(2)}) copy-start(f32[768,512]{1,0:T(8,128)} %fusion.98) | copy-start | bytes 4718596
  252.8 20.0 %collective-permute-start.10 = (bf16[2,128,512]{2,1,0:T(8,128)(2,1)}, bf16[2,128,512]{2,1,0:T(8,128)(2,1)}, u32[]{:S(2)}, u32[]{:S(2)}) collective-permute-start(bf16[2,128,512]{2,1,0:T(8,128)(2,1)} %pad_maximum_fusion.14), channel_id=1, source_target_pairs={{0,128},{128,0},{256,384},{384,256},{1,129},{129,1},{257,385},{385... | collective-permute-start | bytes 786440 | tf_op jit(solution)/shard_map/ppermute | solution.py:208
  265.8 19.7 %all-to-all-start.5 = ((f32[16,8,128]{2,1,0:T(8,128)}), f32[16,8,128]{2,1,0:T(8,128)S(1)}, u32[]{:S(2)}, u32[]{:S(2)}) async-start(f32[16,8,128]{2,1,0:T(8,128)} %bitcast.87), calls=%async_computation.5 | async-start | bytes 131072 | tf_op jit(solution)/shard_map/all_to_all | solution.py:213
  274.5 11.6 %collective-permute-start.11 = (bf16[128,512]{1,0:T(8,128)(2,1)}, bf16[128,512]{1,0:T(8,128)(2,1)}, u32[]{:S(2)}, u32[]{:S(2)}) collective-permute-start(bf16[128,512]{1,0:T(8,128)(2,1)} %fusion.37), channel_id=1, source_target_pairs={{0,256},{128,384},{256,0},{384,128},{1,257},{129,385},{257,1},{385... | collective-permute-start | bytes 393224 | tf_op jit(solution)/shard_map/ppermute | solution.py:211
  (4 other events, 3.0 us)
Sparse Core Ops, SparseCore 0:
  10.7 133.0 all-gather.2
